TPU v7x, 32 devices: a whole 2x2x4 slice. The times are simulated.
32 devices in a mesh: rows: 8 (over z, core), seq: 4 (over y, x).
Axes of the slice: x: 2, y: 2, z: 4, core: 2. Of those that a mesh axis runs over, the one named last changes fastest.
Arguments:
- tokens: bfloat16 [16, 1024, 1152], P('rows', 'seq'), may hold values from -6 to 6
- conditioning: bfloat16 [128, 1152], P('rows'), may hold values from -6 to 6
- segment_ids: int32 [16, 1024], P('rows'), may hold values from 0 to 7, as said below
- image_index: int32 [16, 8], P('rows'), may hold values from 0 to 15
- row_fill: int32 [16], P('rows'), may hold values from 512 to 1024, as said below
- ada_weight: bfloat16 [1152, 6912], P(None, 'seq'), may hold values from -0.1875 to 0.1875
- ada_bias: bfloat16 [6912], replicated, may hold values from -1.796875 to 1.796875
- qkv_weight: bfloat16 [1152, 3456], replicated, may hold values from -0.1875 to 0.1875
- qv_bias: bfloat16 [2, 1152], replicated, may hold values from -1.796875 to 1.796875
- proj_weight: bfloat16 [1152, 1152], replicated, may hold values from -2 to 2
- proj_bias: bfloat16 [1152], replicated, may hold values from -1.796875 to 1.796875
- up_weight: bfloat16 [1152, 4608], replicated, may hold values from -0.1875 to 0.1875
- up_bias: bfloat16 [4608], replicated, may hold values from -1.796875 to 1.796875
- down_weight: bfloat16 [4608, 1152], replicated, may hold values from -0.09375 to 0.09375
- down_bias: bfloat16 [1152], replicated, may hold values from -1.796875 to 1.796875
- cotangent: bfloat16 [16, 1024, 1152], P('rows', 'seq'), may hold values from -6 to 6
Outputs:
- block_out: bfloat16 [16, 1024, 1152], P('rows', 'seq')
- grad_tokens: float32 [16, 1024, 1152], P('rows', 'seq')
- grad_cond: float32 [128, 1152], P('rows')
- grad_ada_weight: float32 [1152, 6912], P('rows', 'seq')
- grad_ada_bias: float32 [6912], replicated
- grad_qkv_weight: float32 [1152, 3456], P('rows', 'seq')
- grad_qv_bias: float32 [2, 1152], replicated
- grad_proj_weight: float32 [1152, 1152], P('rows', 'seq')
- grad_proj_bias: float32 [1152], replicated
- grad_up_weight: float32 [1152, 4608], P('rows', 'seq')
- grad_up_bias: float32 [4608], replicated
- grad_down_weight: float32 [4608, 1152], P('rows', 'seq')
- grad_down_bias: float32 [1152], replicated
Inputs may be any that keep to these rules, and one draw needn't show every extreme that they name: `segment_ids`: never falls along a row; in every aligned block of 2 rows one row has a segment that holds every position from 1024 // (2 * 4) to 1024 - 1024 // (2 * 4). `row_fill`: that row's fill is above 1024 - 1024 // (2 * 4).
All inputs are finite; a program needn't handle non-finite values.
Results may differ from a plain program's by a relative error of at most 0.012.
The roundings to bfloat16 on the way count: a program that leaves them out, or rounds other values in their place, can miss the bound.
Values may be sent and summed in bfloat16 or wider, within the bound.
A program may use at most 256 MiB of HBM per device.

v0:
```python
from functools import partial

import jax
import jax.numpy as jnp
from jax import lax
from jax.sharding import PartitionSpec as P

HEADS = 16


norm_eps = 1e-06


def modulate(values, offset, factor):
    center = values - jnp.mean(values, axis=-1, keepdims=True)
    spread = jnp.mean(center * center, axis=-1, keepdims=True)
    return center * lax.rsqrt(spread + norm_eps) * (1.0 + factor) + offset


def gelu_tanh(values):
    return jax.nn.gelu(values, approximate=True)


def allowed_pairs(segments, filled):
    places = lax.iota(jnp.int32, segments.shape[0])
    inside = places < filled
    same_segment = (segments[:, None] == segments[None, :]) & inside[:, None] & inside[None, :]
    return same_segment | (places[:, None] == places[None, :])


def head_scores(query_block, key_block, allowed):
    raw_scores = jnp.einsum("dq,dk->qk", query_block, key_block, preferred_element_type=jnp.float32)
    return jnp.where(allowed, raw_scores * query_block.shape[0] ** (-0.5), -1e30)


def head_forward(query_block, key_block, value_block, allowed):
    scores = head_scores(query_block, key_block, allowed)
    row_peak = jnp.max(scores, axis=-1, keepdims=True)
    raised = jnp.exp(scores - row_peak)
    totals = jnp.sum(raised, axis=-1, keepdims=True)
    soft_weights = (raised / totals).astype(jnp.bfloat16)
    output = jnp.einsum("dk,qk->dq", value_block, soft_weights, preferred_element_type=jnp.float32)
    return (output.astype(jnp.bfloat16), row_peak[:, 0] + jnp.log(totals[:, 0]))


def head_backward(query_block, key_block, value_block, grad_out, log_totals, allowed):
    scores = head_scores(query_block, key_block, allowed)
    soft_weights = jnp.exp(scores - log_totals[:, None])
    grad_values = jnp.einsum(
        "dq,qk->dk", grad_out, soft_weights.astype(jnp.bfloat16), preferred_element_type=jnp.float32
    )
    grad_weights = jnp.einsum(
        "dq,dk->qk", grad_out, value_block, preferred_element_type=jnp.float32
    )
    row_dot = jnp.sum(soft_weights * grad_weights, axis=-1, keepdims=True)
    grad_raw = (soft_weights * (grad_weights - row_dot) * query_block.shape[0] ** (-0.5)).astype(
        jnp.bfloat16
    )
    grad_query = jnp.einsum("dk,qk->dq", key_block, grad_raw, preferred_element_type=jnp.float32)
    grad_keys = jnp.einsum("dq,qk->dk", query_block, grad_raw, preferred_element_type=jnp.float32)
    return jnp.stack([grad_query, grad_keys, grad_values]).astype(jnp.bfloat16)


def attend_row(inputs):
    packed_row, segments, filled = inputs
    allowed = allowed_pairs(segments, filled)
    return jax.vmap(partial(head_forward, allowed=allowed))(
        packed_row[0], packed_row[1], packed_row[2]
    )


def attend_back_row(inputs):
    packed_row, grad_row, segments, filled, log_row = inputs
    allowed = allowed_pairs(segments, filled)
    return jax.vmap(partial(head_backward, allowed=allowed), out_axes=1)(
        packed_row[0], packed_row[1], packed_row[2], grad_row, log_row
    )


def on_device(
    tokens,
    conditioning,
    segment_ids,
    image_index,
    row_fill,
    ada_weight,
    ada_bias,
    qkv_weight,
    qv_bias,
    proj_weight,
    proj_bias,
    up_weight,
    up_bias,
    down_weight,
    down_bias,
    cotangent,
):
    row_count, local_len, width = tokens.shape
    seq_count = lax.axis_size("seq")
    seq_index = lax.axis_index("seq")
    full_len = local_len * seq_count
    heads_dev = HEADS // seq_count
    head_size = width // HEADS
    image_count = conditioning.shape[0]
    cond_wide = conditioning.astype(jnp.float32)
    cond_low = jax.nn.silu(cond_wide).astype(jnp.bfloat16)
    mod_part = jnp.dot(cond_low, ada_weight, preferred_element_type=jnp.float32)
    modulation = lax.all_gather(mod_part, "seq", axis=1, tiled=True) + ada_bias.astype(jnp.float32)
    local_seg = lax.dynamic_slice_in_dim(segment_ids, seq_index * local_len, local_len, 1)
    slot_ids = lax.iota(jnp.int32, image_index.shape[1])
    slot_mod = jnp.take(modulation, image_index, axis=0)
    slot_pick = (local_seg[:, :, None] == slot_ids).astype(jnp.float32)
    mod_tok = jnp.einsum("rts,rse->rte", slot_pick, slot_mod, precision=lax.Precision.HIGHEST)
    shift_a, scale_a, gate_a, shift_b, scale_b, gate_b = jnp.split(mod_tok, 6, axis=-1)
    tokens_wide = tokens.astype(jnp.float32)
    bias_qkv = jnp.concatenate(
        [
            qv_bias[0].astype(jnp.float32),
            jnp.zeros((width,), jnp.float32),
            qv_bias[1].astype(jnp.float32),
        ]
    )

    def project_heads():
        normed = modulate(tokens_wide, shift_a, scale_a).astype(jnp.bfloat16)
        mixed = (
            jnp.einsum("rtd,df->rft", normed, qkv_weight, preferred_element_type=jnp.float32)
            + bias_qkv[:, None]
        )
        return (normed, mixed.astype(jnp.bfloat16).reshape(row_count, 3, width, local_len))

    normed_a, packed = project_heads()
    spread_heads = lax.all_to_all(packed, "seq", split_axis=2, concat_axis=3, tiled=True)
    head_view = spread_heads.reshape(row_count, 3, heads_dev, head_size, full_len)
    attended, log_totals = lax.map(attend_row, (head_view, segment_ids, row_fill))
    attended_tok = lax.all_to_all(
        attended.reshape(row_count, heads_dev * head_size, full_len),
        "seq",
        split_axis=2,
        concat_axis=1,
        tiled=True,
    )
    branch_a = jnp.einsum(
        "rft,fe->rte", attended_tok, proj_weight, preferred_element_type=jnp.float32
    ) + proj_bias.astype(jnp.float32)
    middle = tokens_wide + gate_a * branch_a
    normed_b = modulate(middle, shift_b, scale_b).astype(jnp.bfloat16)
    hidden_pre = jnp.einsum(
        "rtd,df->rtf", normed_b, up_weight, preferred_element_type=jnp.float32
    ) + up_bias.astype(jnp.float32)
    activated = gelu_tanh(hidden_pre).astype(jnp.bfloat16)
    branch_b = jnp.einsum(
        "rtf,fe->rte", activated, down_weight, preferred_element_type=jnp.float32
    ) + down_bias.astype(jnp.float32)
    block_out = (middle + gate_b * branch_b).astype(jnp.bfloat16)
    upstream = cotangent.astype(jnp.float32)
    grad_branch_b = (upstream * gate_b).astype(jnp.bfloat16)
    grad_gate_b = upstream * branch_b
    part_down = jnp.einsum(
        "rtf,rte->fe", activated, grad_branch_b, preferred_element_type=jnp.float32
    )
    part_down_bias = jnp.sum(grad_branch_b.astype(jnp.float32), axis=(0, 1))
    grad_act = jnp.einsum(
        "rte,fe->rtf", grad_branch_b, down_weight, preferred_element_type=jnp.float32
    )
    _, gelu_back = jax.vjp(gelu_tanh, hidden_pre)
    grad_pre = gelu_back(grad_act)[0].astype(jnp.bfloat16)
    part_up = jnp.einsum("rtd,rtf->df", normed_b, grad_pre, preferred_element_type=jnp.float32)
    part_up_bias = jnp.sum(grad_pre.astype(jnp.float32), axis=(0, 1))
    grad_normed_b = jnp.einsum(
        "rtf,df->rtd", grad_pre, up_weight, preferred_element_type=jnp.float32
    )
    _, norm_back_b = jax.vjp(modulate, middle, shift_b, scale_b)
    grad_mid_norm, grad_shift_b, grad_scale_b = norm_back_b(grad_normed_b)
    grad_middle = upstream + grad_mid_norm
    grad_branch_a = (grad_middle * gate_a).astype(jnp.bfloat16)
    grad_gate_a = grad_middle * branch_a
    part_proj = jnp.einsum(
        "rft,rte->fe", attended_tok, grad_branch_a, preferred_element_type=jnp.float32
    )
    part_proj_bias = jnp.sum(grad_branch_a.astype(jnp.float32), axis=(0, 1))
    grad_attended = jnp.einsum(
        "rte,fe->rft", grad_branch_a, proj_weight, preferred_element_type=jnp.float32
    ).astype(jnp.bfloat16)
    grad_heads_in = lax.all_to_all(grad_attended, "seq", split_axis=1, concat_axis=2, tiled=True)
    grad_view = grad_heads_in.reshape(row_count, heads_dev, head_size, full_len)
    _, packed_again = project_heads()
    kept_heads = lax.all_to_all(packed_again, "seq", split_axis=2, concat_axis=3, tiled=True)
    kept_view = kept_heads.reshape(row_count, 3, heads_dev, head_size, full_len)
    grad_heads = lax.map(attend_back_row, (kept_view, grad_view, segment_ids, row_fill, log_totals))
    grad_packed = lax.all_to_all(
        grad_heads.reshape(row_count, 3, heads_dev * head_size, full_len),
        "seq",
        split_axis=3,
        concat_axis=2,
        tiled=True,
    )
    grad_flat = grad_packed.reshape(row_count, 3 * width, local_len)
    part_qkv = jnp.einsum("rtd,rft->df", normed_a, grad_flat, preferred_element_type=jnp.float32)
    column_sums = jnp.sum(grad_packed.astype(jnp.float32), axis=(0, 3))
    part_qv_bias = jnp.stack([column_sums[0], column_sums[2]])
    grad_normed_a = jnp.einsum(
        "rft,df->rtd", grad_flat, qkv_weight, preferred_element_type=jnp.float32
    )
    _, norm_back_a = jax.vjp(modulate, tokens_wide, shift_a, scale_a)
    grad_tok_norm, grad_shift_a, grad_scale_a = norm_back_a(grad_normed_a)
    grad_tokens = grad_middle + grad_tok_norm
    grad_mod_tok = jnp.concatenate(
        [grad_shift_a, grad_scale_a, grad_gate_a, grad_shift_b, grad_scale_b, grad_gate_b], axis=-1
    )
    slot_grads = jnp.einsum(
        "rts,rte->rse", slot_pick, grad_mod_tok, precision=lax.Precision.HIGHEST
    )
    image_pick = (image_index[:, :, None] == lax.iota(jnp.int32, image_count)).astype(jnp.float32)
    grad_modulation = jnp.einsum(
        "rsi,rse->ie", image_pick, slot_grads, precision=lax.Precision.HIGHEST
    )
    part_ada_bias = jnp.sum(grad_modulation, axis=0)
    mod_columns = lax.psum_scatter(grad_modulation, "seq", scatter_dimension=1, tiled=True)
    grad_mod_low = mod_columns.astype(jnp.bfloat16)
    part_ada = jnp.einsum("id,ie->de", cond_low, grad_mod_low, preferred_element_type=jnp.float32)
    cond_term = jnp.einsum(
        "ie,de->id", grad_mod_low, ada_weight, preferred_element_type=jnp.float32
    )
    grad_cond_low = lax.psum(cond_term, "seq")
    _, silu_back = jax.vjp(jax.nn.silu, cond_wide)
    grad_cond = silu_back(grad_cond_low)[0]
    over_seq = (
        lax.psum_scatter(part_qkv, "seq", scatter_dimension=1, tiled=True),
        lax.psum_scatter(part_proj, "seq", scatter_dimension=1, tiled=True),
        lax.psum_scatter(part_up, "seq", scatter_dimension=1, tiled=True),
        lax.psum_scatter(part_down, "seq", scatter_dimension=1, tiled=True),
    )
    grad_qkv_weight, grad_proj_weight, grad_up_weight, grad_down_weight, grad_ada_weight = (
        lax.psum_scatter(over_seq[0], "rows", scatter_dimension=0, tiled=True),
        lax.psum_scatter(over_seq[1], "rows", scatter_dimension=0, tiled=True),
        lax.psum_scatter(over_seq[2], "rows", scatter_dimension=0, tiled=True),
        lax.psum_scatter(over_seq[3], "rows", scatter_dimension=0, tiled=True),
        lax.psum_scatter(part_ada, "rows", scatter_dimension=0, tiled=True),
    )
    grad_qv_bias, grad_proj_bias, grad_up_bias, grad_down_bias, grad_ada_bias = lax.psum(
        (part_qv_bias, part_proj_bias, part_up_bias, part_down_bias, part_ada_bias), ("rows", "seq")
    )
    return (
        block_out,
        grad_tokens,
        grad_cond,
        grad_ada_weight,
        grad_ada_bias,
        grad_qkv_weight,
        grad_qv_bias,
        grad_proj_weight,
        grad_proj_bias,
        grad_up_weight,
        grad_up_bias,
        grad_down_weight,
        grad_down_bias,
    )


def solution(mesh):
    in_specs = (
        P("rows", "seq", None),
        P("rows", None),
        P("rows", None),
        P("rows", None),
        P("rows"),
        P(None, "seq"),
        P(),
        P(),
        P(),
        P(),
        P(),
        P(),
        P(),
        P(),
        P(),
        P("rows", "seq", None),
    )
    out_specs = (
        P("rows", "seq", None),
        P("rows", "seq", None),
        P("rows", None),
        P("rows", "seq"),
        P(),
        P("rows", "seq"),
        P(),
        P("rows", "seq"),
        P(),
        P("rows", "seq"),
        P(),
        P("rows", "seq"),
        P(),
    )
    return jax.shard_map(
        on_device, mesh=mesh, in_specs=in_specs, out_specs=out_specs, check_vma=False
    )
```

profile of v0, /device:TPU:0, one launch (start us, length us, event | category | flops | bytes accessed | tf_op | source)
XLA Modules:
  0.0 1624.1 jit_solution(7303756480098807431)
XLA Ops:
  13.1 11.3 all-gather
  37.1 6.5 fusion.106
  43.5 5.1 copy-done.4
  50.2 10.0 fusion.80
  60.2 5.8 copy.133
  66.0 17.1 %copy.134 = bf16[2,3,1152,256]{3,0,1,2:T(2,128)(2,1)} copy(bf16[2,3,1152,256]{3,2,1,0:T(8,128)(2,1)} %bitcast.193) | data formatting | bytes 7077888 | tf_op jit(solution)/shard_map/reshape | solution.py:130
  83.1 4.7 all-to-all-start
  87.8 38.6 %all-to-all-done = bf16[2,3,1152,256]{3,0,1,2:T(2,128)(2,1)} async-done(((bf16[2,3,1152,256]{3,0,1,2:T(2,128)(2,1)}), bf16[2,3,1152,256]{3,0,1,2:T(2,128)(2,1)}, u32[]{:S(2)}, u32[]{:S(2)}) %all-to-all-start) | async-done | bytes 3538976 | tf_op jit(solution)/shard_map/all_to_all | solution.py:133
  128.9 4.5 copy.136
  133.4 7.5 reshape.218
  140.9 47.4 %while.22 = (s32[]{:T(128)}, bf16[2,4,72,1024]{3,2,1,0:T(8,128)(2,1)}, f32[2,4,1024]{2,1,0:T(4,128)S(1)}, bf16[2,3,4,72,1024]{4,3,2,1,0:T(8,128)(2,1)}, s32[2,10...) while((s32[]{:T(128)}, bf16[2,4,72,1024]{3,2,1,0:T(8,128)(2,1)}, ...), condition=%wide.region_5.6_spmd, body=%wide.region_2.5_spmd.sunk | while | flops 1263825920 | bytes 128336072 | solution.py:135
  144.6 4.9 fusion.169
  149.5 3.7 fusion.170
  155.2 9.4 fusion.171
  168.3 4.9 fusion.169
  178.9 9.4 fusion.171
  188.3 4.8 copy.137
  193.1 4.5 all-to-all-start.1
  197.7 18.7 %all-to-all-done.1 = bf16[2,288,1024]{1,0,2:T(2,128)(2,1)} async-done(((bf16[2,288,1024]{1,0,2:T(2,128)(2,1)}), bf16[2,288,1024]{1,0,2:T(2,128)(2,1)}, u32[]{:S(2)}, u32[]{:S(2)}) %all-to-all-start.1) | async-done | bytes 1179680 | tf_op jit(solution)/shard_map/all_to_all | solution.py:136
  216.4 5.1 copy.164
  223.0 6.0 fusion.130
  232.7 13.4 fusion.63
  246.1 17.6 %convert_reduce_fusion = (f32[4608]{0:T(1024)}, bf16[2,256,4608]{2,1,0:T(8,128)(2,1)}) fusion(f32[2,256,4608]{2,1,0:T(8,128)} %fusion.63, f32[4608]{0:T(1024)S(1)} %convert_element_type.122, bf16[2,256,1152]{2,1,0:T(8,128)(2,1)S(1)} %get-tuple-element.198, bf16[4608,1152]{1,0:T(8,128)(2,1)} %param.33), kind=kOutput, calls=%fused_computation.81 | convolution fusion | flops 5490077184 | bytes 25989120 | tf_op jit(solution)/shard_map/rte,fe->rtf/dot_general | solution.py:163
  263.7 12.2 multiply_reduce_fusion.1
  275.9 16.2 fusion.129
  292.1 3.7 convert_reduce_fusion.4
  299.7 4.2 copy.141
  307.5 14.4 all-to-all-done.2
  326.7 159.9 %while.23 = (s32[]{:T(128)}, bf16[2,3,4,72,1024]{4,3,2,1,0:T(8,128)(2,1)}, bf16[2,3,4,72,1024]{4,3,2,1,0:T(8,128)(2,1)}, s32[2,1024]{1,0:T(2,128)S(1)}, s32[2]{0...) while((s32[]{:T(128)}, ...), condition=%wide.region_12.13_spmd, body=%wide.region_10.12_spmd.sunk | while | flops 3090066432 | bytes 196150960 | solution.py:190
  330.8 11.8 subtract_exponential_fusion.3
  342.6 9.2 fusion.179
  351.8 22.3 %fusion.181 = bf16[1,1,4,72,1024]{4,3,2,1,0:T(8,128)(2,1)S(1)} fusion(f32[4,1024,1024]{1,2,0:T(8,128)} %subtract_exponential_fusion.3, f32[4,1024,1024]{1,2,0:T(8,128)} %fusion.179, bf16[2,3,4,72,1024]{4,3,2,1,0:T(8,128)(2,1)} %get-tuple-element.362, s32[]{:T(128)} %get-tuple-element.349, s32[]{:T(128)S(6)} %add.324), kind=kOutput, calls=%fused_computation.40.clone.1 | convolution fusion | flops 625251328 | bytes 68289024 | tf_op jit(solution)/shard_map/while/body/eval_jaxpr/vmap(dk,qk->dq)/dot_general | solution.py:59
  374.1 22.8 %fusion.180 = bf16[1,1,4,72,1024]{4,3,2,1,0:T(8,128)(2,1)S(1)} fusion(f32[4,1024,1024]{1,2,0:T(8,128)} %subtract_exponential_fusion.3, f32[4,1024,1024]{1,2,0:T(8,128)} %fusion.179, bf16[2,3,4,72,1024]{4,3,2,1,0:T(8,128)(2,1)} %get-tuple-element.362, s32[]{:T(128)} %get-tuple-element.349), kind=kOutput, calls=%fused_computation.39.clone.1 | convolution fusion | flops 625251328 | bytes 68289024 | tf_op jit(solution)/shard_map/while/body/eval_jaxpr/vmap(dq,qk->dk)/dot_general | solution.py:60
  396.9 8.4 fusion.178
  410.4 11.8 subtract_exponential_fusion.3
  422.3 9.2 fusion.179
  431.4 22.3 %fusion.181 = bf16[1,1,4,72,1024]{4,3,2,1,0:T(8,128)(2,1)S(1)} fusion(f32[4,1024,1024]{1,2,0:T(8,128)} %subtract_exponential_fusion.3, f32[4,1024,1024]{1,2,0:T(8,128)} %fusion.179, bf16[2,3,4,72,1024]{4,3,2,1,0:T(8,128)(2,1)} %get-tuple-element.362, s32[]{:T(128)} %get-tuple-element.349, s32[]{:T(128)S(6)} %add.324), kind=kOutput, calls=%fused_computation.40.clone.1 | convolution fusion | flops 625251328 | bytes 68289024 | tf_op jit(solution)/shard_map/while/body/eval_jaxpr/vmap(dk,qk->dq)/dot_general | solution.py:59
  453.8 22.8 %fusion.180 = bf16[1,1,4,72,1024]{4,3,2,1,0:T(8,128)(2,1)S(1)} fusion(f32[4,1024,1024]{1,2,0:T(8,128)} %subtract_exponential_fusion.3, f32[4,1024,1024]{1,2,0:T(8,128)} %fusion.179, bf16[2,3,4,72,1024]{4,3,2,1,0:T(8,128)(2,1)} %get-tuple-element.362, s32[]{:T(128)} %get-tuple-element.349), kind=kOutput, calls=%fused_computation.39.clone.1 | convolution fusion | flops 625251328 | bytes 68289024 | tf_op jit(solution)/shard_map/while/body/eval_jaxpr/vmap(dq,qk->dk)/dot_general | solution.py:60
  476.6 8.4 fusion.178
  486.6 12.3 copy.144
  498.9 58.9 %all_to_all.68 = bf16[2,3,288,1024]{2,0,1,3:T(2,128)(2,1)} all-to-all(bf16[2,3,288,1024]{2,0,1,3:T(2,128)(2,1)} %copy.144), channel_id=1, replica_groups=mesh['rows'=8,'seq'=4] {'seq'}, dimensions={3} | all-to-all | bytes 7077888 | tf_op jit(solution)/shard_map/all_to_all | solution.py:191
  557.8 13.0 copy.165
  570.8 4.5 copy.146
  575.4 10.3 constant_dynamic-update-slice_fusion.1
  588.5 4.0 fusion.97
  597.9 4.6 fusion.119
  605.5 12.9 convolution_bitcast_fusion
  620.1 4.1 convolution_bitcast_fusion.3
  625.5 11.2 convolution_bitcast_fusion.2
  638.0 12.8 convolution_bitcast_fusion.1
  657.4 188.2 %reduce-scatter.29.cloned.1.call-done = f32[4608,288]{0,1:T(8,128)} async-done(((f32[4608,1152]{0,1:T(8,128)}), f32[4608,288]{0,1:T(8,128)}) %reduce-scatter.29.cloned.1.call-update) | async-done | bytes 5308432 | tf_op jit(solution)/shard_map/reduce_scatter | solution.py:232
  845.6 6.7 copy.172
  852.4 58.5 %reduce-scatter.23.cloned.1.call-done = f32[1152,288]{0,1:T(8,128)} async-done(((f32[1152,1152]{0,1:T(8,128)}), f32[1152,288]{0,1:T(8,128)}) %reduce-scatter.23.cloned.1.call-update) | async-done | bytes 1327120 | tf_op jit(solution)/shard_map/reduce_scatter | solution.py:230
  914.1 4.5 fusion.115
  918.6 142.8 %reduce-scatter.21.cloned.1.call-done = f32[1152,864]{0,1:T(8,128)} async-done(((f32[1152,3456]{0,1:T(8,128)}), f32[1152,864]{0,1:T(8,128)}) %reduce-scatter.21.cloned.1.call-update) | async-done | bytes 3981328 | tf_op jit(solution)/shard_map/reduce_scatter | solution.py:229
  1061.5 5.6 copy.168
  1067.1 187.3 %reduce-scatter.25.cloned.1.call-done = f32[1152,1152]{1,0:T(8,128)} async-done(((f32[1152,4608]{1,0:T(8,128)}), f32[1152,1152]{1,0:T(8,128)}) %reduce-scatter.25.cloned.1.call-update) | async-done | bytes 5308432 | tf_op jit(solution)/shard_map/reduce_scatter | solution.py:231
  1254.4 3.8 convert_reduce_fusion.1
  1258.7 41.6 %all-reduce = (f32[6912]{0:T(1024)}, f32[2,1152]{1,0:T(2,128)}, f32[1152]{0:T(1024)}, f32[4608]{0:T(1024)}, f32[1152]{0:T(1024)}) all-reduce(f32[6912]{0:T(1024)S(1)} %get-tuple-element.220, f32[2,1152]{1,0:T(2,128)S(1)} %pad_maximum_fusion.1, f32[1152]{0:T(1024)S(1)} %copy-done.39, ...), channel_id=1, replica_groups=mesh['rows'=8,'seq'=4] {'rows','seq'}, use_global_device_ids=true, to_apply=%region_19.20 | all-reduce | flops 16128 | bytes 129024 | tf_op jit(solution)/shard_map/psum | solution.py:241
  1301.9 77.6 %reduce-scatter.37.cloned.1.call-done = f32[576,288]{1,0:T(8,128)} async-done(((f32[4608,288]{1,0:T(8,128)}), f32[576,288]{1,0:T(8,128)}) %reduce-scatter.37.cloned.1.call-update) | async-done | bytes 663568
  1381.8 33.8 %reduce-scatter.35.cloned.1.call-done = f32[144,288]{1,0:T(8,128)} async-done(((f32[1152,288]{1,0:T(8,128)}), f32[144,288]{1,0:T(8,128)}) %reduce-scatter.35.cloned.1.call-update) | async-done | bytes 165904
  1415.6 89.3 %reduce-scatter.19.cloned.1.call-done = f32[144,1728]{1,0:T(8,128)} async-done(((f32[1152,1728]{1,0:T(8,128)}), f32[144,1728]{1,0:T(8,128)}) %reduce-scatter.19.cloned.1.call-update) | async-done | bytes 995344 | tf_op jit(solution)/shard_map/reduce_scatter | solution.py:239
  1504.9 50.7 %reduce-scatter.33.cloned.1.call-done = f32[144,864]{1,0:T(8,128)} async-done(((f32[1152,864]{1,0:T(8,128)}), f32[144,864]{1,0:T(8,128)}) %reduce-scatter.33.cloned.1.call-update) | async-done | bytes 497680
  1555.6 61.6 %reduce-scatter.27.cloned.1.call-done = f32[144,1152]{1,0:T(8,128)} async-done(((f32[1152,1152]{1,0:T(8,128)}), f32[144,1152]{1,0:T(8,128)}) %reduce-scatter.27.cloned.1.call-update) | async-done | bytes 663568 | tf_op jit(solution)/shard_map/reduce_scatter | solution.py:237
  (222 shorter events, 94.8 us)
Async XLA Ops:
  7.2 215.8 %copy-start = (bf16[1152,1152]{1,0:T(8,128)(2,1)S(1)}, bf16[1152,1152]{1,0:T(8,128)(2,1)}, u32[]{:S(2)}) copy-start(bf16[1152,1152]{1,0:T(8,128)(2,1)} %param.29) | copy-start | bytes 7962628
  37.0 11.6 copy-start.6
  37.0 11.6 copy-start.31
  37.0 11.6 copy-start.35
  43.5 5.1 copy-start.4
  83.1 43.4 %all-to-all-start = ((bf16[2,3,1152,256]{3,0,1,2:T(2,128)(2,1)}), bf16[2,3,1152,256]{3,0,1,2:T(2,128)(2,1)}, u32[]{:S(2)}, u32[]{:S(2)}) async-start(bf16[2,3,1152,256]{3,0,1,2:T(2,128)(2,1)} %copy.134), calls=%async_computation | async-start | bytes 7077888 | tf_op jit(solution)/shard_map/all_to_all | solution.py:133
  133.4 7.5 copy-start.29
  133.4 7.5 copy-start.56
  144.6 4.9 copy-start.3
  149.5 5.7 copy-start.2
  168.3 4.9 copy-start.3
  173.2 5.7 copy-start.2
  188.3 9.4 copy-start.53
  188.3 9.4 copy-start.52
  188.3 9.4 copy-start.54
  193.1 23.3 %all-to-all-start.1 = ((bf16[2,288,1024]{1,0,2:T(2,128)(2,1)}), bf16[2,288,1024]{1,0,2:T(2,128)(2,1)}, u32[]{:S(2)}, u32[]{:S(2)}) async-start(bf16[2,288,1024]{1,0,2:T(2,128)(2,1)} %copy.137), calls=%async_computation.1 | async-start | bytes 3145728 | tf_op jit(solution)/shard_map/all_to_all | solution.py:136
  197.7 78.2 %copy-start.46 = (f32[4608]{0:T(1024)}, f32[4608]{0:T(1024)S(1)}, u32[]{:S(2)}) copy-start(f32[4608]{0:T(1024)S(1)} %convert_element_type.122) | copy-start | bytes 55300
  221.5 8.0 copy-start.10
  223.0 6.1 copy-start.17
  223.0 8.1 copy-start.5
  229.1 46.8 %copy-start.8 = (f32[2,256,1152]{2,1,0:T(8,128)}, f32[2,256,1152]{2,1,0:T(8,128)S(1)}, u32[]{:S(2)}) copy-start(f32[2,256,1152]{2,1,0:T(8,128)S(1)} %get-tuple-element.204) | copy-start | bytes 7077892
  229.1 46.8 %copy-start.43 = (f32[2,256]{1,0:T(2,128)}, f32[2,256]{1,0:T(2,128)S(1)}, u32[]{:S(2)}) copy-start(f32[2,256]{1,0:T(2,128)S(1)} %broadcast_multiply_fusion) | copy-start | bytes 6148
  231.2 44.7 %copy-start.50 = (f32[2,256]{1,0:T(2,128)}, f32[2,256]{1,0:T(2,128)S(1)}, u32[]{:S(2)}) copy-start(f32[2,256]{1,0:T(2,128)S(1)} %fusion.124) | copy-start | bytes 6148
  232.7 13.4 copy-start.19
  232.7 13.4 copy-start.26
  275.8 16.3 %copy-start.15 = (f32[2,256,1152]{2,1,0:T(8,128)}, f32[2,256,1152]{2,1,0:T(8,128)S(1)}, u32[]{:S(2)}) copy-start(f32[2,256,1152]{2,1,0:T(8,128)S(1)} %get-tuple-element.217) | copy-start | bytes 7077892
  292.1 3.7 copy-start.12
  292.1 3.7 copy-start.37
  303.9 18.0 %all-to-all-start.2 = ((bf16[2,1152,256]{2,0,1:T(2,128)(2,1)}), bf16[2,1152,256]{2,0,1:T(2,128)(2,1)S(1)}, u32[]{:S(2)}, u32[]{:S(2)}) async-start(bf16[2,1152,256]{2,0,1:T(2,128)(2,1)} %copy.141), calls=%async_computation.2 | async-start | bytes 2359296 | tf_op jit(solution)/shard_map/all_to_all | solution.py:185
  307.4 345.1 %reduce-scatter.31.cloned.1.call-start = ((), (), s32[]{:S(2)}) async-start(), calls=%async_computation.21 | async-start | bytes 4423680
  570.8 4.5 copy-start.7
  570.8 4.5 copy-start.32
  575.4 10.4 copy-start.49
  575.4 10.4 copy-start.36
  585.7 2.8 copy-start.11
  585.7 2.8 copy-start.13
  585.7 2.8 copy-start.38
  588.5 4.1 copy-start.14
  592.6 1.7 copy-start.16
  594.3 1.7 copy-start.9
  594.3 1.7 copy-start.44
  594.3 1.7 copy-start.51
  595.9 1.7 copy-start.21
  596.3 1.5 copy-start.34
  597.8 4.6 copy-start.55
  603.0 2.5 copy-start.27
  603.0 2.5 copy-start.47
  605.4 240.1 %reduce-scatter.29.cloned.1.call-start = ((), (), s32[]{:S(2)}) async-start(), calls=%async_computation.20 | async-start | bytes 26542080 | tf_op jit(solution)/shard_map/reduce_scatter | solution.py:232
  618.4 1.6 copy-start.23
  618.5 292.4 %reduce-scatter.23.cloned.1.call-start = ((), (), s32[]{:S(2)}) async-start(), calls=%async_computation.17 | async-start | bytes 6635520 | tf_op jit(solution)/shard_map/reduce_scatter | solution.py:230
  624.2 1.4 copy-start.25
  624.2 437.3 %reduce-scatter.21.cloned.1.call-start = ((), (), s32[]{:S(2)}) async-start(), calls=%async_computation.16 | async-start | bytes 19906560 | tf_op jit(solution)/shard_map/reduce_scatter | solution.py:229
  636.7 617.6 %reduce-scatter.25.cloned.1.call-start = ((), (), s32[]{:S(2)}) async-start(), calls=%async_computation.18 | async-start | bytes 26542080 | tf_op jit(solution)/shard_map/reduce_scatter | solution.py:231
  650.8 649.5 %all-reduce.3.cloned.1.call-start = ((), (), s32[]{:S(2)}) async-start(), calls=%async_computation.14 | async-start | bytes 147456 | tf_op jit(solution)/shard_map/psum | solution.py:225
  657.3 722.1 %reduce-scatter.37.cloned.1.call-start = ((), (), s32[]{:S(2)}) async-start(), calls=%async_computation.24 | async-start | bytes 7962624
  852.3 61.8 %copy-start.28 = (bf16[16,1152]{1,0:T(8,128)(2,1)S(1)}, bf16[16,1152]{1,0:T(8,128)(2,1)}, u32[]{:S(2)}) copy-start(bf16[16,1152]{1,0:T(8,128)(2,1)} %param.21) | copy-start | bytes 110596
  852.3 563.3 %reduce-scatter.35.cloned.1.call-start = ((), (), s32[]{:S(2)}) async-start(), calls=%async_computation.23 | async-start | bytes 1990656
  914.0 590.9 %reduce-scatter.19.cloned.1.call-start = ((), (), s32[]{:S(2)}) async-start(), calls=%async_computation.15 | async-start | bytes 9289728 | tf_op jit(solution)/shard_map/reduce_scatter | solution.py:239
  918.6 637.0 %reduce-scatter.33.cloned.1.call-start = ((), (), s32[]{:S(2)}) async-start(), calls=%async_computation.22 | async-start | bytes 4644864
  1067.0 550.1 %reduce-scatter.27.cloned.1.call-start = ((), (), s32[]{:S(2)}) async-start(), calls=%async_computation.19 | async-start | bytes 5971968 | tf_op jit(solution)/shard_map/reduce_scatter | solution.py:237
  1254.4 4.3 copy-start.39
  1254.4 4.3 copy-start.42
  1254.4 4.3 copy-start.45
  1254.4 362.7 %copy-start.1 = (bf16[1152,1152]{1,0:T(8,128)(2,1)S(1)}, bf16[1152,1152]{1,0:T(8,128)(2,1)}, u32[]{:S(2)}) copy-start(bf16[1152,1152]{1,0:T(8,128)(2,1)} %param.29) | copy-start | bytes 7962628
  (9 other events, 8.1 us)
Sparse Core Ops, SparseCore 0:
  605.6 46.9 reduce-scatter.30
  655.6 189.9 reduce-scatter.28
  848.9 61.9 reduce-scatter.22
  914.2 147.2 reduce-scatter.20
  1064.4 189.9 reduce-scatter.24
  1258.0 40.4 all-reduce.2
  1300.8 78.6 reduce-scatter.36
  1382.3 33.2 reduce-scatter.34
  1418.5 86.3 reduce-scatter.18
  1507.8 47.7 reduce-scatter.32
  1558.5 58.6 reduce-scatter.26
where the time goes:
time: 1630 us; the launch traced here: 1620 us
  waiting for transfers between devices  963 us (59%)
  matrix products  330 us (20%)
  local copies, waits for them, and re-layouts  138 us (8%)
  blocking collectives  112 us (7%)
  other arithmetic  52.2 us (3%)
    reduce_scatter x1, waiting for transfers between devices, on_device(): lax.psum_scatter(part_down, 'seq', scatter_dimension=1, tiled=True)  188 us
    reduce_scatter x1, waiting for transfers between devices, on_device(): lax.psum_scatter(part_up, 'seq', scatter_dimension=1, tiled=True)  187 us
    unnamed x15, waiting for transfers between devices  164 us
    reduce_scatter x1, waiting for transfers between devices, on_device(): lax.psum_scatter(part_qkv, 'seq', scatter_dimension=1, tiled=True)  143 us
    reduce_scatter x1, waiting for transfers between devices, on_device(): lax.psum_scatter(part_ada, 'rows', scatter_dimension=0, tiled=True)  89.3 us
    reduce_scatter x1, waiting for transfers between devices, on_device(): lax.psum_scatter(over_seq[2], 'rows', scatter_dimension=0, tiled=True)  61.6 us
    all_to_all x1, blocking collectives, on_device(): lax.all_to_all(grad_heads.reshape(row_count, 3, heads_dev * head_size, fu...  58.9 us
    reduce_scatter x1, waiting for transfers between devices, on_device(): lax.psum_scatter(part_proj, 'seq', scatter_dimension=1, tiled=True)  58.5 us
  transfers between devices with their start and end apart: 14, of which 13 were waited for; matrix products, arithmetic and copies ran while one was open for 5% of the time, Pallas kernels for 0%

commit v1 on v0

v1 whole, which is shorter than its diff:
```python
from functools import partial
import math

import jax
import jax.numpy as jnp
from jax import lax
from jax.experimental import pallas as pl
from jax.experimental.pallas import tpu as pltpu
from jax.sharding import PartitionSpec as P

HEADS = 16
LOG2E = math.log2(math.e)
VMEM_LIMIT = 48 << 20
BF16 = jnp.bfloat16
F32 = jnp.float32

norm_eps = 1e-06


def modulate(values, offset, factor):
    center = values - jnp.mean(values, axis=-1, keepdims=True)
    spread = jnp.mean(center * center, axis=-1, keepdims=True)
    return center * lax.rsqrt(spread + norm_eps) * (1.0 + factor) + offset


def gelu_tanh(values):
    return jax.nn.gelu(values, approximate=True)


def swap(values, axis, mask):
    count = lax.axis_size(axis)
    return lax.ppermute(values, axis, [(i, i ^ mask) for i in range(count)])


def flip_blocks(values, axis, mask):
    return jnp.take(values, lax.iota(jnp.int32, values.shape[axis]) ^ mask, axis=axis)


def qkv_kernel(slot_row, seg, mod, tokens, weight, bias, normed_ref, qkv_ref):
    width = tokens.shape[-1]
    values = tokens[0].astype(F32)
    picked = (seg[0] == slot_row[...]).astype(BF16)
    table = mod[0]
    high = table.astype(BF16)
    rest = table - high.astype(F32)
    middle = rest.astype(BF16)
    last = (rest - middle.astype(F32)).astype(BF16)
    stacked = jnp.concatenate([high, middle, last], axis=0)
    per_token = jnp.dot(picked, stacked, preferred_element_type=F32)
    normed = modulate(values, per_token[:, :width], per_token[:, width:]).astype(BF16)
    normed_ref[0] = normed
    mixed = lax.dot_general(weight[...], normed, (((1,), (1,)), ((), ())), preferred_element_type=F32)
    mixed = (mixed + bias[...]).astype(BF16)
    _, parts, heads, size, _ = qkv_ref.shape
    for part in range(parts):
        for head in range(heads):
            start = (part * heads + head) * size
            qkv_ref[0, part, head] = mixed[start : start + size]


def project_qkv(tokens, seg, slot_mod, weight, bias, heads, block):
    rows, length, width = tokens.shape
    slots = slot_mod.shape[1]
    features = weight.shape[0]
    size = features // (3 * heads)
    slot_row = jnp.tile(lax.iota(jnp.int32, slots), 3)[None]
    return pl.pallas_call(
        qkv_kernel,
        grid=(rows, length // block),
        in_specs=[
            pl.BlockSpec((1, 3 * slots), lambda r, t: (0, 0)),
            pl.BlockSpec((1, block, 1), lambda r, t: (r, t, 0)),
            pl.BlockSpec((1, slots, 2 * width), lambda r, t: (r, 0, 0)),
            pl.BlockSpec((1, block, width), lambda r, t: (r, t, 0)),
            pl.BlockSpec((features, width), lambda r, t: (0, 0)),
            pl.BlockSpec((features, 1), lambda r, t: (0, 0)),
        ],
        out_specs=[
            pl.BlockSpec((1, block, width), lambda r, t: (r, t, 0)),
            pl.BlockSpec((1, 3, heads, size, block), lambda r, t: (r, 0, 0, 0, t)),
        ],
        out_shape=[
            jax.ShapeDtypeStruct((rows, length, width), BF16),
            jax.ShapeDtypeStruct((rows, 3, heads, size, length), BF16),
        ],
        compiler_params=pltpu.CompilerParams(vmem_limit_bytes=VMEM_LIMIT),
        cost_estimate=pl.CostEstimate(
            flops=2 * rows * length * width * features,
            bytes_accessed=2 * rows * length * (2 * width + features),
            transcendentals=0,
        ),
    )(slot_row, seg[:, :, None], slot_mod, tokens, weight, bias[:, None])


def attend_kernel(block, scale, code_col, code_row, query, key, value, out_ref, lse_ref):
    length = query.shape[-1]
    keys = key[0, 0].astype(F32).T.astype(BF16)
    values = value[0, 0]
    codes = code_col[0]
    for step in range(length // block):
        here = pl.ds(step * block, block)
        scores = jnp.dot(keys, query[0, 0, :, here], preferred_element_type=F32)
        scores = jnp.where(codes == code_row[0, :, here], scores * scale, -1e30)
        peak = jnp.max(scores, axis=0, keepdims=True)
        raised = jnp.exp2(scores - peak)
        total = jnp.sum(raised, axis=0, keepdims=True)
        probs = (raised * (1.0 / total)).astype(BF16)
        out_ref[0, 0, :, here] = jnp.dot(values, probs, preferred_element_type=F32).astype(BF16)
        lse_ref[0, 0, :, here] = peak + jnp.log2(total)


def attend(packed, col, row, block):
    rows, _, heads, size, length = packed.shape
    part = lambda j: pl.BlockSpec((1, None, 1, size, length), lambda r, h: (r, j, h, 0, 0))
    return pl.pallas_call(
        partial(attend_kernel, block, size**-0.5 * LOG2E),
        grid=(rows, heads),
        in_specs=[
            pl.BlockSpec((1, length, 1), lambda r, h: (r, 0, 0)),
            pl.BlockSpec((1, 1, length), lambda r, h: (r, 0, 0)),
            part(0),
            part(1),
            part(2),
        ],
        out_specs=[
            pl.BlockSpec((1, 1, size, length), lambda r, h: (r, h, 0, 0)),
            pl.BlockSpec((1, 1, 1, length), lambda r, h: (r, h, 0, 0)),
        ],
        out_shape=[
            jax.ShapeDtypeStruct((rows, heads, size, length), BF16),
            jax.ShapeDtypeStruct((rows, heads, 1, length), F32),
        ],
        compiler_params=pltpu.CompilerParams(vmem_limit_bytes=VMEM_LIMIT),
        cost_estimate=pl.CostEstimate(
            flops=8 * rows * heads * length * length * 128,
            bytes_accessed=8 * rows * heads * length * size,
            transcendentals=rows * heads * length * length,
        ),
    )(col, row, packed, packed, packed)


def attend_back_kernel(
    block, inner, scale, code_col, code_row, query, key, value, out, grad_out, lse, grad_ref, key_sum, value_sum, keys, values
):
    length = query.shape[-1]
    size = query.shape[-2]
    keys[...] = key[0, 0].astype(F32).T.astype(BF16)
    values[...] = value[0, 0].astype(F32).T.astype(BF16)
    for step in range(length // block):
        here = pl.ds(step * block, block)
        query_low = query[0, 0, :, here]
        grad_low = grad_out[0, 0, :, here]
        query_rows = query_low.astype(F32).T.astype(BF16)
        grad_rows = grad_low.astype(F32).T.astype(BF16)
        row_dot = jnp.sum(grad_low.astype(F32) * out[0, 0, :, here].astype(F32), axis=0, keepdims=True)
        grad_query = jnp.zeros((size, block), F32)
        for part in range(length // inner):
            there = pl.ds(part * inner, inner)
            scores = jnp.dot(keys[there, :], query_low, preferred_element_type=F32)
            scores = jnp.where(code_col[0, there, :] == code_row[0, :, here], scores * (scale * LOG2E), -1e30)
            probs = jnp.exp2(scores - lse[0, 0, :, here])
            grad_probs = jnp.dot(values[there, :], grad_low, preferred_element_type=F32)
            grad_raw = (probs * (grad_probs - row_dot) * scale).astype(BF16)
            value_part = jnp.dot(probs.astype(BF16), grad_rows, preferred_element_type=F32)
            key_part = jnp.dot(grad_raw, query_rows, preferred_element_type=F32)
            if step == 0:
                value_sum[there, :] = value_part
                key_sum[there, :] = key_part
            else:
                value_sum[there, :] += value_part
                key_sum[there, :] += key_part
            grad_query += jnp.dot(key[0, 0, :, there], grad_raw, preferred_element_type=F32)
        grad_ref[0, 0, 0, :, here] = grad_query.astype(BF16)
    grad_ref[0, 1, 0] = key_sum[...].T.astype(BF16)
    grad_ref[0, 2, 0] = value_sum[...].T.astype(BF16)


def attend_back(packed, out, grad_out, lse, col, row, block, inner):
    rows, _, heads, size, length = packed.shape
    part = lambda j: pl.BlockSpec((1, None, 1, size, length), lambda r, h: (r, j, h, 0, 0))
    whole = pl.BlockSpec((1, 1, size, length), lambda r, h: (r, h, 0, 0))
    return pl.pallas_call(
        partial(attend_back_kernel, block, inner, size**-0.5),
        grid=(rows, heads),
        in_specs=[
            pl.BlockSpec((1, length, 1), lambda r, h: (r, 0, 0)),
            pl.BlockSpec((1, 1, length), lambda r, h: (r, 0, 0)),
            part(0),
            part(1),
            part(2),
            whole,
            whole,
            pl.BlockSpec((1, 1, 1, length), lambda r, h: (r, h, 0, 0)),
        ],
        out_specs=pl.BlockSpec((1, 3, 1, size, length), lambda r, h: (r, 0, h, 0, 0)),
        out_shape=jax.ShapeDtypeStruct((rows, 3, heads, size, length), BF16),
        scratch_shapes=[
            pltpu.VMEM((length, size), F32),
            pltpu.VMEM((length, size), F32),
            pltpu.VMEM((length, size), BF16),
            pltpu.VMEM((length, size), BF16),
        ],
        compiler_params=pltpu.CompilerParams(vmem_limit_bytes=VMEM_LIMIT),
        cost_estimate=pl.CostEstimate(
            flops=20 * rows * heads * length * length * 128,
            bytes_accessed=16 * rows * heads * length * size,
            transcendentals=rows * heads * length * length,
        ),
    )(col, row, packed, packed, packed, out, grad_out, lse)


def gather_seq(values):
    count = lax.axis_size("seq")
    if count == 4:
        first, second = swap(values, "seq", 1), swap(values, "seq", 2)
        half = values.shape[0] // 2
        third = jnp.concatenate([swap(second[:half], "seq", 1), swap(first[half:], "seq", 2)], axis=0)
        return [values, first, second, third]
    return [values] + [swap(values, "seq", m) for m in range(1, count)]


def exchange_seq(blocks):
    return [blocks[0]] + [swap(blocks[m], "seq", m) for m in range(1, len(blocks))]


def sum_seq(values):
    total = values
    for m in range(1, lax.axis_size("seq")):
        total = total + swap(values, "seq", m)
    return total


def halve_seq(parts, order):
    index = lax.axis_index("seq")
    count = lax.axis_size("seq")
    shape = parts.shape[1:]
    bits = [count >> (k + 1) for k in range(count.bit_length() - 1)]
    current = parts.reshape((2,) * len(bits) + shape)
    left = list(bits)
    for bit in [bits[k] for k in order]:
        axis = left.index(bit)
        mine = (index // bit) % 2
        keep = lax.dynamic_index_in_dim(current, mine, axis, keepdims=False)
        send = lax.dynamic_index_in_dim(current, 1 - mine, axis, keepdims=False).astype(BF16)
        current = keep + swap(send, "seq", bit).astype(F32)
        left.pop(axis)
    return current


def reduce_weight(part):
    groups, index, count = lax.axis_size("rows"), lax.axis_index("rows"), lax.axis_size("seq")
    chips = groups // 2
    core = index % 2
    depth, width = part.shape[0] // groups, part.shape[1] // count
    view = part.reshape(chips, 2, depth, part.shape[1])
    keep = lax.dynamic_index_in_dim(view, core, 1, keepdims=False)
    send = lax.dynamic_index_in_dim(view, 1 - core, 1, keepdims=False).astype(BF16)
    both = keep + swap(send, "rows", 1).astype(F32)
    blocks = both.reshape(chips * depth, count, width).transpose(1, 0, 2)
    half = chips * depth // 2
    levels = count.bit_length() - 1
    up = halve_seq(blocks[:, :half], list(range(levels)))
    down = halve_seq(blocks[:, half:], list(range(levels))[::-1])
    summed = jnp.concatenate([up, down], axis=0).reshape(chips, depth, width)
    return spread_rows(summed)


def spread_rows(summed):
    chip = lax.axis_index("rows") // 2
    chips = summed.shape[0]
    total = lax.dynamic_index_in_dim(summed, chip, 0, keepdims=False)
    for m in range(1, chips):
        send = lax.dynamic_index_in_dim(summed, chip ^ m, 0, keepdims=False).astype(BF16)
        total = total + swap(send, "rows", 2 * m).astype(F32)
    return total


def on_device(
    tokens,
    conditioning,
    segment_ids,
    image_index,
    row_fill,
    ada_weight,
    ada_bias,
    qkv_weight,
    qv_bias,
    proj_weight,
    proj_bias,
    up_weight,
    up_bias,
    down_weight,
    down_bias,
    cotangent,
):
    row_count, local_len, width = tokens.shape
    seq_count = lax.axis_size("seq")
    seq_index = lax.axis_index("seq")
    row_index = lax.axis_index("rows")
    full_len = local_len * seq_count
    heads_dev = HEADS // seq_count
    head_size = width // HEADS
    own = heads_dev * head_size
    image_count = conditioning.shape[0]

    tokens_all = jnp.concatenate(gather_seq(tokens), axis=1)
    seg_blocks = flip_blocks(segment_ids.reshape(row_count, seq_count, local_len), 1, seq_index)
    seg_all = seg_blocks.reshape(row_count, full_len)
    places = (lax.iota(jnp.int32, seq_count) ^ seq_index)[:, None] * local_len + lax.iota(jnp.int32, local_len)
    places = places.reshape(1, full_len)
    codes = jnp.where(places < row_fill[:, None], seg_all, -1 - places)
    code_col, code_row = codes[:, :, None], codes[:, None, :]

    qkv_turned = qkv_weight.T.reshape(3, seq_count, own, width)
    qkv_order = flip_blocks(qkv_turned, 1, seq_index).transpose(1, 0, 2, 3)
    qkv_own = qkv_order[0].reshape(3 * own, width)
    qkv_back = qkv_order.reshape(3 * width, width)
    proj_order = flip_blocks(proj_weight.reshape(seq_count, own, width), 0, seq_index).reshape(width, width)
    bias_own = lax.dynamic_slice_in_dim(qv_bias.astype(F32), seq_index * own, own, 1)
    bias_own = jnp.concatenate([bias_own[0], jnp.zeros((own,), F32), bias_own[1]])

    cond_wide = conditioning.astype(F32)
    cond_low = jax.nn.silu(cond_wide).astype(BF16)
    cond_all = lax.all_gather(cond_low, "rows", axis=0, tiled=True)
    mod_part = jnp.dot(cond_low, ada_weight, preferred_element_type=F32)
    modulation = lax.all_gather(mod_part, "seq", axis=1, tiled=True) + ada_bias.astype(F32)
    local_seg = lax.dynamic_slice_in_dim(segment_ids, seq_index * local_len, local_len, 1)
    slot_ids = lax.iota(jnp.int32, image_index.shape[1])
    slot_mod = jnp.take(modulation, image_index, axis=0)

    normed_all, packed = project_qkv(
        tokens_all, seg_all, slot_mod[:, :, : 2 * width], qkv_own, bias_own, heads_dev, min(256, full_len)
    )
    attended, log_totals = attend(packed, code_col, code_row, 512)

    slot_pick = (local_seg[:, :, None] == slot_ids).astype(F32)
    mod_tok = jnp.einsum("rts,rse->rte", slot_pick, slot_mod, precision=lax.Precision.HIGHEST)
    shift_a, scale_a, gate_a, shift_b, scale_b, gate_b = jnp.split(mod_tok, 6, axis=-1)
    tokens_wide = tokens.astype(F32)

    def by_block(values):
        return [values[..., m * local_len : (m + 1) * local_len] for m in range(seq_count)]

    attended_tok = jnp.concatenate(
        exchange_seq(by_block(attended.reshape(row_count, own, full_len))), axis=1
    )
    branch_a = jnp.einsum(
        "rft,fe->rte", attended_tok, proj_order, preferred_element_type=F32
    ) + proj_bias.astype(F32)
    middle = tokens_wide + gate_a * branch_a
    normed_b = modulate(middle, shift_b, scale_b).astype(BF16)
    hidden_pre = jnp.einsum(
        "rtd,df->rtf", normed_b, up_weight, preferred_element_type=F32
    ) + up_bias.astype(F32)
    activated = gelu_tanh(hidden_pre).astype(BF16)
    branch_b = jnp.einsum(
        "rtf,fe->rte", activated, down_weight, preferred_element_type=F32
    ) + down_bias.astype(F32)
    block_out = (middle + gate_b * branch_b).astype(BF16)
    upstream = cotangent.astype(F32)
    grad_branch_b = (upstream * gate_b).astype(BF16)
    grad_gate_b = upstream * branch_b
    part_down_bias = jnp.sum(grad_branch_b.astype(F32), axis=(0, 1))
    grad_act = jnp.einsum("rte,fe->rtf", grad_branch_b, down_weight, preferred_element_type=F32)
    _, gelu_back = jax.vjp(gelu_tanh, hidden_pre)
    grad_pre = gelu_back(grad_act)[0].astype(BF16)
    part_up_bias = jnp.sum(grad_pre.astype(F32), axis=(0, 1))
    grad_normed_b = jnp.einsum("rtf,df->rtd", grad_pre, up_weight, preferred_element_type=F32)
    _, norm_back_b = jax.vjp(modulate, middle, shift_b, scale_b)
    grad_mid_norm, grad_shift_b, grad_scale_b = norm_back_b(grad_normed_b)
    grad_middle = upstream + grad_mid_norm
    grad_branch_a = (grad_middle * gate_a).astype(BF16)
    grad_gate_a = grad_middle * branch_a
    part_proj_bias = jnp.sum(grad_branch_a.astype(F32), axis=(0, 1))
    grad_attended = jnp.einsum(
        "fe,rte->rft", proj_order, grad_branch_a, preferred_element_type=F32
    ).astype(BF16)
    grad_heads_in = jnp.concatenate(
        exchange_seq([grad_attended[:, m * own : (m + 1) * own] for m in range(seq_count)]), axis=2
    )
    grad_view = grad_heads_in.reshape(row_count, heads_dev, head_size, full_len)

    part_down = jnp.einsum("rtf,rte->fe", activated, grad_branch_b, preferred_element_type=F32)
    part_up = jnp.einsum("rtd,rtf->df", normed_b, grad_pre, preferred_element_type=F32)
    attended_plain = flip_blocks(
        attended_tok.reshape(row_count, seq_count, own, local_len), 1, seq_index
    ).reshape(row_count, width, local_len)
    part_proj = jnp.einsum("rft,rte->fe", attended_plain, grad_branch_a, preferred_element_type=F32)
    grad_down_weight = reduce_weight(part_down)
    grad_up_weight = reduce_weight(part_up)
    grad_proj_weight = reduce_weight(part_proj)

    grad_heads = attend_back(packed, attended, grad_view, log_totals, code_col, code_row, 256, 512)
    grad_own = grad_heads.reshape(row_count, 3 * own, full_len)
    grad_flat = jnp.concatenate(exchange_seq(by_block(grad_own)), axis=1)
    grad_normed_a = jnp.einsum("rft,fd->rtd", grad_flat, qkv_back, preferred_element_type=F32)

    part_qkv = jnp.einsum("rft,rtd->fd", grad_own, normed_all, preferred_element_type=F32)
    own_sums = jnp.sum(grad_own.astype(F32), axis=(0, 2)).reshape(3, own)
    groups = lax.axis_size("rows")
    chips = groups // 2
    core = row_index % 2
    turned = part_qkv.T.reshape(chips, 2, width // groups, 3 * own)
    keep = lax.dynamic_index_in_dim(turned, core, 1, keepdims=False)
    send = lax.dynamic_index_in_dim(turned, 1 - core, 1, keepdims=False).astype(BF16)
    qkv_sum = spread_rows(keep + swap(send, "rows", 1).astype(F32))
    qkv_blocks = lax.all_gather(qkv_sum.astype(BF16), "seq", axis=0).reshape(seq_count, width // groups, 3, own)
    qkv_cols = qkv_blocks.transpose(1, 2, 0, 3).reshape(width // groups, 3 * width)
    grad_qkv_weight = lax.dynamic_slice_in_dim(
        qkv_cols, seq_index * (3 * width // seq_count), 3 * width // seq_count, 1
    ).astype(F32)

    _, norm_back_a = jax.vjp(modulate, tokens_wide, shift_a, scale_a)
    grad_tok_norm, grad_shift_a, grad_scale_a = norm_back_a(grad_normed_a)
    grad_tokens = grad_middle + grad_tok_norm
    grad_mod_tok = jnp.concatenate(
        [grad_shift_a, grad_scale_a, grad_gate_a, grad_shift_b, grad_scale_b, grad_gate_b], axis=-1
    )
    slot_grads = jnp.einsum("rts,rte->rse", slot_pick, grad_mod_tok, precision=lax.Precision.HIGHEST)
    image_pick = (image_index[:, :, None] == lax.iota(jnp.int32, image_count)).astype(F32)
    grad_modulation = jnp.einsum("rsi,rse->ie", image_pick, slot_grads, precision=lax.Precision.HIGHEST)
    part_ada_bias = jnp.sum(grad_modulation, axis=0)
    mod_view = grad_modulation.reshape(image_count, seq_count, -1)
    mod_blocks = [
        lax.dynamic_index_in_dim(mod_view, seq_index ^ m, 1, keepdims=False) for m in range(seq_count)
    ]
    mod_columns = sum(exchange_seq(mod_blocks))
    grad_mod_low = mod_columns.astype(BF16)
    grad_mod_all = lax.all_gather(grad_mod_low, "rows", axis=0, tiled=True)
    cond_cols = lax.dynamic_slice_in_dim(cond_all, row_index * (width // groups), width // groups, 1)
    grad_ada_weight = jnp.einsum("id,ie->de", cond_cols, grad_mod_all, preferred_element_type=F32)
    cond_term = jnp.einsum("ie,de->id", grad_mod_low, ada_weight, preferred_element_type=F32)
    grad_cond_low = sum_seq(cond_term)
    _, silu_back = jax.vjp(jax.nn.silu, cond_wide)
    grad_cond = silu_back(grad_cond_low)[0]

    part_qv_bias = jnp.zeros((2, seq_count, own), F32)
    part_qv_bias = lax.dynamic_update_slice(
        part_qv_bias, jnp.stack([own_sums[0], own_sums[2]])[:, None], (0, seq_index, 0)
    ).reshape(2, width)
    grad_proj_bias, grad_up_bias, grad_down_bias = lax.psum(
        (part_proj_bias, part_up_bias, part_down_bias), ("rows", "seq")
    )
    grad_qv_bias, grad_ada_bias = lax.psum((part_qv_bias, part_ada_bias), ("rows", "seq"))
    return (
        block_out,
        grad_tokens,
        grad_cond,
        grad_ada_weight,
        grad_ada_bias,
        grad_qkv_weight,
        grad_qv_bias,
        grad_proj_weight,
        grad_proj_bias,
        grad_up_weight,
        grad_up_bias,
        grad_down_weight,
        grad_down_bias,
    )


def solution(mesh):
    in_specs = (
        P("rows", "seq", None),
        P("rows", None),
        P("rows", None),
        P("rows", None),
        P("rows"),
        P(None, "seq"),
        P(),
        P(),
        P(),
        P(),
        P(),
        P(),
        P(),
        P(),
        P(),
        P("rows", "seq", None),
    )
    out_specs = (
        P("rows", "seq", None),
        P("rows", "seq", None),
        P("rows", None),
        P("rows", "seq"),
        P(),
        P("rows", "seq"),
        P(),
        P("rows", "seq"),
        P(),
        P("rows", "seq"),
        P(),
        P("rows", "seq"),
        P(),
    )
    return jax.shard_map(
        on_device, mesh=mesh, in_specs=in_specs, out_specs=out_specs, check_vma=False
    )
```

time: 1630 us -> 815 us (0.50)
  waiting for transfers between devices: 963 us -> 126 us
  matrix products: 330 us -> 133 us
  local copies, waits for them, and re-layouts: 138 us -> 241 us
  Pallas kernels: 0 us -> 57.1 us
  starting transfers between devices: 13.2 us -> 53.4 us
  other arithmetic: 52.2 us -> 78 us
    reduce_scatter x6 -> x0, waiting for transfers between devices: 728 us -> none  [the longest x1 188 us: on_device(): lax.psum_scatter(part_down, 'seq', scatter_dimension=1, tiled=True)]
    dot_general x25 -> x10, matrix products: 268 us -> 69.3 us  [the longest x1 13.4 us: on_device(): jnp.einsum('rtd,df->rtf', normed_b, up_weight, preferred_element_type=F32)]
    unnamed x15 -> x0, waiting for transfers between devices: 164 us -> none
    ppermute x0 -> x47, waiting for transfers between devices: none -> 126 us  [swap(): return lax.ppermute(values, axis, [(i, i ^ mask) for i in range(count)])]
    all_to_all x3 -> x0, waiting for transfers between devices: 71.7 us -> none  [the longest x1 38.6 us: on_device(): lax.all_to_all(packed, 'seq', split_axis=2, concat_axis=3, tiled=True)]
    all_gather x1 -> x4, blocking collectives: 11.3 us -> 73 us  [the longest x1 29 us: on_device(): cond_all = lax.all_gather(cond_low, 'rows', axis=0, tiled=True)]
    all_to_all x1 -> x0, blocking collectives: 58.9 us -> none  [on_device(): lax.all_to_all(grad_heads.reshape(row_count, 3, heads_dev * head_size, fu...]
    pallas_call x0 -> x3, Pallas kernels: none -> 57.1 us  [the longest x1 26.6 us: attend_back(): pl.pallas_call(partial(attend_back_kernel, block, inner, size ** (-0.5)),...]
  transfers between devices with their start and end apart: 14 -> 47, of which waited for: 13 -> 14; matrix products, arithmetic and copies ran while one was open for 5% -> 39% of each run, Pallas kernels for 0% -> 3%
where the time goes in v1:
time: 815 us; the launch traced here: 805 us
  local copies, waits for them, and re-layouts  241 us (30%)
  matrix products  133 us (16%)
  waiting for transfers between devices  126 us (15%)
  blocking collectives  115 us (14%)
  other arithmetic  78 us (10%)
  Pallas kernels  57.1 us (7%)
  starting transfers between devices  53.4 us (7%)
    ppermute x47, waiting for transfers between devices, swap(): return lax.ppermute(values, axis, [(i, i ^ mask) for i in range(count)])  126 us
    ppermute x47, starting transfers between devices, swap(): return lax.ppermute(values, axis, [(i, i ^ mask) for i in range(count)])  53.4 us
    reshape x4, local copies, waits for them, and re-layouts, reduce_weight(): blocks = both.reshape(chips * depth, count, width).transpose(1, 0, 2)  48.5 us
    unnamed x176, local copies, waits for them, and re-layouts  46.6 us
    psum x1, blocking collectives, on_device(): lax.psum((part_qv_bias, part_ada_bias), ('rows', 'seq'))  41.8 us
    gather x11, local copies, waits for them, and re-layouts, flip_blocks(): jnp.take(values, lax.iota(jnp.int32, values.shape[axis]) ^ mask, axis=axis)  29.2 us
    all_gather x1, blocking collectives, on_device(): cond_all = lax.all_gather(cond_low, 'rows', axis=0, tiled=True)  29 us
    pallas_call x1, Pallas kernels, attend_back(): pl.pallas_call(partial(attend_back_kernel, block, inner, size ** (-0.5)),...  26.6 us
  transfers between devices with their start and end apart: 47, of which 14 were waited for; matrix products, arithmetic and copies ran while one was open for 39% of the time, Pallas kernels for 3%

profile of v1, /device:TPU:0, one launch (start us, length us, event | category | flops | bytes accessed | tf_op | source)
XLA Modules:
  0.0 805.4 jit_solution(12920287213003310383)
XLA Ops:
  0.7 3.0 collective-permute-start
  7.1 11.6 %copy.182 = bf16[1152,3456]{0,1:T(8,128)(2,1)} copy(bf16[1152,3456]{1,0:T(8,128)(2,1)} %param.23) | data formatting | bytes 15925248 | tf_op args[7]
  18.7 4.0 mini-gather-slice.3
  22.7 4.8 mini-gather-slice.2
  34.0 3.3 convolution_bitcast_fusion.1
  37.3 8.8 %all-gather.1 = f32[4,1728,16]{1,2,0:T(8,128)S(1)} all-gather(f32[1,1728,16]{1,2,0:T(8,128)S(1)} %convolution_bitcast_fusion.1), channel_id=1, replica_groups=mesh['rows'=8,'seq'=4] {'seq'}, dimensions={0}, use_global_device_ids=true | all-gather | bytes 552960 | tf_op jit(solution)/shard_map/all_gather | solution.py:326
  54.9 4.7 copy.228
  59.7 5.6 gather_fusion.4
  65.2 4.0 copy.229
  69.3 4.7 gather_fusion.5
  74.0 5.0 maximum_select_fusion
  79.0 3.1 copy-done.23
  82.3 3.7 bitcast_select_fusion
  92.3 8.0 collective-permute-done.3
  102.2 4.4 maximum_maximum_fusion.tokens
  106.6 12.8 %shard_map.255 = (bf16[2,1024,1152]{2,1,0:T(8,128)(2,1)}, bf16[2,3,4,72,1024]{4,3,2,1,0:T(8,128)(2,1)}) custom-call(s32[1,24]{1,0:T(1,128)S(1)} %copy-done.5, s32[2,1024,1]{2,1,0:T(8,128)S(1)} %get-tuple-element.39.seg, f32[2,8,2304]{2,1,0:T(8,128)S(1)} %slice.126.mod, bf16[2,1024,1152]{2,1,0:T(8,128)(2,1)} %maximum_maximum_fusion.tokens, ...), custom_call_target="tpu_custom_call" | custom-call | flops 4076863488 | bytes 12976128 | tf_op jit(solution)/shard_map/pallas_call | solution.py:67
  121.5 17.7 %shard_map.256 = (bf16[2,4,72,1024]{3,2,1,0:T(8,128)(2,1)S(1)}, f32[2,4,1,1024]{3,2,1,0:T(1,128)S(1)}) custom-call(s32[2,1024,1]{2,1,0:T(8,128)S(1)} %get-tuple-element.38.code_col, s32[2,1,1024]{2,1,0:T(1,128)S(1)} %compare_select_fusion.1.code_row, bf16[2,3,4,72,1024]{4,3,2,1,0:T(8,128)(2,1)S(1)} %copy-done.6, bf16[2,3,4,72,1024]{4,3,2,1,0:T(8,128)(2,1)S(1)} %copy-done.6, ...), custom_call_target="tpu_custom_call" | custom-call | flops 8589934592 | bytes 4718592 | tf_op jit(solution)/shard_map/pallas_call | solution.py:115
  148.2 8.9 %fusion.88 = f32[2,256,6912]{2,1,0:T(8,128)} fusion(f32[2,8,6912]{2,1,0:T(8,128)S(1)} %copy-done.39, s32[2,256]{1,0:T(2,128)S(1)} %constant_dynamic-slice_fusion.12), kind=kOutput, calls=%fused_computation.195 | convolution fusion | flops 339742720 | bytes 14600192 | tf_op jit(solution)/shard_map/rts,rse->rte/dot_general | solution.py:337
  157.3 6.7 copy.195
  164.2 3.7 concatenate.33
  170.6 6.6 fusion.102
  181.0 13.4 %fusion.6 = f32[2,256,4608]{2,1,0:T(8,128)} fusion(bf16[2,256,1152]{2,1,0:T(8,128)(2,1)S(1)} %get-tuple-element.41, bf16[1152,4608]{1,0:T(8,128)(2,1)} %param.27), kind=kOutput, calls=%fused_computation.18 | convolution fusion | flops 5435817984 | bytes 21233664 | tf_op jit(solution)/shard_map/rtd,df->rtf/dot_general | solution.py:352
  194.4 14.4 %fusion.99 = f32[4608,1152,1]{1,0,2:T(8,128)} fusion(bf16[2,256,1152]{2,1,0:T(8,128)(2,1)S(1)} %get-tuple-element.31, f32[2,256,4608]{2,1,0:T(8,128)} %fusion.6, f32[4608]{0:T(1024)S(1)} %convert_element_type.334), kind=kOutput, calls=%fused_computation.244 | convolution fusion | flops 5459410944 | bytes 31868928 | tf_op jit(solution)/shard_map/rtf,rte->fe/dot_general | solution.py:383
  208.8 16.1 %convert_reduce_fusion = (f32[4608]{0:T(1024)S(1)}, bf16[2,256,4608]{2,1,0:T(8,128)(2,1)S(1)}) fusion(f32[2,256,4608]{2,1,0:T(8,128)} %fusion.6, f32[4608]{0:T(1024)S(1)} %convert_element_type.334, bf16[2,256,1152]{2,1,0:T(8,128)(2,1)} %copy-done.42, bf16[4608,1152]{1,0:T(8,128)(2,1)} %param.29), kind=kOutput, calls=%fused_computation.27 | convolution fusion | flops 5490077184 | bytes 25989120 | tf_op jit(solution)/shard_map/rte,fe->rtf/dot_general | solution.py:364
  224.9 12.3 %multiply_reduce_fusion = (f32[2,256]{1,0:T(2,128)S(1)}, f32[2,256,1152]{2,1,0:T(8,128)}) fusion(f32[2,256,1152]{2,1,0:T(8,128)S(1)} %get-tuple-element.37, f32[2,256]{1,0:T(2,128)S(1)} %broadcast_multiply_fusion.1, f32[2,256,6912]{2,1,0:T(8,128)} %fusion.88, bf16[2,256,4608]{2,1,0:T(8,128)(2,1)S(1)} %get-tuple-element.94, bf16[1152,4608]{1,0:T(8,128)(2,1)} %param.27), kind=kOutput, calls=%fused_computation.87 | convolution fusion | flops 5438766592 | bytes 22417408 | tf_op jit(solution)/shard_map/rtf,df->rtd/dot_general | solution.py:368
  237.2 11.5 %fusion.112 = f32[1152,4608,1]{1,0,2:T(8,128)} fusion(bf16[2,256,1152]{2,1,0:T(8,128)(2,1)} %copy-done.34, bf16[2,256,4608]{2,1,0:T(8,128)(2,1)S(1)} %get-tuple-element.94), kind=kOutput, calls=%fused_computation.256 | convolution fusion | flops 5435817984 | bytes 27131904 | tf_op jit(solution)/shard_map/rtd,rtf->df/dot_general | solution.py:384
  248.7 3.0 gather_fusion.3
  254.5 15.5 %fusion.101 = (f32[2,256]{1,0:T(2,128)S(1)}, f32[2,256,1152]{2,1,0:T(8,128)S(1)}, bf16[2,256,1152]{2,1,0:T(8,128)(2,1)}, f32[2,256,1152]{2,1,0:T(8,128)}) fusion(f32[2,256]{1,0:T(2,128)S(1)} %multiply_multiply_fusion.3, f32[2,256,1152]{2,1,0:T(8,128)S(1)} %copy-done.9, f32[2,256]{1,0:T(2,128)S(1)} %broadcast_multiply_fusion.1, f32[2,256]{1,0:T(2,128)S(1)} %fusion.94, ...), kind=kOutput, calls=%fused_computation.245 | convolution fusion | flops 5466488320 | bytes 35420672 | tf_op jit(solution)/shard_map/rtf,fe->rte/dot_general | solution.py:356
  270.0 3.1 convert_reduce_fusion.4
  284.9 7.0 fusion.18
  291.9 7.1 fusion.17
  302.0 26.6 %shard_map.257 = bf16[2,3,4,72,1024]{4,3,2,1,0:T(8,128)(2,1)} custom-call(s32[2,1024,1]{2,1,0:T(8,128)S(1)} %get-tuple-element.38.code_col, s32[2,1,1024]{2,1,0:T(1,128)S(1)} %copy-done.4, bf16[2,3,4,72,1024]{4,3,2,1,0:T(8,128)(2,1)} %get-tuple-element.17.query.key.value, bf16[2,3,4,72,1024]{4,3,2,1,0:T(8,128)(2,1)} %get-tuple-element.17.query.key.value, ...), custom_call_target="tpu_custom_call" | custom-call | flops 21474836480 | bytes 9437184 | tf_op jit(solution)/shard_map/pallas_call | solution.py:182
  328.6 3.6 fusion.106
  335.7 7.2 fusion.19
  349.3 6.5 collective-permute-done.12
  357.3 16.9 %collective-permute-done.11 = bf16[2,864,256]{2,1,0:T(8,128)(2,1)} collective-permute-done((bf16[2,864,256]{2,1,0:T(8,128)(2,1)}, bf16[2,864,256]{2,1,0:T(8,128)(2,1)}, u32[]{:S(2)}, u32[]{:S(2)}) %collective-permute-start.11) | collective-permute-done | bytes 884768 | tf_op jit(solution)/shard_map/ppermute | solution.py:32
  378.6 7.0 concatenate.35
  385.6 10.0 %fusion.31 = (f32[2,256]{1,0:T(2,128)S(1)}, f32[2,256]{1,0:T(2,128)S(1)}, f32[2,256,6912]{2,1,0:T(8,128)S(1)}, f32[2,256,1152]{2,1,0:T(8,128)S(1)}) fusion(bf16[2,256,1152]{2,1,0:T(8,128)(2,1)S(1)} %copy-done.17, f32[2,256]{1,0:T(2,128)S(1)} %broadcast_multiply_fusion, f32[2,256,6912]{2,1,0:T(8,128)} %fusion.88, bf16[2,3456,256]{1,2,0:T(8,128)(2,1)} %concatenate.35, ...), kind=kOutput, calls=%fused_computation.70 | convolution fusion | flops 4081581056 | bytes 19765248 | tf_op jit(solution)/shard_map/rft,fd->rtd/dot_general | solution.py:396
  398.4 4.3 fusion.34
  408.4 4.6 fusion.87
  418.1 41.8 %all-reduce = (f32[6912]{0:T(1024)}, f32[2,1152]{1,0:T(2,128)}, f32[1152]{0:T(1024)}, f32[4608]{0:T(1024)}, f32[1152]{0:T(1024)}) all-reduce(f32[6912]{0:T(1024)S(1)} %get-tuple-element.91, f32[2,1152]{1,0:T(2,128)S(1)} %reshape.499, f32[1152]{0:T(1024)S(1)} %get-tuple-element.32, ...), channel_id=1, replica_groups=mesh['rows'=8,'seq'=4] {'rows','seq'}, use_global_device_ids=true, to_apply=%region_9.10 | all-reduce | flops 16128 | bytes 129024 | tf_op jit(solution)/shard_map/psum | solution.py:444
  460.5 3.7 fusion.111
  470.4 15.6 %all_gather.17 = bf16[128,1728]{1,0:T(8,128)(2,1)} all-gather(bf16[16,1728]{1,0:T(8,128)(2,1)S(1)} %fusion.75), channel_id=1, replica_groups=mesh['rows'=8,'seq'=4] {'rows'}, dimensions={0}, use_global_device_ids=true | all-gather | bytes 497664 | tf_op jit(solution)/shard_map/all_gather | solution.py:429
  488.1 3.0 bitcast_add_fusion.6
  491.1 4.0 reshape.501
  512.8 29.0 %all_gather.16 = bf16[128,1152]{1,0:T(8,128)(2,1)S(1)} all-gather(bf16[16,1152]{1,0:T(8,128)(2,1)S(1)} %get-tuple-element.80), channel_id=1, replica_groups=mesh['rows'=8,'seq'=4] {'rows'}, dimensions={0}, use_global_device_ids=true | all-gather | bytes 331776 | tf_op jit(solution)/shard_map/all_gather | solution.py:324
  546.5 19.6 %all-gather = bf16[576,864]{1,0:T(8,128)(2,1)S(1)} all-gather(bf16[144,864]{1,0:T(8,128)(2,1)S(1)} %fusion.60), channel_id=2, replica_groups=mesh['rows'=8,'seq'=4] {'seq'}, dimensions={0}, use_global_device_ids=true | all-gather | bytes 1244160 | tf_op jit(solution)/shard_map/all_gather | solution.py:407
  574.3 3.8 collective-permute-done.25
  586.5 3.9 collective-permute-done.29
  591.1 10.5 %bitcast_add_fusion = f32[4,576,1152]{2,1,0:T(8,128)} fusion(bf16[4,576,1152]{2,1,0:T(8,128)(2,1)} %collective-permute-done.39, f32[4,2,576,1152]{3,2,1,0:T(8,128)} %bitcast.313, s32[]{:T(128)S(6)} %select_n.286), kind=kLoop, calls=%fused_computation.10 | loop fusion | flops 5308416 | bytes 26542084 | tf_op jit(solution)/shard_map/add | solution.py:258
  601.7 15.7 %reshape.580 = f32[2304,4,288]{2,1,0:T(4,128)} reshape(f32[4,576,1152]{2,1,0:T(8,128)} %bitcast_add_fusion) | data formatting | bytes 21233664 | tf_op jit(solution)/shard_map/reshape | solution.py:259
  617.4 15.5 %copy.219 = f32[2304,4,288]{0,2,1:T(8,128)} copy(f32[2304,4,288]{2,1,0:T(4,128)} %reshape.580) | data formatting | bytes 21233664 | tf_op jit(solution)/shard_map/reshape | solution.py:259
  632.9 4.9 fusion.103
  641.7 11.1 %bitcast_add_fusion.1 = f32[4,144,4608]{2,1,0:T(8,128)} fusion(bf16[4,144,4608]{2,1,0:T(8,128)(2,1)} %collective-permute-done.31, f32[4,2,144,4608]{3,2,1,0:T(8,128)} %bitcast.282, s32[]{:T(128)S(6)} %select_n.286), kind=kLoop, calls=%fused_computation.11 | loop fusion | flops 5308416 | bytes 26542084 | tf_op jit(solution)/shard_map/add | solution.py:258
  652.9 13.2 %reshape.506 = f32[576,4,1152]{2,1,0:T(4,128)} reshape(f32[4,144,4608]{2,1,0:T(8,128)} %bitcast_add_fusion.1) | data formatting | bytes 21233664 | tf_op jit(solution)/shard_map/reshape | solution.py:259
  666.0 9.8 %fusion.104 = (f32[4,288,1152]{2,0,1:T(4,128)}, f32[4,288,1152]{2,0,1:T(4,128)}) fusion(f32[4,576,1152]{2,0,1:T(4,128)} %bitcast.283), kind=kLoop, calls=%fused_computation.248 | loop fusion | bytes 21233664 | tf_op jit(solution)/shard_map/slice | solution.py:262
  675.9 8.2 %reshape.507 = f32[2,2,288,1152]{3,1,0,2:T(2,128)} reshape(f32[4,288,1152]{2,0,1:T(4,128)} %get-tuple-element.44) | data formatting | bytes 10616832 | tf_op jit(solution)/shard_map/reshape | solution.py:238
  684.1 2.8 constant_dynamic-slice_fusion.1
  694.5 21.9 %collective-permute-done.32 = bf16[2,288,1152]{2,1,0:T(8,128)(2,1)S(1)} collective-permute-done((bf16[2,288,1152]{2,1,0:T(8,128)(2,1)S(1)}, bf16[2,288,1152]{2,1,0:T(8,128)(2,1)S(1)}, u32[]{:S(2)}, u32[]{:S(2)}) %collective-permute-start.32) | collective-permute-done | bytes 1327136 | tf_op jit(solution)/shard_map/ppermute | solution.py:32
  717.7 2.9 collective-permute-done.34
  724.9 21.1 %collective-permute-done.33 = bf16[288,1152]{1,0:T(8,128)(2,1)S(1)} collective-permute-done((bf16[288,1152]{1,0:T(8,128)(2,1)S(1)}, bf16[288,1152]{1,0:T(8,128)(2,1)S(1)}, u32[]{:S(2)}, u32[]{:S(2)}) %collective-permute-start.33) | collective-permute-done | bytes 663584 | tf_op jit(solution)/shard_map/ppermute | solution.py:32
  753.1 3.6 reshape.514
  765.4 30.7 %collective-permute-done.37 = bf16[144,1152]{1,0:T(8,128)(2,1)} collective-permute-done((bf16[144,1152]{1,0:T(8,128)(2,1)}, bf16[144,1152]{1,0:T(8,128)(2,1)}, u32[]{:S(2)}, u32[]{:S(2)}) %collective-permute-start.37) | collective-permute-done | bytes 331808 | tf_op jit(solution)/shard_map/ppermute | solution.py:32
  798.4 5.5 collective-permute-done.45
  (390 shorter events, 175.5 us)
Async XLA Ops:
  0.6 51.8 %copy-start = (bf16[1152,1152]{1,0:T(8,128)(2,1)S(1)}, bf16[1152,1152]{1,0:T(8,128)(2,1)}, u32[]{:S(2)}) copy-start(bf16[1152,1152]{1,0:T(8,128)(2,1)} %param.25) | copy-start | bytes 7962628
  0.7 85.4 %collective-permute-start = (bf16[2,256,1152]{2,1,0:T(8,128)(2,1)}, bf16[2,256,1152]{2,1,0:T(8,128)(2,1)}, u32[]{:S(2)}, u32[]{:S(2)}) collective-permute-start(bf16[2,256,1152]{2,1,0:T(8,128)(2,1)} %param.16), channel_id=1, source_target_pairs={{0,1},{1,0},{2,3},{3,2},{4,5},{5,4},{6,7},{7,6},{8,9},{9,8},{10,11... | collective-permute-start | bytes 3538952 | tf_op jit(solution)/shard_map/ppermute | solution.py:32
  3.7 85.7 %collective-permute-start.1 = (bf16[2,256,1152]{2,1,0:T(8,128)(2,1)}, bf16[2,256,1152]{2,1,0:T(8,128)(2,1)}, u32[]{:S(2)}, u32[]{:S(2)}) collective-permute-start(bf16[2,256,1152]{2,1,0:T(8,128)(2,1)} %param.16), channel_id=1, source_target_pairs={{0,2},{1,3},{2,0},{3,1},{4,6},{5,7},{6,4},{7,5},{8,10},{9,11},{10,... | collective-permute-start | bytes 3538952 | tf_op jit(solution)/shard_map/ppermute | solution.py:32
  5.2 23.0 %copy-start.66 = (pred[4]{0:T(512)(128)(4,1)}, pred[4]{0:T(512)(128)(4,1)S(1)}, u32[]{:S(2)}) copy-start(pred[4]{0:T(512)(128)(4,1)S(1)} %compare_and_fusion) | copy-start | bytes 16
  86.1 16.2 %copy-start.16 = (bf16[2,256,1152]{2,1,0:T(8,128)(2,1)S(1)}, bf16[2,256,1152]{2,1,0:T(8,128)(2,1)}, u32[]{:S(2)}) copy-start(bf16[2,256,1152]{2,1,0:T(8,128)(2,1)} %param.16) | copy-start | bytes 3538948
  87.3 13.0 %collective-permute-start.3 = (bf16[1,256,1152]{2,1,0:T(8,128)(2,1)S(1)}, bf16[1,256,1152]{2,1,0:T(8,128)(2,1)S(1)}, u32[]{:S(2)}, u32[]{:S(2)}) collective-permute-start(bf16[1,256,1152]{2,1,0:T(8,128)(2,1)S(1)} %slice.128), channel_id=1, source_target_pairs={{0,2},{1,3},{2,0},{3,1},{4,6},{5,7},{6,4},{7,5},{8,10},{9,11},{10,... | collective-permute-start | bytes 1769480 | tf_op jit(solution)/shard_map/ppermute | solution.py:32
  90.5 11.8 %collective-permute-start.2 = (bf16[1,256,1152]{2,1,0:T(8,128)(2,1)S(1)}, bf16[1,256,1152]{2,1,0:T(8,128)(2,1)S(1)}, u32[]{:S(2)}, u32[]{:S(2)}) collective-permute-start(bf16[1,256,1152]{2,1,0:T(8,128)(2,1)S(1)} %slice.127), channel_id=1, source_target_pairs={{0,1},{1,0},{2,3},{3,2},{4,5},{5,4},{6,7},{7,6},{8,9},{9,8},{10,11... | collective-permute-start | bytes 1769480 | tf_op jit(solution)/shard_map/ppermute | solution.py:32
  91.3 57.0 %copy-start.52 = (s32[2,256]{1,0:T(2,128)}, s32[2,256]{1,0:T(2,128)S(1)}, u32[]{:S(2)}) copy-start(s32[2,256]{1,0:T(2,128)S(1)} %constant_dynamic-slice_fusion.12) | copy-start | bytes 6148
  91.4 28.1 %copy-start.3 = (s32[2,1,1024]{2,1,0:T(1,128)}, s32[2,1,1024]{2,1,0:T(1,128)S(1)}, u32[]{:S(2)}) copy-start(s32[2,1,1024]{2,1,0:T(1,128)S(1)} %compare_select_fusion.1.code_row) | copy-start | bytes 24580
  92.3 14.4 %copy-start.2 = (f32[864,1]{1,0:T(8,128)S(1)}, f32[864,1]{1,0:T(8,128)}, u32[]{:S(2)}) copy-start(f32[864,1]{1,0:T(8,128)} %broadcast_in_dim.144.bias) | copy-start | bytes 10372
  92.3 14.3 %copy-start.5 = (s32[1,24]{1,0:T(1,128)S(1)}, s32[1,24]{1,0:T(1,128)}, u32[]{:S(2)}) copy-start(s32[1,24]{1,0:T(1,128)} %broadcast_in_dim_tile.3.slot_row) | copy-start | bytes 292
  144.7 12.4 %copy-start.64 = (bf16[1152]{0:T(1024)(128)(2,1)S(1)}, bf16[1152]{0:T(1024)(128)(2,1)}, u32[]{:S(2)}) copy-start(bf16[1152]{0:T(1024)(128)(2,1)} %param.30) | copy-start | bytes 6916
  144.7 12.4 %copy-start.61 = (bf16[4608]{0:T(1024)(128)(2,1)S(1)}, bf16[4608]{0:T(1024)(128)(2,1)}, u32[]{:S(2)}) copy-start(bf16[4608]{0:T(1024)(128)(2,1)} %param.28) | copy-start | bytes 27652
  144.7 19.4 %collective-permute-start.4 = (bf16[2,288,256]{1,2,0:T(8,128)(2,1)}, bf16[2,288,256]{1,2,0:T(8,128)(2,1)S(1)}, u32[]{:S(2)}, u32[]{:S(2)}) collective-permute-start(bf16[2,288,256]{1,2,0:T(8,128)(2,1)} %copy.231), channel_id=1, source_target_pairs={{0,1},{1,0},{2,3},{3,2},{4,5},{5,4},{6,7},{7,6},{8,9},{9,8},{10,11... | collective-permute-start | bytes 884744 | tf_op jit(solution)/shard_map/ppermute | solution.py:32
  145.8 18.4 %collective-permute-start.5 = (bf16[2,288,256]{1,2,0:T(8,128)(2,1)}, bf16[2,288,256]{1,2,0:T(8,128)(2,1)}, u32[]{:S(2)}, u32[]{:S(2)}) collective-permute-start(bf16[2,288,256]{1,2,0:T(8,128)(2,1)} %copy.232), channel_id=1, source_target_pairs={{0,2},{1,3},{2,0},{3,1},{4,6},{5,7},{6,4},{7,5},{8,10},{9,11},{10,... | collective-permute-start | bytes 884744 | tf_op jit(solution)/shard_map/ppermute | solution.py:32
  146.8 17.4 %collective-permute-start.6 = (bf16[2,288,256]{1,2,0:T(8,128)(2,1)}, bf16[2,288,256]{1,2,0:T(8,128)(2,1)}, u32[]{:S(2)}, u32[]{:S(2)}) collective-permute-start(bf16[2,288,256]{1,2,0:T(8,128)(2,1)} %copy.233), channel_id=1, source_target_pairs={{0,3},{1,2},{2,1},{3,0},{4,7},{5,6},{6,5},{7,4},{8,11},{9,10},{10,... | collective-permute-start | bytes 884744 | tf_op jit(solution)/shard_map/ppermute | solution.py:32
  177.2 47.6 %copy-start.8 = (f32[2,256,1152]{2,1,0:T(8,128)}, f32[2,256,1152]{2,1,0:T(8,128)S(1)}, u32[]{:S(2)}) copy-start(f32[2,256,1152]{2,1,0:T(8,128)S(1)} %get-tuple-element.37) | copy-start | bytes 7077892
  181.0 13.4 %copy-start.34 = (bf16[2,256,1152]{2,1,0:T(8,128)(2,1)}, bf16[2,256,1152]{2,1,0:T(8,128)(2,1)S(1)}, u32[]{:S(2)}) copy-start(bf16[2,256,1152]{2,1,0:T(8,128)(2,1)S(1)} %get-tuple-element.41) | copy-start | bytes 3538948
  181.0 13.4 %copy-start.42 = (bf16[2,256,1152]{2,1,0:T(8,128)(2,1)}, bf16[2,256,1152]{2,1,0:T(8,128)(2,1)S(1)}, u32[]{:S(2)}) copy-start(bf16[2,256,1152]{2,1,0:T(8,128)(2,1)S(1)} %get-tuple-element.31) | copy-start | bytes 3538948
  275.6 23.4 %collective-permute-start.9 = (bf16[2,288,256]{1,2,0:T(8,128)(2,1)S(1)}, bf16[2,288,256]{1,2,0:T(8,128)(2,1)S(1)}, u32[]{:S(2)}, u32[]{:S(2)}) collective-permute-start(bf16[2,288,256]{1,2,0:T(8,128)(2,1)S(1)} %get-tuple-element.65), channel_id=1, source_target_pairs={{0,3},{1,2},{2,1},{3,0},{4,7},{5,6},{6,5},{7,4},{8,11},{9,10},{10,... | collective-permute-start | bytes 884744 | tf_op jit(solution)/shard_map/ppermute | solution.py:32
  277.1 21.9 %collective-permute-start.8 = (bf16[2,288,256]{1,2,0:T(8,128)(2,1)S(1)}, bf16[2,288,256]{1,2,0:T(8,128)(2,1)S(1)}, u32[]{:S(2)}, u32[]{:S(2)}) collective-permute-start(bf16[2,288,256]{1,2,0:T(8,128)(2,1)S(1)} %get-tuple-element.66), channel_id=1, source_target_pairs={{0,2},{1,3},{2,0},{3,1},{4,6},{5,7},{6,4},{7,5},{8,10},{9,11},{10,... | collective-permute-start | bytes 884744 | tf_op jit(solution)/shard_map/ppermute | solution.py:32
  278.1 20.9 %collective-permute-start.7 = (bf16[2,288,256]{1,2,0:T(8,128)(2,1)S(1)}, bf16[2,288,256]{1,2,0:T(8,128)(2,1)S(1)}, u32[]{:S(2)}, u32[]{:S(2)}) collective-permute-start(bf16[2,288,256]{1,2,0:T(8,128)(2,1)S(1)} %get-tuple-element.67), channel_id=1, source_target_pairs={{0,1},{1,0},{2,3},{3,2},{4,5},{5,4},{6,7},{7,6},{8,9},{9,8},{10,11... | collective-permute-start | bytes 884744 | tf_op jit(solution)/shard_map/ppermute | solution.py:32
  284.9 201.0 %collective-permute-start.23 = (bf16[4,144,1152]{2,1,0:T(8,128)(2,1)}, bf16[4,144,1152]{2,1,0:T(8,128)(2,1)}, u32[]{:S(2)}, u32[]{:S(2)}) collective-permute-start(bf16[4,144,1152]{2,1,0:T(8,128)(2,1)} %fusion.40), channel_id=1, source_target_pairs={{0,4},{4,0},{8,12},{12,8},{16,20},{20,16},{24,28},{28,24},{1,5},{5... | collective-permute-start | bytes 3981320 | tf_op jit(solution)/shard_map/ppermute | solution.py:32
  332.3 23.5 %collective-permute-start.12 = (bf16[2,864,256]{2,1,0:T(8,128)(2,1)S(1)}, bf16[2,864,256]{2,1,0:T(8,128)(2,1)}, u32[]{:S(2)}, u32[]{:S(2)}) collective-permute-start(bf16[2,864,256]{2,1,0:T(8,128)(2,1)S(1)} %get-tuple-element.50), channel_id=1, source_target_pairs={{0,3},{1,2},{2,1},{3,0},{4,7},{5,6},{6,5},{7,4},{8,11},{9,10},{10,... | collective-permute-start | bytes 2654216 | tf_op jit(solution)/shard_map/ppermute | solution.py:32
  333.7 40.5 %collective-permute-start.11 = (bf16[2,864,256]{2,1,0:T(8,128)(2,1)}, bf16[2,864,256]{2,1,0:T(8,128)(2,1)}, u32[]{:S(2)}, u32[]{:S(2)}) collective-permute-start(bf16[2,864,256]{2,1,0:T(8,128)(2,1)} %get-tuple-element.51), channel_id=1, source_target_pairs={{0,2},{1,3},{2,0},{3,1},{4,6},{5,7},{6,4},{7,5},{8,10},{9,11},{10,... | collective-permute-start | bytes 2654216 | tf_op jit(solution)/shard_map/ppermute | solution.py:32
  334.7 41.7 %collective-permute-start.10 = (bf16[2,864,256]{2,1,0:T(8,128)(2,1)}, bf16[2,864,256]{2,1,0:T(8,128)(2,1)}, u32[]{:S(2)}, u32[]{:S(2)}) collective-permute-start(bf16[2,864,256]{2,1,0:T(8,128)(2,1)} %get-tuple-element.52), channel_id=1, source_target_pairs={{0,1},{1,0},{2,3},{3,2},{4,5},{5,4},{6,7},{7,6},{8,9},{9,8},{10,11... | collective-permute-start | bytes 2654216 | tf_op jit(solution)/shard_map/ppermute | solution.py:32
  348.7 118.3 %collective-permute-start.19 = (bf16[4,144,864]{2,1,0:T(8,128)(2,1)}, bf16[4,144,864]{2,1,0:T(8,128)(2,1)}, u32[]{:S(2)}, u32[]{:S(2)}) collective-permute-start(bf16[4,144,864]{2,1,0:T(8,128)(2,1)} %fusion.49), channel_id=1, source_target_pairs={{0,4},{4,0},{8,12},{12,8},{16,20},{20,16},{24,28},{28,24},{1,5},{5... | collective-permute-start | bytes 2985992 | tf_op jit(solution)/shard_map/ppermute | solution.py:32
  413.0 75.0 %slice-start.2 = ((s8[5308416]{0:T(1024)(128)(4,1)}), s8[1114112]{0:T(1024)(128)(4,1)S(1)}, s32[]{:S(2)}) async-start(s8[5308416]{0:T(1024)(128)(4,1)} %bitcast.291), calls=%async_computation.2 | async-start | bytes 2228224
  414.4 45.6 %collective-permute-start.13 = (f32[16,1728]{1,0:T(8,128)S(1)}, f32[16,1728]{1,0:T(8,128)S(1)}, u32[]{:S(2)}, u32[]{:S(2)}) collective-permute-start(f32[16,1728]{1,0:T(8,128)S(1)} %bitcast.330), channel_id=1, source_target_pairs={{0,1},{1,0},{2,3},{3,2},{4,5},{5,4},{6,7},{7,6},{8,9},{9,8},{10,11... | collective-permute-start | bytes 331784 | tf_op jit(solution)/shard_map/ppermute | solution.py:32
  415.4 44.5 %collective-permute-start.14 = (f32[16,1728]{1,0:T(8,128)S(1)}, f32[16,1728]{1,0:T(8,128)S(1)}, u32[]{:S(2)}, u32[]{:S(2)}) collective-permute-start(f32[16,1728]{1,0:T(8,128)S(1)} %bitcast.329), channel_id=1, source_target_pairs={{0,2},{1,3},{2,0},{3,1},{4,6},{5,7},{6,4},{7,5},{8,10},{9,11},{10,... | collective-permute-start | bytes 331784 | tf_op jit(solution)/shard_map/ppermute | solution.py:32
  416.4 44.0 %collective-permute-start.15 = (f32[16,1728]{1,0:T(8,128)S(1)}, f32[16,1728]{1,0:T(8,128)S(1)}, u32[]{:S(2)}, u32[]{:S(2)}) collective-permute-start(f32[16,1728]{1,0:T(8,128)S(1)} %bitcast.328), channel_id=1, source_target_pairs={{0,3},{1,2},{2,1},{3,0},{4,7},{5,6},{6,5},{7,4},{8,11},{9,10},{10,... | collective-permute-start | bytes 331784 | tf_op jit(solution)/shard_map/ppermute | solution.py:32
  460.0 131.1 %collective-permute-start.39 = (bf16[4,576,1152]{2,1,0:T(8,128)(2,1)}, bf16[4,576,1152]{2,1,0:T(8,128)(2,1)}, u32[]{:S(2)}, u32[]{:S(2)}) collective-permute-start(bf16[4,576,1152]{2,1,0:T(8,128)(2,1)} %fusion.17), channel_id=1, source_target_pairs={{0,4},{4,0},{8,12},{12,8},{16,20},{20,16},{24,28},{28,24},{1,5},{5... | collective-permute-start | bytes 15925256 | tf_op jit(solution)/shard_map/ppermute | solution.py:32
  460.0 181.7 %collective-permute-start.31 = (bf16[4,144,4608]{2,1,0:T(8,128)(2,1)}, bf16[4,144,4608]{2,1,0:T(8,128)(2,1)}, u32[]{:S(2)}, u32[]{:S(2)}) collective-permute-start(bf16[4,144,4608]{2,1,0:T(8,128)(2,1)} %fusion.18), channel_id=1, source_target_pairs={{0,4},{4,0},{8,12},{12,8},{16,20},{20,16},{24,28},{28,24},{1,5},{5... | collective-permute-start | bytes 15925256 | tf_op jit(solution)/shard_map/ppermute | solution.py:32
  460.5 27.5 %slice-start.3 = ((s8[5308416]{0:T(1024)(128)(4,1)}), s8[4194304]{0:T(1024)(128)(4,1)S(1)}, s32[]{:S(2)}) async-start(s8[5308416]{0:T(1024)(128)(4,1)} %bitcast.291), calls=%async_computation.3 | async-start | bytes 8388608
  464.2 43.5 %collective-permute-start.18 = (f32[16,1152]{1,0:T(8,128)}, f32[16,1152]{1,0:T(8,128)}, u32[]{:S(2)}, u32[]{:S(2)}) collective-permute-start(f32[16,1152]{1,0:T(8,128)} %fusion.111), channel_id=1, source_target_pairs={{0,3},{1,2},{2,1},{3,0},{4,7},{5,6},{6,5},{7,4},{8,11},{9,10},{10,... | collective-permute-start | bytes 221192 | tf_op jit(solution)/shard_map/ppermute | solution.py:32
  467.0 41.0 %collective-permute-start.17 = (f32[16,1152]{1,0:T(8,128)}, f32[16,1152]{1,0:T(8,128)}, u32[]{:S(2)}, u32[]{:S(2)}) collective-permute-start(f32[16,1152]{1,0:T(8,128)} %fusion.111), channel_id=1, source_target_pairs={{0,2},{1,3},{2,0},{3,1},{4,6},{5,7},{6,4},{7,5},{8,10},{9,11},{10,... | collective-permute-start | bytes 221192 | tf_op jit(solution)/shard_map/ppermute | solution.py:32
  469.3 18.7 %copy-start.31 = (f32[4,144,864]{2,1,0:T(8,128)}, f32[4,144,864]{2,1,0:T(8,128)S(1)}, u32[]{:S(2)}) copy-start(f32[4,144,864]{2,1,0:T(8,128)S(1)} %bitcast_add_fusion.7) | copy-start | bytes 5971972
  486.0 24.0 %collective-permute-start.16 = (f32[16,1152]{1,0:T(8,128)}, f32[16,1152]{1,0:T(8,128)}, u32[]{:S(2)}, u32[]{:S(2)}) collective-permute-start(f32[16,1152]{1,0:T(8,128)} %fusion.111), channel_id=1, source_target_pairs={{0,1},{1,0},{2,3},{3,2},{4,5},{5,4},{6,7},{7,6},{8,9},{9,8},{10,11... | collective-permute-start | bytes 221192 | tf_op jit(solution)/shard_map/ppermute | solution.py:32
  503.9 37.9 %copy-start.41 = (bf16[128,1728]{1,0:T(8,128)(2,1)S(1)}, bf16[128,1728]{1,0:T(8,128)(2,1)}, u32[]{:S(2)}) copy-start(bf16[128,1728]{1,0:T(8,128)(2,1)} %all_gather.17) | copy-start | bytes 1327108
  507.7 35.5 %collective-permute-start.20 = (bf16[144,864]{1,0:T(8,128)(2,1)S(1)}, bf16[144,864]{1,0:T(8,128)(2,1)S(1)}, u32[]{:S(2)}, u32[]{:S(2)}) collective-permute-start(bf16[144,864]{1,0:T(8,128)(2,1)S(1)} %copy-done.45), channel_id=1, source_target_pairs={{0,8},{4,12},{8,0},{12,4},{16,24},{20,28},{24,16},{28,20},{1,9},{5... | collective-permute-start | bytes 746504 | tf_op jit(solution)/shard_map/ppermute | solution.py:32
  508.0 36.4 %collective-permute-start.22 = (bf16[144,864]{1,0:T(8,128)(2,1)S(1)}, bf16[144,864]{1,0:T(8,128)(2,1)S(1)}, u32[]{:S(2)}, u32[]{:S(2)}) collective-permute-start(bf16[144,864]{1,0:T(8,128)(2,1)S(1)} %copy-done.44), channel_id=1, source_target_pairs={{0,24},{4,28},{8,16},{12,20},{16,8},{20,12},{24,0},{28,4},{1,25},{... | collective-permute-start | bytes 746504 | tf_op jit(solution)/shard_map/ppermute | solution.py:32
  510.0 35.4 %collective-permute-start.21 = (bf16[144,864]{1,0:T(8,128)(2,1)S(1)}, bf16[144,864]{1,0:T(8,128)(2,1)S(1)}, u32[]{:S(2)}, u32[]{:S(2)}) collective-permute-start(bf16[144,864]{1,0:T(8,128)(2,1)S(1)} %copy-done.43), channel_id=1, source_target_pairs={{0,16},{4,20},{8,24},{12,28},{16,0},{20,4},{24,8},{28,12},{1,17},{... | collective-permute-start | bytes 746504 | tf_op jit(solution)/shard_map/ppermute | solution.py:32
  543.2 27.8 %collective-permute-start.24 = (bf16[2,288,288]{2,1,0:T(8,128)(2,1)}, bf16[2,288,288]{2,1,0:T(8,128)(2,1)}, u32[]{:S(2)}, u32[]{:S(2)}) collective-permute-start(bf16[2,288,288]{2,1,0:T(8,128)(2,1)} %bitcast.269), channel_id=1, source_target_pairs={{0,2},{1,3},{2,0},{3,1},{4,6},{5,7},{6,4},{7,5},{8,10},{9,11},{10,... | collective-permute-start | bytes 995336 | tf_op jit(solution)/shard_map/ppermute | solution.py:32
  544.4 28.9 %collective-permute-start.26 = (bf16[2,288,288]{2,1,0:T(8,128)(2,1)}, bf16[2,288,288]{2,1,0:T(8,128)(2,1)S(1)}, u32[]{:S(2)}, u32[]{:S(2)}) collective-permute-start(bf16[2,288,288]{2,1,0:T(8,128)(2,1)} %bitcast.270), channel_id=1, source_target_pairs={{0,1},{1,0},{2,3},{3,2},{4,5},{5,4},{6,7},{7,6},{8,9},{9,8},{10,11... | collective-permute-start | bytes 995336 | tf_op jit(solution)/shard_map/ppermute | solution.py:32
  572.1 6.0 collective-permute-start.25
  573.4 6.0 collective-permute-start.27
  579.6 5.4 collective-permute-start.28
  579.7 6.8 collective-permute-start.30
  581.7 8.6 %collective-permute-start.29 = (bf16[144,288]{1,0:T(8,128)(2,1)S(1)}, bf16[144,288]{1,0:T(8,128)(2,1)S(1)}, u32[]{:S(2)}, u32[]{:S(2)}) collective-permute-start(bf16[144,288]{1,0:T(8,128)(2,1)S(1)} %get-tuple-element.75), channel_id=1, source_target_pairs={{0,16},{4,20},{8,24},{12,28},{16,0},{20,4},{24,8},{28,12},{1,17},{... | collective-permute-start | bytes 248840 | tf_op jit(solution)/shard_map/ppermute | solution.py:32
  637.9 53.7 %collective-permute-start.40 = (bf16[2,1152,288]{1,2,0:T(8,128)(2,1)S(1)}, bf16[2,1152,288]{1,2,0:T(8,128)(2,1)}, u32[]{:S(2)}, u32[]{:S(2)}) collective-permute-start(bf16[2,1152,288]{1,2,0:T(8,128)(2,1)S(1)} %fusion.42), channel_id=1, source_target_pairs={{0,2},{1,3},{2,0},{3,1},{4,6},{5,7},{6,4},{7,5},{8,10},{9,11},{10,... | collective-permute-start | bytes 3981320 | tf_op jit(solution)/shard_map/ppermute | solution.py:32
  640.2 82.0 %collective-permute-start.42 = (bf16[2,1152,288]{1,2,0:T(8,128)(2,1)S(1)}, bf16[2,1152,288]{1,2,0:T(8,128)(2,1)}, u32[]{:S(2)}, u32[]{:S(2)}) collective-permute-start(bf16[2,1152,288]{1,2,0:T(8,128)(2,1)S(1)} %fusion.43), channel_id=1, source_target_pairs={{0,1},{1,0},{2,3},{3,2},{4,5},{5,4},{6,7},{7,6},{8,9},{9,8},{10,11... | collective-permute-start | bytes 3981320 | tf_op jit(solution)/shard_map/ppermute | solution.py:32
  687.1 29.3 %collective-permute-start.32 = (bf16[2,288,1152]{2,1,0:T(8,128)(2,1)S(1)}, bf16[2,288,1152]{2,1,0:T(8,128)(2,1)S(1)}, u32[]{:S(2)}, u32[]{:S(2)}) collective-permute-start(bf16[2,288,1152]{2,1,0:T(8,128)(2,1)S(1)} %bitcast.324), channel_id=1, source_target_pairs={{0,2},{1,3},{2,0},{3,1},{4,6},{5,7},{6,4},{7,5},{8,10},{9,11},{10,... | collective-permute-start | bytes 3981320 | tf_op jit(solution)/shard_map/ppermute | solution.py:32
  688.5 32.1 %collective-permute-start.34 = (bf16[2,288,1152]{2,1,0:T(8,128)(2,1)S(1)}, bf16[2,288,1152]{2,1,0:T(8,128)(2,1)S(1)}, u32[]{:S(2)}, u32[]{:S(2)}) collective-permute-start(bf16[2,288,1152]{2,1,0:T(8,128)(2,1)S(1)} %fusion.41), channel_id=1, source_target_pairs={{0,1},{1,0},{2,3},{3,2},{4,5},{5,4},{6,7},{7,6},{8,9},{9,8},{10,11... | collective-permute-start | bytes 3981320 | tf_op jit(solution)/shard_map/ppermute | solution.py:32
  693.5 57.6 %collective-permute-start.41 = (bf16[1152,288]{0,1:T(8,128)(2,1)S(1)}, bf16[1152,288]{0,1:T(8,128)(2,1)S(1)}, u32[]{:S(2)}, u32[]{:S(2)}) collective-permute-start(bf16[1152,288]{0,1:T(8,128)(2,1)S(1)} %fusion.54), channel_id=1, source_target_pairs={{0,1},{1,0},{2,3},{3,2},{4,5},{5,4},{6,7},{7,6},{8,9},{9,8},{10,11... | collective-permute-start | bytes 1990664 | tf_op jit(solution)/shard_map/ppermute | solution.py:32
  716.7 29.2 %collective-permute-start.33 = (bf16[288,1152]{1,0:T(8,128)(2,1)S(1)}, bf16[288,1152]{1,0:T(8,128)(2,1)S(1)}, u32[]{:S(2)}, u32[]{:S(2)}) collective-permute-start(bf16[288,1152]{1,0:T(8,128)(2,1)S(1)} %fusion.52), channel_id=1, source_target_pairs={{0,1},{1,0},{2,3},{3,2},{4,5},{5,4},{6,7},{7,6},{8,9},{9,8},{10,11... | collective-permute-start | bytes 1990664 | tf_op jit(solution)/shard_map/ppermute | solution.py:32
  720.9 25.1 %collective-permute-start.35 = (bf16[288,1152]{1,0:T(8,128)(2,1)S(1)}, bf16[288,1152]{1,0:T(8,128)(2,1)S(1)}, u32[]{:S(2)}, u32[]{:S(2)}) collective-permute-start(bf16[288,1152]{1,0:T(8,128)(2,1)S(1)} %fusion.53), channel_id=1, source_target_pairs={{0,2},{1,3},{2,0},{3,1},{4,6},{5,7},{6,4},{7,5},{8,10},{9,11},{10,... | collective-permute-start | bytes 1990664 | tf_op jit(solution)/shard_map/ppermute | solution.py:32
  724.0 27.2 %collective-permute-start.43 = (bf16[1152,288]{0,1:T(8,128)(2,1)S(1)}, bf16[1152,288]{0,1:T(8,128)(2,1)S(1)}, u32[]{:S(2)}, u32[]{:S(2)}) collective-permute-start(bf16[1152,288]{0,1:T(8,128)(2,1)S(1)} %fusion.55), channel_id=1, source_target_pairs={{0,2},{1,3},{2,0},{3,1},{4,6},{5,7},{6,4},{7,5},{8,10},{9,11},{10,... | collective-permute-start | bytes 1990664 | tf_op jit(solution)/shard_map/ppermute | solution.py:32
  747.6 17.3 %collective-permute-start.36 = (bf16[144,1152]{1,0:T(8,128)(2,1)}, bf16[144,1152]{1,0:T(8,128)(2,1)S(1)}, u32[]{:S(2)}, u32[]{:S(2)}) collective-permute-start(bf16[144,1152]{1,0:T(8,128)(2,1)} %get-tuple-element.57), channel_id=1, source_target_pairs={{0,8},{4,12},{8,0},{12,4},{16,24},{20,28},{24,16},{28,20},{1,9},{5... | collective-permute-start | bytes 995336 | tf_op jit(solution)/shard_map/ppermute | solution.py:32
  747.6 17.8 %collective-permute-start.38 = (bf16[144,1152]{1,0:T(8,128)(2,1)}, bf16[144,1152]{1,0:T(8,128)(2,1)}, u32[]{:S(2)}, u32[]{:S(2)}) collective-permute-start(bf16[144,1152]{1,0:T(8,128)(2,1)} %get-tuple-element.58), channel_id=1, source_target_pairs={{0,24},{4,28},{8,16},{12,20},{16,8},{20,12},{24,0},{28,4},{1,25},{... | collective-permute-start | bytes 995336 | tf_op jit(solution)/shard_map/ppermute | solution.py:32
  749.3 46.9 %collective-permute-start.37 = (bf16[144,1152]{1,0:T(8,128)(2,1)}, bf16[144,1152]{1,0:T(8,128)(2,1)}, u32[]{:S(2)}, u32[]{:S(2)}) collective-permute-start(bf16[144,1152]{1,0:T(8,128)(2,1)} %get-tuple-element.59), channel_id=1, source_target_pairs={{0,16},{4,20},{8,24},{12,28},{16,0},{20,4},{24,8},{28,12},{1,17},{... | collective-permute-start | bytes 995336 | tf_op jit(solution)/shard_map/ppermute | solution.py:32
  758.9 45.0 %collective-permute-start.45 = (bf16[576,288]{0,1:T(8,128)(2,1)S(1)}, bf16[576,288]{0,1:T(8,128)(2,1)S(1)}, u32[]{:S(2)}, u32[]{:S(2)}) collective-permute-start(bf16[576,288]{0,1:T(8,128)(2,1)S(1)} %bitcast.327), channel_id=1, source_target_pairs={{0,16},{4,20},{8,24},{12,28},{16,0},{20,4},{24,8},{28,12},{1,17},{... | collective-permute-start | bytes 995336 | tf_op jit(solution)/shard_map/ppermute | solution.py:32
  760.1 43.9 %collective-permute-start.46 = (bf16[576,288]{0,1:T(8,128)(2,1)S(1)}, bf16[576,288]{0,1:T(8,128)(2,1)S(1)}, u32[]{:S(2)}, u32[]{:S(2)}) collective-permute-start(bf16[576,288]{0,1:T(8,128)(2,1)S(1)} %bitcast.326), channel_id=1, source_target_pairs={{0,24},{4,28},{8,16},{12,20},{16,8},{20,12},{24,0},{28,4},{1,25},{... | collective-permute-start | bytes 995336 | tf_op jit(solution)/shard_map/ppermute | solution.py:32
  762.2 42.7 %copy-start.1 = (bf16[1152,1152]{1,0:T(8,128)(2,1)S(1)}, bf16[1152,1152]{1,0:T(8,128)(2,1)}, u32[]{:S(2)}) copy-start(bf16[1152,1152]{1,0:T(8,128)(2,1)} %param.25) | copy-start | bytes 7962628
  764.9 39.1 %collective-permute-start.44 = (bf16[576,288]{0,1:T(8,128)(2,1)S(1)}, bf16[576,288]{0,1:T(8,128)(2,1)S(1)}, u32[]{:S(2)}, u32[]{:S(2)}) collective-permute-start(bf16[576,288]{0,1:T(8,128)(2,1)S(1)} %bitcast.325), channel_id=1, source_target_pairs={{0,8},{4,12},{8,0},{12,4},{16,24},{20,28},{24,16},{28,20},{1,9},{5... | collective-permute-start | bytes 995336 | tf_op jit(solution)/shard_map/ppermute | solution.py:32
  (61 other events, 301.7 us)

commit v2 on v1

v2 whole, which is shorter than its diff:
```python
from functools import partial
import math

import jax
import jax.numpy as jnp
from jax import lax
from jax.experimental import pallas as pl
from jax.experimental.pallas import tpu as pltpu
from jax.sharding import PartitionSpec as P

HEADS = 16
LOG2E = math.log2(math.e)
VMEM_LIMIT = 48 << 20
BF16 = jnp.bfloat16
F32 = jnp.float32

norm_eps = 1e-06


def modulate(values, offset, factor):
    center = values - jnp.mean(values, axis=-1, keepdims=True)
    spread = jnp.mean(center * center, axis=-1, keepdims=True)
    return center * lax.rsqrt(spread + norm_eps) * (1.0 + factor) + offset


def gelu_tanh(values):
    return jax.nn.gelu(values, approximate=True)


def swap(values, axis, mask):
    count = lax.axis_size(axis)
    return lax.ppermute(values, axis, [(i, i ^ mask) for i in range(count)])


def flip_blocks(values, axis, mask):
    return jnp.take(values, lax.iota(jnp.int32, values.shape[axis]) ^ mask, axis=axis)


def qkv_kernel(slot_row, seg, mod, tokens, weight, bias, normed_ref, qkv_ref):
    width = tokens.shape[-1]
    values = tokens[0].astype(F32)
    picked = (seg[0] == slot_row[...]).astype(BF16)
    table = mod[0]
    high = table.astype(BF16)
    rest = table - high.astype(F32)
    middle = rest.astype(BF16)
    last = (rest - middle.astype(F32)).astype(BF16)
    stacked = jnp.concatenate([high, middle, last], axis=0)
    per_token = jnp.dot(picked, stacked, preferred_element_type=F32)
    normed = modulate(values, per_token[:, :width], per_token[:, width:]).astype(BF16)
    normed_ref[0] = normed
    mixed = lax.dot_general(weight[...], normed, (((1,), (1,)), ((), ())), preferred_element_type=F32)
    mixed = (mixed + bias[...]).astype(BF16)
    _, parts, heads, size, _ = qkv_ref.shape
    for part in range(parts):
        for head in range(heads):
            start = (part * heads + head) * size
            qkv_ref[0, part, head] = mixed[start : start + size]


def project_qkv(tokens, seg, slot_mod, weight, bias, heads, block):
    rows, length, width = tokens.shape
    slots = slot_mod.shape[1]
    features = weight.shape[0]
    size = features // (3 * heads)
    slot_row = jnp.tile(lax.iota(jnp.int32, slots), 3)[None]
    return pl.pallas_call(
        qkv_kernel,
        grid=(rows, length // block),
        in_specs=[
            pl.BlockSpec((1, 3 * slots), lambda r, t: (0, 0)),
            pl.BlockSpec((1, block, 1), lambda r, t: (r, t, 0)),
            pl.BlockSpec((1, slots, 2 * width), lambda r, t: (r, 0, 0)),
            pl.BlockSpec((1, block, width), lambda r, t: (r, t, 0)),
            pl.BlockSpec((features, width), lambda r, t: (0, 0)),
            pl.BlockSpec((features, 1), lambda r, t: (0, 0)),
        ],
        out_specs=[
            pl.BlockSpec((1, block, width), lambda r, t: (r, t, 0)),
            pl.BlockSpec((1, 3, heads, size, block), lambda r, t: (r, 0, 0, 0, t)),
        ],
        out_shape=[
            jax.ShapeDtypeStruct((rows, length, width), BF16),
            jax.ShapeDtypeStruct((rows, 3, heads, size, length), BF16),
        ],
        compiler_params=pltpu.CompilerParams(vmem_limit_bytes=VMEM_LIMIT),
        cost_estimate=pl.CostEstimate(
            flops=2 * rows * length * width * features,
            bytes_accessed=2 * rows * length * (2 * width + features),
            transcendentals=0,
        ),
    )(slot_row, seg[:, :, None], slot_mod, tokens, weight, bias[:, None])


def peers_of(seq):
    x, y = lax.rem(seq, 2), lax.div(seq, 2)
    return [seq + 1 - 2 * x, seq + 2 - 4 * y, 3 - seq]


def greet(devices):
    barrier = pltpu.get_barrier_semaphore()
    for device in devices:
        pl.semaphore_signal(barrier, inc=1, device_id={"seq": device}, device_id_type=pl.DeviceIdType.MESH)
    pl.semaphore_wait(barrier, len(devices))


def send_block(source, target, sent, came, index, device):
    return pltpu.make_async_remote_copy(
        src_ref=source,
        dst_ref=target,
        send_sem=sent.at[index],
        recv_sem=came.at[index],
        device_id={"seq": device},
        device_id_type=pl.DeviceIdType.MESH,
    )


def attend_kernel(block, scale, code_col, code_row, query, key, value, out_ref, lse_ref, token_ref=None, sent=None, came=None, kept=None):
    length = query.shape[-1]
    keys = key[0, 0].astype(F32).T.astype(BF16)
    values = value[0, 0]
    codes = code_col[0]
    row, head = (pl.program_id(0), pl.program_id(1)) if sent is not None else (0, 0)
    rows, heads = out_ref.shape[:2]
    if sent is not None:
        seq = lax.axis_index("seq")
        peers = peers_of(seq)
        size = length // 4

        @pl.when((row == 0) & (head == 0))
        def _():
            greet(peers)

        def to_peer(r, h, m):
            lanes = pl.ds(m * size, size)
            place = (r * heads + h) * 3 + m - 1
            return send_block(out_ref.at[r, h, :, lanes], token_ref.at[r, seq, h], sent, came, place, peers[m - 1])

        def to_self(r, h):
            return pltpu.make_async_copy(out_ref.at[r, h, :, pl.ds(0, size)], token_ref.at[r, seq, h], kept.at[r * heads + h])

    for step in range(length // block):
        here = pl.ds(step * block, block)
        scores = jnp.dot(keys, query[0, 0, :, here], preferred_element_type=F32)
        scores = jnp.where(codes == code_row[0, :, here], scores * scale, -1e30)
        peak = jnp.max(scores, axis=0, keepdims=True)
        raised = jnp.exp2(scores - peak)
        total = jnp.sum(raised, axis=0, keepdims=True)
        probs = (raised * (1.0 / total)).astype(BF16)
        out_ref[row, head, :, here] = jnp.dot(values, probs, preferred_element_type=F32).astype(BF16)
        lse_ref[0, 0, :, here] = peak + jnp.log2(total)

    if sent is not None:
        to_self(row, head).start()
        for m in range(1, 4):
            to_peer(row, head, m).start()

        @pl.when((row == rows - 1) & (head == heads - 1))
        def _():
            for r in range(rows):
                for h in range(heads):
                    to_self(r, h).wait()
                    for m in range(1, 4):
                        to_peer(r, h, m).wait()


def attend(packed, col, row, block, exchange):
    rows, _, heads, size, length = packed.shape
    part = lambda j: pl.BlockSpec((1, None, 1, size, length), lambda r, h: (r, j, h, 0, 0))
    out_specs = [
        pl.BlockSpec((1, 1, size, length), lambda r, h: (r, h, 0, 0)),
        pl.BlockSpec((1, 1, 1, length), lambda r, h: (r, h, 0, 0)),
    ]
    out_shape = [
        jax.ShapeDtypeStruct((rows, heads, size, length), BF16),
        jax.ShapeDtypeStruct((rows, heads, 1, length), F32),
    ]
    scratch = []
    extra = {}
    if exchange:
        out_specs[0] = pl.BlockSpec((rows, heads, size, length), lambda r, h: (0, 0, 0, 0))
        out_specs.append(pl.BlockSpec(memory_space=pl.ANY))
        out_shape.append(jax.ShapeDtypeStruct((rows, 4, heads, size, length // 4), BF16))
        count = rows * heads
        scratch = [pltpu.SemaphoreType.DMA((3 * count,)), pltpu.SemaphoreType.DMA((3 * count,)), pltpu.SemaphoreType.DMA((count,))]
        extra = dict(collective_id=2, has_side_effects=True)
    return pl.pallas_call(
        partial(attend_kernel, block, size**-0.5 * LOG2E),
        grid=(rows, heads),
        in_specs=[
            pl.BlockSpec((1, length, 1), lambda r, h: (r, 0, 0)),
            pl.BlockSpec((1, 1, length), lambda r, h: (r, 0, 0)),
            part(0),
            part(1),
            part(2),
        ],
        out_specs=out_specs,
        out_shape=out_shape,
        scratch_shapes=scratch,
        compiler_params=pltpu.CompilerParams(vmem_limit_bytes=VMEM_LIMIT, **extra),
        cost_estimate=pl.CostEstimate(
            flops=8 * rows * heads * length * length * 128,
            bytes_accessed=8 * rows * heads * length * size,
            transcendentals=rows * heads * length * length,
        ),
    )(col, row, packed, packed, packed)


def attend_back_kernel(
    block,
    inner,
    scale,
    exchange,
    code_col,
    code_row,
    query,
    key,
    value,
    out,
    grad_out,
    lse,
    grad_ref,
    *rest,
):
    length = query.shape[-1]
    size = query.shape[-2]
    row, head = (pl.program_id(0), pl.program_id(1)) if exchange else (0, 0)
    rows, _, heads = grad_ref.shape[:3]
    if exchange:
        token_ref, key_sum, value_sum, keys, values, sent, came, kept = rest
        seq = lax.axis_index("seq")
        peers = peers_of(seq)
        local = length // 4

        @pl.when((row == 0) & (head == 0))
        def _():
            greet(peers)

        def to_peer(r, h, m):
            lanes = pl.ds(m * local, local)
            place = (r * heads + h) * 3 + m - 1
            return send_block(grad_ref.at[r, :, h, :, lanes], token_ref.at[r, :, seq, h], sent, came, place, peers[m - 1])

        def to_self(r, h):
            lanes = pl.ds(0, local)
            return pltpu.make_async_copy(grad_ref.at[r, :, h, :, lanes], token_ref.at[r, :, seq, h], kept.at[r * heads + h])

    else:
        key_sum, value_sum, keys, values = rest
    keys[...] = key[0, 0].astype(F32).T.astype(BF16)
    values[...] = value[0, 0].astype(F32).T.astype(BF16)
    for step in range(length // block):
        here = pl.ds(step * block, block)
        query_low = query[0, 0, :, here]
        grad_low = grad_out[0, 0, :, here]
        query_rows = query_low.astype(F32).T.astype(BF16)
        grad_rows = grad_low.astype(F32).T.astype(BF16)
        row_dot = jnp.sum(grad_low.astype(F32) * out[0, 0, :, here].astype(F32), axis=0, keepdims=True)
        grad_query = jnp.zeros((size, block), F32)
        for part in range(length // inner):
            there = pl.ds(part * inner, inner)
            scores = jnp.dot(keys[there, :], query_low, preferred_element_type=F32)
            scores = jnp.where(code_col[0, there, :] == code_row[0, :, here], scores * (scale * LOG2E), -1e30)
            probs = jnp.exp2(scores - lse[0, 0, :, here])
            grad_probs = jnp.dot(values[there, :], grad_low, preferred_element_type=F32)
            grad_raw = (probs * (grad_probs - row_dot) * scale).astype(BF16)
            value_part = jnp.dot(probs.astype(BF16), grad_rows, preferred_element_type=F32)
            key_part = jnp.dot(grad_raw, query_rows, preferred_element_type=F32)
            if step == 0:
                value_sum[there, :] = value_part
                key_sum[there, :] = key_part
            else:
                value_sum[there, :] += value_part
                key_sum[there, :] += key_part
            grad_query += jnp.dot(key[0, 0, :, there], grad_raw, preferred_element_type=F32)
        grad_ref[row, 0, head, :, here] = grad_query.astype(BF16)
    grad_ref[row, 1, head] = key_sum[...].T.astype(BF16)
    grad_ref[row, 2, head] = value_sum[...].T.astype(BF16)

    if exchange:
        to_self(row, head).start()
        for m in range(1, 4):
            to_peer(row, head, m).start()

        @pl.when((row == rows - 1) & (head == heads - 1))
        def _():
            for r in range(rows):
                for h in range(heads):
                    to_self(r, h).wait()
                    for m in range(1, 4):
                        to_peer(r, h, m).wait()


def attend_back(packed, out, grad_out, lse, col, row, block, inner, exchange):
    rows, _, heads, size, length = packed.shape
    part = lambda j: pl.BlockSpec((1, None, 1, size, length), lambda r, h: (r, j, h, 0, 0))
    whole = pl.BlockSpec((1, 1, size, length), lambda r, h: (r, h, 0, 0))
    out_specs = [pl.BlockSpec((1, 3, 1, size, length), lambda r, h: (r, 0, h, 0, 0))]
    out_shape = [jax.ShapeDtypeStruct((rows, 3, heads, size, length), BF16)]
    scratch = []
    extra = {}
    if exchange:
        out_specs = [
            pl.BlockSpec((rows, 3, heads, size, length), lambda r, h: (0, 0, 0, 0, 0)),
            pl.BlockSpec(memory_space=pl.ANY),
        ]
        out_shape.append(jax.ShapeDtypeStruct((rows, 3, 4, heads, size, length // 4), BF16))
        count = rows * heads
        scratch = [pltpu.SemaphoreType.DMA((3 * count,)), pltpu.SemaphoreType.DMA((3 * count,)), pltpu.SemaphoreType.DMA((count,))]
        extra = dict(collective_id=3, has_side_effects=True)
    return pl.pallas_call(
        partial(attend_back_kernel, block, inner, size**-0.5, exchange),
        grid=(rows, heads),
        in_specs=[
            pl.BlockSpec((1, length, 1), lambda r, h: (r, 0, 0)),
            pl.BlockSpec((1, 1, length), lambda r, h: (r, 0, 0)),
            part(0),
            part(1),
            part(2),
            whole,
            whole,
            pl.BlockSpec((1, 1, 1, length), lambda r, h: (r, h, 0, 0)),
        ],
        out_specs=out_specs,
        out_shape=out_shape,
        scratch_shapes=[
            pltpu.VMEM((length, size), F32),
            pltpu.VMEM((length, size), F32),
            pltpu.VMEM((length, size), BF16),
            pltpu.VMEM((length, size), BF16),
        ]
        + scratch,
        compiler_params=pltpu.CompilerParams(vmem_limit_bytes=VMEM_LIMIT, **extra),
        cost_estimate=pl.CostEstimate(
            flops=20 * rows * heads * length * length * 128,
            bytes_accessed=16 * rows * heads * length * size,
            transcendentals=rows * heads * length * length,
        ),
    )(col, row, packed, packed, packed, out, grad_out, lse)


def mlp_kernel(
    normed, grad_out, normed_turned, grad_turned, up, down, bias, out_sum, grad_sum, up_keep, up_send, down_keep, down_send, bias_sum
):
    step = pl.program_id(0)
    half = up_keep.shape[0]
    c0 = math.sqrt(2 / math.pi)
    c1 = c0 * 0.044715
    hidden = jnp.dot(normed[...], up[...], preferred_element_type=F32) + bias[...]
    square = hidden * hidden
    gate = 0.5 + 0.5 * jnp.tanh(hidden * (c0 + c1 * square))
    raised = hidden * gate
    slope = gate + raised * (1.0 - gate) * (2 * c0 + 6 * c1 * square)
    active = raised.astype(BF16)
    back = (((1,), (1,)), ((), ()))
    grad_active = lax.dot_general(grad_out[...], down[...], back, preferred_element_type=F32)
    grad_wide = (grad_active * slope).astype(BF16)
    out_part = jnp.dot(active, down[...], preferred_element_type=F32)
    grad_part = lax.dot_general(grad_wide, up[...], back, preferred_element_type=F32)

    @pl.when(step == 0)
    def _():
        out_sum[...] = out_part
        grad_sum[...] = grad_part

    @pl.when(step > 0)
    def _():
        out_sum[...] += out_part
        grad_sum[...] += grad_part

    bias_sum[...] = jnp.sum(grad_wide.astype(F32), axis=0, keepdims=True)
    up_keep[...] = jnp.dot(normed_turned[:half], grad_wide, preferred_element_type=F32)
    up_send[...] = jnp.dot(normed_turned[half:], grad_wide, preferred_element_type=F32).astype(BF16)
    down_keep[...] = jnp.dot(grad_turned[:half], active, preferred_element_type=F32)
    down_send[...] = jnp.dot(grad_turned[half:], active, preferred_element_type=F32).astype(BF16)


def feed_forward(normed, grad_out, normed_turned, grad_turned, up, down, bias, tile):
    count, width = normed.shape
    hidden = up.shape[1]
    half = width // 2
    fixed = lambda *shape: pl.BlockSpec(shape, lambda t: (0, 0))
    across = lambda rows: pl.BlockSpec((rows, tile), lambda t: (0, t))
    shape = jax.ShapeDtypeStruct
    return pl.pallas_call(
        mlp_kernel,
        grid=(hidden // tile,),
        in_specs=[
            fixed(count, width),
            fixed(count, width),
            fixed(width, count),
            fixed(width, count),
            across(width),
            pl.BlockSpec((tile, width), lambda t: (t, 0)),
            across(1),
        ],
        out_specs=[fixed(count, width), fixed(count, width), across(half), across(half), across(half), across(half), across(1)],
        out_shape=[
            shape((count, width), F32),
            shape((count, width), F32),
            shape((half, hidden), F32),
            shape((half, hidden), BF16),
            shape((half, hidden), F32),
            shape((half, hidden), BF16),
            shape((1, hidden), F32),
        ],
        compiler_params=pltpu.CompilerParams(vmem_limit_bytes=56 << 20),
        cost_estimate=pl.CostEstimate(
            flops=12 * count * width * hidden,
            bytes_accessed=10 * width * hidden,
            transcendentals=count * hidden,
        ),
    )(normed, grad_out, normed_turned, grad_turned, up, down, bias)


def turn_halves(values, groups, mine):
    count, width = values.shape
    view = values.T.reshape(groups, 2, width // (2 * groups), count)
    keep = lax.dynamic_index_in_dim(view, mine, 1, keepdims=False).reshape(width // 2, count)
    send = lax.dynamic_index_in_dim(view, 1 - mine, 1, keepdims=False).reshape(width // 2, count)
    return jnp.concatenate([keep, send], axis=0)


STAGES = 4


def mlp_reduce_kernel(
    tiles,
    normed,
    grad_out,
    normed_turned,
    grad_turned,
    up0,
    up1,
    up2,
    up3,
    down0,
    down1,
    down2,
    down3,
    bias,
    out_sum,
    grad_sum,
    bias_sum,
    up_total,
    down_total,
    up_mine,
    down_mine,
    up_core,
    down_core,
    up_core_got,
    down_core_got,
    up_half,
    down_half,
    up_out,
    down_out,
    up_got,
    down_got,
    up_quarter,
    down_quarter,
    up_last,
    down_last,
    up_last_got,
    down_last_got,
    chip_full,
    chip_out,
    chip_got,
    core_sent,
    core_came,
    seq_sent,
    seq_came,
    last_sent,
    last_came,
    chip_sent,
    chip_came,
):
    step = pl.program_id(0)
    seq, row = lax.axis_index("seq"), lax.axis_index("rows")
    half = normed_turned.shape[0] // 2
    x, y = lax.rem(seq, 2), lax.div(seq, 2)
    core_peer = {"rows": row + 1 - 2 * lax.rem(row, 2)}
    x_peer = {"seq": seq + 1 - 2 * x}
    y_peer = {"seq": seq + 2 - 4 * y}
    chip, core = lax.div(row, 2), lax.rem(row, 2)
    to_chip = [lax.rem(chip + k, 4) for k in range(4)]
    chip_peers = [{"rows": 2 * to_chip[k] + core} for k in range(4)]

    @pl.when(step == 0)
    def _():
        barrier = pltpu.get_barrier_semaphore()
        for peer in (core_peer, x_peer, y_peer, *chip_peers[1:]):
            pl.semaphore_signal(barrier, inc=1, device_id=peer, device_id_type=pl.DeviceIdType.MESH)
        pl.semaphore_wait(barrier, 6)

    def copies(source, target, sent, came, slot, kind, device):
        return pltpu.make_async_remote_copy(
            src_ref=source.at[slot],
            dst_ref=target.at[slot],
            send_sem=sent.at[kind, slot],
            recv_sem=came.at[kind, slot],
            device_id=device,
            device_id_type=pl.DeviceIdType.MESH,
        )

    def to_core(slot):
        return (
            copies(up_core, up_core_got, core_sent, core_came, slot, 0, core_peer),
            copies(down_core, down_core_got, core_sent, core_came, slot, 1, core_peer),
        )

    def to_seq(slot):
        return (
            copies(up_out, up_got, seq_sent, seq_came, slot, 0, x_peer),
            copies(down_out, down_got, seq_sent, seq_came, slot, 1, y_peer),
        )

    def to_last(slot):
        return (
            copies(up_last, up_last_got, last_sent, last_came, slot, 0, y_peer),
            copies(down_last, down_last_got, last_sent, last_came, slot, 1, x_peer),
        )

    def to_chips(slot):
        return [
            pltpu.make_async_remote_copy(
                src_ref=chip_out.at[slot, to_chip[k]],
                dst_ref=chip_got.at[slot, k - 1],
                send_sem=chip_sent.at[k - 1, slot],
                recv_sem=chip_came.at[k - 1, slot],
                device_id=chip_peers[k],
                device_id_type=pl.DeviceIdType.MESH,
            )
            for k in range(1, 4)
        ]

    @pl.when(step >= 4)
    def _():
        slot = lax.rem(step, 2)
        for copy in to_chips(slot):
            copy.wait()
        for kind, total in enumerate((up_total, down_total)):
            value = chip_full[slot, chip, kind]
            for k in range(3):
                value = value + chip_got[slot, k, kind].astype(F32)
            total[...] = value

    @pl.when((step >= 3) & (step < tiles + 3))
    def _():
        slot = lax.rem(step + 1, 2)
        for copy in to_last(slot):
            copy.wait()
        size = half // 4
        ups = up_quarter[slot] + up_last_got[slot].astype(F32)
        downs = down_quarter[slot] + down_last_got[slot].astype(F32)
        for place in range(4):
            up_block = ups[place * size : (place + 1) * size]
            down_block = downs[:, place * 128 : (place + 1) * 128]
            chip_full[slot, place, 0] = up_block
            chip_full[slot, place, 1] = down_block
            chip_out[slot, place, 0] = up_block.astype(BF16)
            chip_out[slot, place, 1] = down_block.astype(BF16)
        for copy in to_chips(slot):
            copy.start()

    @pl.when((step >= 2) & (step < tiles + 2))
    def _():
        slot = lax.rem(step, 2)
        for copy in to_seq(slot):
            copy.wait()
        up_quarter[slot] = up_half[slot, y] + up_got[slot, y].astype(F32)
        up_last[slot] = (up_half[slot, 1 - y] + up_got[slot, 1 - y].astype(F32)).astype(BF16)
        down_quarter[slot] = down_half[slot, x] + down_got[slot, x].astype(F32)
        down_last[slot] = (down_half[slot, 1 - x] + down_got[slot, 1 - x].astype(F32)).astype(BF16)
        for copy in to_last(slot):
            copy.start()

    @pl.when((step >= 1) & (step <= tiles))
    def _():
        slot = lax.rem(step + 1, 2)
        for copy in to_core(slot):
            copy.wait()
        for other in range(2):
            kept, gone = 2 * other + x, 2 * other + 1 - x
            up_half[slot, other] = up_mine[slot, kept] + up_core_got[slot, kept].astype(F32)
            up_out[slot, other] = (up_mine[slot, gone] + up_core_got[slot, gone].astype(F32)).astype(BF16)
            kept, gone = 2 * y + other, 2 * (1 - y) + other
            down_half[slot, other] = down_mine[slot, kept] + down_core_got[slot, kept].astype(F32)
            down_out[slot, other] = (down_mine[slot, gone] + down_core_got[slot, gone].astype(F32)).astype(BF16)
        for copy in to_seq(slot):
            copy.start()

    @pl.when(step < tiles)
    def _():
        slot = lax.rem(step, 2)
        up = jnp.concatenate([up0[...], up1[...], up2[...], up3[...]], axis=1)
        down = jnp.concatenate([down0[...], down1[...], down2[...], down3[...]], axis=0)
        biases = jnp.concatenate([bias[owner] for owner in range(4)], axis=1)
        c0 = math.sqrt(2 / math.pi)
        c1 = c0 * 0.044715
        hidden = jnp.dot(normed[...], up, preferred_element_type=F32) + biases
        square = hidden * hidden
        gate = 0.5 + 0.5 * jnp.tanh(hidden * (c0 + c1 * square))
        raised = hidden * gate
        slope = gate + raised * (1.0 - gate) * (2 * c0 + 6 * c1 * square)
        active = raised.astype(BF16)
        down_part = jnp.dot(grad_turned[...], active, preferred_element_type=F32)
        for owner in range(4):
            size = half // 4
            down_mine[slot, owner] = down_part[owner * size : (owner + 1) * size]
            down_core[slot, owner] = down_part[half + owner * size : half + (owner + 1) * size].astype(BF16)
        to_core(slot)[1].start()
        back = (((1,), (1,)), ((), ()))
        grad_active = lax.dot_general(grad_out[...], down, back, preferred_element_type=F32)
        grad_wide = (grad_active * slope).astype(BF16)
        up_part = jnp.dot(normed_turned[...], grad_wide, preferred_element_type=F32)
        for owner in range(4):
            columns = slice(owner * 128, (owner + 1) * 128)
            up_mine[slot, owner] = up_part[:half, columns]
            up_core[slot, owner] = up_part[half:, columns].astype(BF16)
        to_core(slot)[0].start()
        sums = jnp.sum(grad_wide.astype(F32), axis=0, keepdims=True)
        for owner in range(4):
            bias_sum[owner] = sums[:, owner * 128 : (owner + 1) * 128]
        out_part = jnp.dot(active, down, preferred_element_type=F32)
        grad_part = lax.dot_general(grad_wide, up, back, preferred_element_type=F32)

        @pl.when(step == 0)
        def _():
            out_sum[...] = out_part
            grad_sum[...] = grad_part

        @pl.when(step > 0)
        def _():
            out_sum[...] += out_part
            grad_sum[...] += grad_part


def feed_forward_reduce(normed, grad_out, normed_turned, grad_turned, up, down, bias):
    count, width = normed.shape
    hidden = up.shape[1]
    part = hidden // 4
    tiles = part // 128
    half, quarter = width // 2, width // 8
    last = tiles - 1
    shape = jax.ShapeDtypeStruct
    fixed = lambda *dims: pl.BlockSpec(dims, lambda t: (0, 0), pipeline_mode=pl.Buffered(buffer_count=1))
    result = lambda *dims: pl.BlockSpec(dims, lambda t: (0, 0))
    done = lambda t: jnp.maximum(t - STAGES, 0)

    def up_block(owner):
        return pl.BlockSpec((width, 128), lambda t: (0, owner * tiles + jnp.minimum(t, last)))

    def down_block(owner):
        return pl.BlockSpec((128, width), lambda t: (owner * tiles + jnp.minimum(t, last), 0))

    bias_block = pl.BlockSpec((4, 1, 128), lambda t: (0, 0, jnp.minimum(t, last)))
    pair = lambda dtype, *dims: pltpu.VMEM((2,) + dims, dtype)
    return pl.pallas_call(
        partial(mlp_reduce_kernel, tiles),
        grid=(tiles + STAGES,),
        in_specs=[fixed(count, width), fixed(count, width), fixed(width, count), fixed(width, count)]
        + [up_block(owner) for owner in range(4)]
        + [down_block(owner) for owner in range(4)]
        + [bias_block],
        out_specs=[
            result(count, width),
            result(count, width),
            bias_block,
            pl.BlockSpec((quarter, 128), lambda t: (0, done(t))),
            pl.BlockSpec((quarter, 128), lambda t: (0, done(t))),
        ],
        out_shape=[
            shape((count, width), F32),
            shape((count, width), F32),
            shape((4, 1, part), F32),
            shape((quarter, part), F32),
            shape((quarter, part), F32),
        ],
        scratch_shapes=[
            pair(F32, 4, half, 128),
            pair(F32, 4, quarter, 512),
            pair(BF16, 4, half, 128),
            pair(BF16, 4, quarter, 512),
            pair(BF16, 4, half, 128),
            pair(BF16, 4, quarter, 512),
            pair(F32, 2, half, 128),
            pair(F32, 2, quarter, 512),
            pair(BF16, 2, half, 128),
            pair(BF16, 2, quarter, 512),
            pair(BF16, 2, half, 128),
            pair(BF16, 2, quarter, 512),
            pair(F32, half, 128),
            pair(F32, quarter, 512),
            pair(BF16, half, 128),
            pair(BF16, quarter, 512),
            pair(BF16, half, 128),
            pair(BF16, quarter, 512),
            pair(F32, 4, 2, quarter, 128),
            pair(BF16, 4, 2, quarter, 128),
            pair(BF16, 3, 2, quarter, 128),
        ]
        + [pltpu.SemaphoreType.DMA((2, 2))] * 6
        + [pltpu.SemaphoreType.DMA((3, 2))] * 2,
        compiler_params=pltpu.CompilerParams(collective_id=1, has_side_effects=True, vmem_limit_bytes=56 << 20),
        cost_estimate=pl.CostEstimate(
            flops=12 * count * width * hidden,
            bytes_accessed=6 * width * hidden,
            transcendentals=count * hidden,
        ),
    )(normed, grad_out, normed_turned, grad_turned, up, up, up, up, down, down, down, down, bias.reshape(4, 1, part))


def qkv_weight_kernel(grad, normed, keep_ref, send_ref, sum_ref, total, turned):
    step = pl.program_id(0)
    chips, depth = lax.axis_size("rows") // 2, total.shape[1] // lax.axis_size("rows")
    mine = lax.rem(lax.axis_index("rows"), 2)
    part = jnp.dot(grad[0], normed[0], preferred_element_type=F32)
    sums = jnp.sum(grad[0].astype(F32), axis=1, keepdims=True)

    @pl.when(step == 0)
    def _():
        total[...] = part
        sum_ref[...] = sums

    @pl.when(step > 0)
    def _():
        total[...] += part
        sum_ref[...] += sums

    @pl.when(step == pl.num_programs(0) - 1)
    def _():
        turned[...] = total[...].T
        for chip in range(chips):
            first = pl.multiple_of((2 * chip + mine) * depth, 8)
            other = pl.multiple_of((2 * chip + 1 - mine) * depth, 8)
            keep_ref[chip] = turned[pl.ds(first, depth), :]
            send_ref[chip] = turned[pl.ds(other, depth), :].astype(BF16)


def qkv_weight_grad(grad, normed):
    rows, features, length = grad.shape
    width = normed.shape[2]
    groups = lax.axis_size("rows")
    shape = (groups // 2, width // groups, features)
    return pl.pallas_call(
        qkv_weight_kernel,
        grid=(rows,),
        in_specs=[
            pl.BlockSpec((1, features, length), lambda r: (r, 0, 0)),
            pl.BlockSpec((1, length, width), lambda r: (r, 0, 0)),
        ],
        out_specs=[
            pl.BlockSpec(shape, lambda r: (0, 0, 0)),
            pl.BlockSpec(shape, lambda r: (0, 0, 0)),
            pl.BlockSpec((features, 1), lambda r: (0, 0)),
        ],
        out_shape=[
            jax.ShapeDtypeStruct(shape, F32),
            jax.ShapeDtypeStruct(shape, BF16),
            jax.ShapeDtypeStruct((features, 1), F32),
        ],
        scratch_shapes=[pltpu.VMEM((features, width), F32), pltpu.VMEM((width, features), F32)],
        compiler_params=pltpu.CompilerParams(vmem_limit_bytes=VMEM_LIMIT),
        cost_estimate=pl.CostEstimate(
            flops=2 * rows * length * width * features,
            bytes_accessed=2 * rows * length * (width + features) + 6 * width * features // 2,
            transcendentals=0,
        ),
    )(grad, normed)


def tail_kernel(
    images,
    mod,
    weight,
    cond,
    ada_ref,
    cond_ref,
    bias_ref,
    got,
    low_mine,
    low_got,
    row_mine,
    row_got,
    cond_mine,
    cond_got,
    column_got,
    sent,
    arrived,
):
    seq_count, row_total = lax.axis_size("seq"), lax.axis_size("rows")
    seq, row = lax.axis_index("seq"), lax.axis_index("rows")
    to_seq = [lax.rem(seq + m, seq_count) for m in range(seq_count)]
    to_row = [lax.rem(row + m, row_total) for m in range(row_total)]
    barrier = pltpu.get_barrier_semaphore()
    for m in range(1, seq_count):
        pl.semaphore_signal(barrier, inc=1, device_id={"seq": to_seq[m]}, device_id_type=pl.DeviceIdType.MESH)
    for m in range(1, row_total):
        pl.semaphore_signal(barrier, inc=1, device_id={"rows": to_row[m]}, device_id_type=pl.DeviceIdType.MESH)
    pl.semaphore_wait(barrier, seq_count + row_total - 2)

    used = [0]

    def start(source, target, device):
        copy = pltpu.make_async_remote_copy(
            src_ref=source,
            dst_ref=target,
            send_sem=sent.at[used[0]],
            recv_sem=arrived.at[used[0]],
            device_id=device,
            device_id_type=pl.DeviceIdType.MESH,
        )
        used[0] += 1
        copy.start()
        return copy

    copies = [start(mod.at[to_seq[m]], got.at[m], {"seq": to_seq[m]}) for m in range(1, seq_count)]
    column_got[0] = cond[row]
    column_copies = [start(cond.at[to_row[m]], column_got.at[m], {"rows": to_row[m]}) for m in range(1, row_total)]
    total = mod[seq]
    for m, copy in enumerate(copies):
        copy.wait()
        total = total + got[m + 1]
    low = total[:images].astype(BF16)
    low_mine[...] = low
    row_mine[...] = total[images:]
    row_mine[0:1] = jnp.sum(total[:images], axis=0, keepdims=True)
    low_got[0] = low
    copies = [start(low_mine, low_got.at[m], {"rows": to_row[m]}) for m in range(1, row_total)]
    copies += [start(row_mine, row_got.at[m], {"rows": to_row[m]}) for m in range(1, row_total)]
    term = lax.dot_general(low, weight[...], (((1,), (1,)), ((), ())), preferred_element_type=F32)
    cond_mine[...] = term
    cond_copies = [start(cond_mine, cond_got.at[m], {"seq": to_seq[m]}) for m in range(1, seq_count)]
    for copy in copies:
        copy.wait()
    sums = row_mine[...]
    for m in range(1, row_total):
        sums = sums + row_got[m]
    bias_ref[seq] = sums
    copies = [start(bias_ref.at[seq], bias_ref.at[seq], {"seq": to_seq[m]}) for m in range(1, seq_count)]
    for copy in column_copies:
        copy.wait()
    gathered = jnp.concatenate([low_got[m] for m in range(row_total)], axis=0)
    columns = jnp.concatenate([column_got[m] for m in range(row_total)], axis=0)
    ada_ref[...] = lax.dot_general(columns, gathered, (((0,), (0,)), ((), ())), preferred_element_type=F32)
    for m, copy in enumerate(cond_copies):
        copy.wait()
        term = term + cond_got[m + 1]
    cond_ref[...] = term
    for copy in copies:
        copy.wait()


def finish(mod, weight, cond, images):
    seq_count, lines, columns = mod.shape
    width, depth = weight.shape[0], cond.shape[2]
    row_total = lax.axis_size("rows")
    extra = lines - images
    copies = 3 * (seq_count - 1) + 3 * (row_total - 1)
    return pl.pallas_call(
        partial(tail_kernel, images),
        in_specs=[pl.BlockSpec(memory_space=pltpu.VMEM)] * 3,
        out_specs=[pl.BlockSpec(memory_space=pltpu.VMEM)] * 3,
        out_shape=[
            jax.ShapeDtypeStruct((depth, columns), F32),
            jax.ShapeDtypeStruct((images, width), F32),
            jax.ShapeDtypeStruct((seq_count, extra, columns), F32),
        ],
        scratch_shapes=[
            pltpu.VMEM((seq_count, lines, columns), F32),
            pltpu.VMEM((images, columns), BF16),
            pltpu.VMEM((row_total, images, columns), BF16),
            pltpu.VMEM((extra, columns), F32),
            pltpu.VMEM((row_total, extra, columns), F32),
            pltpu.VMEM((images, width), F32),
            pltpu.VMEM((seq_count, images, width), F32),
            pltpu.VMEM((row_total, images, depth), BF16),
            pltpu.SemaphoreType.DMA((copies,)),
            pltpu.SemaphoreType.DMA((copies,)),
        ],
        compiler_params=pltpu.CompilerParams(collective_id=0, has_side_effects=True, vmem_limit_bytes=VMEM_LIMIT),
        cost_estimate=pl.CostEstimate(flops=10**9, bytes_accessed=10**7, transcendentals=0),
    )(mod, weight, cond)


def gather_seq(values):
    count = lax.axis_size("seq")
    if count == 4:
        first, second = swap(values, "seq", 1), swap(values, "seq", 2)
        half = values.shape[0] // 2
        third = jnp.concatenate([swap(second[:half], "seq", 1), swap(first[half:], "seq", 2)], axis=0)
        return [values, first, second, third]
    return [values] + [swap(values, "seq", m) for m in range(1, count)]


def exchange_seq(blocks):
    return [blocks[0]] + [swap(blocks[m], "seq", m) for m in range(1, len(blocks))]


def in_order(blocks, axis):
    index = lax.axis_index("seq")
    stacked = jnp.stack(blocks, axis=axis)
    return flip_blocks(stacked, axis, index)


class Halving:
    def __init__(self, blocks, low_first):
        self.blocks = dict(enumerate(blocks))
        bits = [1 << k for k in range(len(blocks).bit_length() - 1)]
        self.bits = bits if low_first else bits[::-1]

    def send(self):
        self.bit = self.bits.pop(0)
        self.kept = [m for m in self.blocks if not m & self.bit]
        return jnp.stack([self.blocks[m | self.bit] for m in self.kept]).astype(BF16)

    def move(self, sent):
        return swap(sent, "seq", self.bit)

    def add(self, came):
        self.blocks = {m: self.blocks[m] + came[k].astype(F32) for k, m in enumerate(self.kept)}


class Spreading:
    def __init__(self, pick):
        chip, chips = lax.axis_index("rows") // 2, lax.axis_size("rows") // 2
        self.own = pick(chip)
        self.sent = [pick(chip ^ m).astype(BF16) for m in range(1, chips)]

    def move(self):
        self.came = [swap(block, "rows", 2 * (m + 1)) for m, block in enumerate(self.sent)]

    def total(self):
        total = self.own
        for block in self.came:
            total = total + block.astype(F32)
        return total


def columns_of(values, index, size):
    return lax.dynamic_slice_in_dim(values, index * size, size, values.ndim - 1)


def lines_of(values, index, size):
    return lax.dynamic_slice_in_dim(values, index * size, size, 0)


def tied(*values):
    return lax.optimization_barrier(values)


def on_device(
    tokens,
    conditioning,
    segment_ids,
    image_index,
    row_fill,
    ada_weight,
    ada_bias,
    qkv_weight,
    qv_bias,
    proj_weight,
    proj_bias,
    up_weight,
    up_bias,
    down_weight,
    down_bias,
    cotangent,
):
    row_count, local_len, width = tokens.shape
    seq_count, groups = lax.axis_size("seq"), lax.axis_size("rows")
    seq_index, row_index = lax.axis_index("seq"), lax.axis_index("rows")
    chips, core = groups // 2, row_index % 2
    full_len = local_len * seq_count
    token_count = row_count * local_len
    heads_dev = HEADS // seq_count
    head_size = width // HEADS
    own = heads_dev * head_size
    image_count = conditioning.shape[0]
    hidden_size = up_weight.shape[1]
    depth = width // groups

    tokens_all = jnp.concatenate(gather_seq(tokens), axis=1)
    order = lax.iota(jnp.int32, seq_count) ^ seq_index
    seg_blocks = flip_blocks(segment_ids.reshape(row_count, seq_count, local_len), 1, seq_index)
    seg_all = seg_blocks.reshape(row_count, full_len)
    places = (order[:, None] * local_len + lax.iota(jnp.int32, local_len)).reshape(1, full_len)
    codes = jnp.where(places < row_fill[:, None], seg_all, -1 - places)
    code_col, code_row = codes[:, :, None], codes[:, None, :]

    qkv_own = jnp.concatenate(
        [lax.dynamic_slice_in_dim(qkv_weight, part * width + seq_index * own, own, 1).T for part in range(3)], axis=0
    )
    bias_own = lax.dynamic_slice_in_dim(qv_bias.astype(F32), seq_index * own, own, 1)
    bias_own = jnp.concatenate([bias_own[0], jnp.zeros((own,), F32), bias_own[1]])

    cond_wide = conditioning.astype(F32)
    cond_low = jax.nn.silu(cond_wide).astype(BF16)
    mod_part = jnp.dot(cond_low, ada_weight, preferred_element_type=F32)
    modulation = lax.all_gather(mod_part, "seq", axis=1, tiled=True) + ada_bias.astype(F32)
    cond_cols = cond_low.reshape(image_count, groups, depth).transpose(1, 0, 2)
    local_seg = lax.dynamic_slice_in_dim(segment_ids, seq_index * local_len, local_len, 1)
    slot_ids = lax.iota(jnp.int32, image_index.shape[1])
    slot_mod = jnp.take(modulation, image_index, axis=0)

    normed_all, packed = project_qkv(
        tokens_all, seg_all, slot_mod[:, :, : 2 * width], qkv_own, bias_own, heads_dev, min(256, full_len)
    )
    square = seq_count == 4 and chips == 4
    attended, log_totals, *attended_sent = attend(packed, code_col, code_row, 512, square)

    slot_pick = (local_seg[:, :, None] == slot_ids).astype(F32)
    mod_tok = jnp.einsum("rts,rse->rte", slot_pick, slot_mod, precision=lax.Precision.HIGHEST)
    shift_a, scale_a, gate_a, shift_b, scale_b, gate_b = jnp.split(mod_tok, 6, axis=-1)
    tokens_wide = tokens.astype(F32)
    upstream = cotangent.astype(F32)
    grad_branch_b = (upstream * gate_b).astype(BF16)
    part_down_bias = jnp.sum(grad_branch_b.astype(F32), axis=(0, 1))
    grad_out = grad_branch_b.reshape(token_count, width)
    grad_turned = turn_halves(grad_out, seq_count, core)

    def by_block(values):
        return [values[..., m * local_len : (m + 1) * local_len] for m in range(seq_count)]

    if square:
        attended_tok = attended_sent[0]
    else:
        attended_tok = in_order(exchange_seq(by_block(attended.reshape(row_count, own, full_len))), 1)
    attended_tok = attended_tok.reshape(row_count, width, local_len)
    branch_a = jnp.einsum(
        "rft,fe->rte", attended_tok, proj_weight, preferred_element_type=F32
    ) + proj_bias.astype(F32)
    middle = tokens_wide + gate_a * branch_a
    normed_b = modulate(middle, shift_b, scale_b).astype(BF16).reshape(token_count, width)
    normed_turned = turn_halves(normed_b, chips, core)

    if square:
        out_sum, grad_sum, part_up_bias, grad_up_weight, down_turned = feed_forward_reduce(
            normed_b, grad_out, normed_turned, grad_turned, up_weight, down_weight, up_bias.astype(F32)
        )
        part_up_bias = part_up_bias.reshape(1, hidden_size)
    else:
        out_sum, grad_sum, up_keep, up_send, down_keep, down_send, part_up_bias = feed_forward(
            normed_b, grad_out, normed_turned, grad_turned, up_weight, down_weight, up_bias.astype(F32)[None], 512
        )
        up_came, down_came = swap(up_send, "rows", 1), swap(down_send, "rows", 1)
    branch_b = out_sum.reshape(row_count, local_len, width) + down_bias.astype(F32)
    grad_normed_b = grad_sum.reshape(row_count, local_len, width)
    block_out = (middle + gate_b * branch_b).astype(BF16)
    grad_gate_b = upstream * branch_b
    _, norm_back_b = jax.vjp(modulate, middle, shift_b, scale_b)
    grad_mid_norm, grad_shift_b, grad_scale_b = norm_back_b(grad_normed_b)
    grad_middle = upstream + grad_mid_norm
    grad_branch_a = (grad_middle * gate_a).astype(BF16)
    grad_gate_a = grad_middle * branch_a
    part_proj_bias = jnp.sum(grad_branch_a.astype(F32), axis=(0, 1))
    grad_attended = jnp.einsum(
        "fe,rte->rft", proj_weight, grad_branch_a, preferred_element_type=F32
    ).astype(BF16)
    heads_blocks = [lax.dynamic_slice_in_dim(grad_attended, (seq_index ^ m) * own, own, 1) for m in range(seq_count)]
    grad_heads_in = jnp.concatenate(exchange_seq(heads_blocks), axis=2)
    grad_view = grad_heads_in.reshape(row_count, heads_dev, head_size, full_len)

    part_proj = jnp.einsum("rte,rft->ef", grad_branch_a, attended_tok, preferred_element_type=F32)
    proj_view = part_proj.reshape(seq_count, 2, depth * groups // (2 * seq_count), width)
    proj_keep = lax.dynamic_index_in_dim(proj_view, core, 1, keepdims=False)
    proj_send = lax.dynamic_index_in_dim(proj_view, 1 - core, 1, keepdims=False).astype(BF16)
    proj_came = swap(proj_send, "rows", 1).reshape(width // 2, width)
    proj_keep = proj_keep.reshape(width // 2, width)
    up_size, down_size = hidden_size // seq_count, width // (2 * seq_count)
    proj_blocks = [
        lines_of(proj_keep, seq_index ^ m, down_size) + lines_of(proj_came, seq_index ^ m, down_size).astype(F32)
        for m in range(seq_count)
    ]
    if square:
        proj_sent = [block.astype(BF16) for block in proj_blocks[1:]]
        grad_view, *proj_sent = tied(grad_view, *proj_sent)
        proj_total = proj_blocks[0]
        for m in range(1, seq_count):
            proj_total = proj_total + swap(proj_sent[m - 1], "seq", m).astype(F32)
    else:
        ups = Halving(
            [
                columns_of(up_keep, seq_index ^ m, up_size) + columns_of(up_came, seq_index ^ m, up_size).astype(F32)
                for m in range(seq_count)
            ],
            True,
        )
        downs = Halving(
            [
                jnp.concatenate(
                    [
                        lines_of(down_keep, seq_index ^ m, down_size)
                        + lines_of(down_came, seq_index ^ m, down_size).astype(F32),
                        proj_blocks[m],
                    ],
                    axis=1,
                )
                for m in range(seq_count)
            ],
            False,
        )
        up_sent, down_sent = ups.send(), downs.send()
        up_came, down_came = ups.move(up_sent), downs.move(down_sent)

    grad_heads, *grad_sent = attend_back(
        packed, attended, grad_view, log_totals, code_col, code_row, 256, 512, square
    )
    grad_own = grad_heads.reshape(row_count, 3 * own, full_len)
    if square:
        grad_flat = grad_sent[0]
    else:
        grad_blocks = exchange_seq(by_block(grad_own))
        grad_flat = in_order([block.reshape(row_count, 3, own, local_len) for block in grad_blocks], 2)
    grad_flat = grad_flat.reshape(row_count, 3 * width, local_len)

    qkv_keep, qkv_send, own_sums = qkv_weight_grad(grad_own, normed_all)
    down_part, proj_part = hidden_size // chips, width // chips
    if square:
        proj_spread = Spreading(lambda chip: columns_of(proj_total, chip, proj_part))
        grad_flat, qkv_send, *proj_spread.sent = tied(grad_flat, qkv_send, *proj_spread.sent)
        proj_spread.move()
    else:
        while ups.bits:
            ups.add(up_came)
            downs.add(down_came)
            up_came, down_came = ups.move(ups.send()), downs.move(downs.send())
        ups.add(up_came)
        downs.add(down_came)
        up_total, down_total = ups.blocks[0], downs.blocks[0][:, :hidden_size]
        proj_total = downs.blocks[0][:, hidden_size:]
        up_spread = Spreading(lambda chip: lines_of(up_total, chip, depth))
        down_spread = Spreading(
            lambda chip: jnp.concatenate(
                [columns_of(down_total, chip, down_part), columns_of(proj_total, chip, proj_part)], axis=1
            )
        )
        up_spread.move()
        down_spread.move()
    qkv_came = swap(qkv_send, "rows", 1)
    grad_normed_a = jnp.einsum("rft,df->rtd", grad_flat, qkv_weight, preferred_element_type=F32)
    _, norm_back_a = jax.vjp(modulate, tokens_wide, shift_a, scale_a)
    grad_tok_norm, grad_shift_a, grad_scale_a = norm_back_a(grad_normed_a)
    grad_tokens = grad_middle + grad_tok_norm
    grad_mod_tok = jnp.concatenate(
        [grad_shift_a, grad_scale_a, grad_gate_a, grad_shift_b, grad_scale_b, grad_gate_b], axis=-1
    )
    slot_grads = jnp.einsum("rts,rte->rse", slot_pick, grad_mod_tok, precision=lax.Precision.HIGHEST)
    image_pick = (image_index[:, :, None] == lax.iota(jnp.int32, image_count)).astype(F32)
    grad_modulation = jnp.einsum("rsi,rse->ie", image_pick, slot_grads, precision=lax.Precision.HIGHEST)

    own_sums = own_sums.reshape(3, own)
    part_qv = lax.dynamic_update_slice(
        jnp.zeros((2, width), F32), jnp.stack([own_sums[0], own_sums[2]]), (0, seq_index * own)
    )
    small = jnp.concatenate([part_qv.reshape(-1), part_proj_bias, part_up_bias[0], part_down_bias])
    columns = ada_weight.shape[1]
    lines = -(-small.size // (seq_count * columns))
    room = seq_count * columns * lines
    small = jnp.pad(small, (0, room - small.size)).reshape(seq_count, lines, columns)
    mod_view = grad_modulation.reshape(image_count, seq_count, columns).transpose(1, 0, 2)
    joined = jnp.concatenate(
        [mod_view, jnp.zeros((seq_count, 1, columns), F32), small, jnp.zeros((seq_count, 7 - lines, columns), F32)], axis=1
    )
    qkv_both = qkv_keep + qkv_came.astype(F32)
    qkv_spread = Spreading(lambda chip: lax.dynamic_index_in_dim(qkv_both, chip, 0, keepdims=False))
    joined, *qkv_spread.sent = tied(joined, *qkv_spread.sent)
    qkv_spread.move()
    if square:
        turned = jnp.concatenate([down_turned, proj_spread.total()], axis=1)
    else:
        grad_up_weight, turned = up_spread.total(), down_spread.total()
    half = down_part // 2
    cut = lambda index: jnp.concatenate(
        [columns_of(turned[:, :down_part], index, half), columns_of(turned[:, down_part:], index, proj_part // 2)], axis=1
    )
    core_keep, core_sent = cut(core), cut(1 - core)
    joined, core_sent = tied(joined, core_sent)
    core_came = swap(core_sent, "rows", 1)
    grad_ada_weight, cond_sum, bias_sums = finish(joined, ada_weight, cond_cols, image_count)
    _, silu_back = jax.vjp(jax.nn.silu, cond_wide)
    grad_cond = silu_back(cond_sum)[0]
    grad_ada_bias = bias_sums[:, 0].reshape(-1)
    small = bias_sums[:, 1 : 1 + lines].reshape(-1)
    grad_qv_bias = small[: 2 * width].reshape(2, width)
    grad_proj_bias = small[2 * width : 3 * width]
    grad_up_bias = small[3 * width : 3 * width + hidden_size]
    grad_down_bias = small[3 * width + hidden_size : 4 * width + hidden_size]

    pair = flip_blocks(jnp.stack([core_keep, core_came]), 0, core).reshape(-1, core_keep.shape[1])
    grad_down_weight, grad_proj_weight = pair[:, :half].T, pair[:, half:].T

    qkv_total = qkv_spread.total()
    pieces = []
    for place in range(3):
        pairs = [((3 * target + place) % seq_count, target) for target in range(seq_count)]
        part_of = [0] * seq_count
        for source, target in pairs:
            part_of[source] = (3 * target + place) // seq_count
        chosen = columns_of(qkv_total, jnp.array(part_of, jnp.int32)[seq_index], own)
        pieces.append(lax.ppermute(chosen, "seq", pairs))
    grad_qkv_weight = jnp.concatenate(pieces, axis=1)
    return (
        block_out,
        grad_tokens,
        grad_cond,
        grad_ada_weight,
        grad_ada_bias,
        grad_qkv_weight,
        grad_qv_bias,
        grad_proj_weight,
        grad_proj_bias,
        grad_up_weight,
        grad_up_bias,
        grad_down_weight,
        grad_down_bias,
    )


def solution(mesh):
    in_specs = (
        P("rows", "seq", None),
        P("rows", None),
        P("rows", None),
        P("rows", None),
        P("rows"),
        P(None, "seq"),
        P(),
        P(),
        P(),
        P(),
        P(),
        P(),
        P(),
        P(),
        P(),
        P("rows", "seq", None),
    )
    out_specs = (
        P("rows", "seq", None),
        P("rows", "seq", None),
        P("rows", None),
        P("rows", "seq"),
        P(),
        P("rows", "seq"),
        P(),
        P("rows", "seq"),
        P(),
        P("rows", "seq"),
        P(),
        P("rows", "seq"),
        P(),
    )
    return jax.shard_map(
        on_device, mesh=mesh, in_specs=in_specs, out_specs=out_specs, check_vma=False
    )
```

time: 815 us -> 509 us (0.62)
  Pallas kernels: 57.1 us -> 263 us
  local copies, waits for them, and re-layouts: 241 us -> 76.1 us
  waiting for transfers between devices: 126 us -> 13.6 us
  blocking collectives: 115 us -> 9.13 us
  matrix products: 133 us -> 41.8 us
  starting transfers between devices: 53.4 us -> 30.3 us
  other arithmetic: 78 us -> 64.7 us
    pallas_call x1 -> x4, Pallas kernels: 26.6 us -> 224 us  [the longest x1 114 us: feed_forward_reduce(): pl.pallas_call(partial(mlp_reduce_kernel, tiles), grid=(tiles + STAGES,),...]
    ppermute x47 -> x19, waiting for transfers between devices: 126 us -> 12.4 us  [swap(): return lax.ppermute(values, axis, [(i, i ^ mask) for i in range(count)])]
    dot_general x13 -> x4, matrix products: 116 us -> 24 us  [the longest x1 12 us: on_device(): jnp.einsum('rft,df->rtd', grad_flat, qkv_weight, preferred_element_type=F32)]
    reshape x12 -> x8, local copies, waits for them, and re-layouts: 68.1 us -> 1.49 us  [the longest x1 0.63 us: feed_forward_reduce(): bias.reshape(4, 1, part)]
    all_gather x3 -> x0, blocking collectives: 64.2 us -> none  [the longest x1 29 us: on_device(): cond_all = lax.all_gather(cond_low, 'rows', axis=0, tiled=True)]
    psum x1 -> x0, blocking collectives: 41.8 us -> none  [on_device(): lax.psum((part_qv_bias, part_ada_bias), ('rows', 'seq'))]
    ppermute x47 -> x19, starting transfers between devices: 53.4 us -> 23 us  [swap(): return lax.ppermute(values, axis, [(i, i ^ mask) for i in range(count)])]
    add x19 -> x4, other arithmetic: 35.8 us -> 6.05 us  [the longest x2 2.78 us: total(): total = total + block.astype(F32)]
  transfers between devices with their start and end apart: 47 -> 22, of which waited for: 14 -> 5; matrix products, arithmetic and copies ran while one was open for 39% -> 23% of each run, Pallas kernels for 3% -> 22%
where the time goes in v2:
time: 509 us; the launch traced here: 502 us
  Pallas kernels  263 us (52%)
  local copies, waits for them, and re-layouts  76.1 us (15%)
  other arithmetic  64.7 us (13%)
  matrix products  41.8 us (8%)
  starting transfers between devices  30.3 us (6%)
  waiting for transfers between devices  13.6 us (3%)
  blocking collectives  9.13 us (2%)
    pallas_call x1, Pallas kernels, feed_forward_reduce(): pl.pallas_call(partial(mlp_reduce_kernel, tiles), grid=(tiles + STAGES,),...  114 us
    pallas_call x1, Pallas kernels, attend_back(): pl.pallas_call(partial(attend_back_kernel, block, inner, size ** (-0.5),...  53.5 us
    pallas_call x1, Pallas kernels, finish(): pl.pallas_call(partial(tail_kernel, images), in_specs=[pl.BlockSpec(memor...  46.1 us
    unnamed x142, local copies, waits for them, and re-layouts  27.5 us
    pallas_call x1, Pallas kernels, attend(): pl.pallas_call(partial(attend_kernel, block, size ** (-0.5) * LOG2E), gri...  26 us
    ppermute x19, starting transfers between devices, swap(): return lax.ppermute(values, axis, [(i, i ^ mask) for i in range(count)])  23 us
    pallas_call x1, Pallas kernels, project_qkv(): pl.pallas_call(qkv_kernel, grid=(rows, length // block), in_specs=[pl.Blo...  12.8 us
    ppermute x19, waiting for transfers between devices, swap(): return lax.ppermute(values, axis, [(i, i ^ mask) for i in range(count)])  12.4 us
  transfers between devices with their start and end apart: 22, of which 5 were waited for; matrix products, arithmetic and copies ran while one was open for 23% of the time, Pallas kernels for 22%

profile of v2, /device:TPU:0, one launch (start us, length us, event | category | flops | bytes accessed | tf_op | source)
XLA Modules:
  0.0 502.4 jit_solution(16011049294379006257)
XLA Ops:
  0.7 3.0 collective-permute-start.1
  3.7 1.5 collective-permute-start
  15.0 6.5 %copy.79.weight = bf16[1152,1728]{1,0:T(8,128)(2,1)} copy(bf16[1152,1728]{0,1:T(8,128)(2,1)} %param.24) | data formatting | bytes 7962624 | tf_op args[5]
  21.4 3.9 convolution_bitcast_fusion.1
  26.0 4.7 constant_dynamic-slice_fusion.15
  30.7 2.3 copy.88
  33.0 2.3 copy.86
  39.5 1.3 copy.64
  41.6 9.1 %all-gather = f32[4,1728,16]{1,2,0:T(8,128)S(1)} all-gather(f32[1,1728,16]{1,2,0:T(8,128)} %convolution_bitcast_fusion.1), channel_id=1, replica_groups=mesh['rows'=8,'seq'=4] {'seq'}, dimensions={0}, use_global_device_ids=true | all-gather | bytes 552960 | tf_op jit(solution)/shard_map/all_gather | solution.py:1000
  51.8 2.1 reshape.535
  53.9 1.8 add_bitcast_fusion
  55.8 2.7 gather_fusion
  64.1 2.1 compare_select_fusion
  66.4 1.4 slice.79
  71.2 8.8 %fusion.31 = f32[2,256,6912]{2,1,0:T(8,128)} fusion(f32[2,8,6912]{2,1,0:T(8,128)S(1)} %copy-done.34, s32[2,256]{1,0:T(2,128)S(1)} %constant_dynamic-slice_fusion.16), kind=kOutput, calls=%fused_computation.109 | convolution fusion | flops 339742720 | bytes 14600192 | tf_op jit(solution)/shard_map/rts,rse->rte/dot_general | solution.py:1013
  80.7 1.8 collective-permute-done.3
  82.5 4.5 maximum_maximum_fusion.tokens
  87.0 12.8 %shard_map.282 = (bf16[2,1024,1152]{2,1,0:T(8,128)(2,1)}, bf16[2,3,4,72,1024]{4,3,2,1,0:T(8,128)(2,1)}) custom-call(s32[1,24]{1,0:T(1,128)S(1)} %broadcast_in_dim_tile.3.slot_row, s32[2,1024,1]{2,1,0:T(8,128)S(1)} %get-tuple-element.131.seg, f32[2,8,2304]{2,1,0:T(8,128)S(1)} %slice.78.mod, bf16[2,1024,1152]{2,1,0:T(8,128)(2,1)} %maximum_maximum_fusion.tokens, ...), custom_call_target="tpu_custom_call" | custom-call | flops 4076863488 | bytes 12976128 | tf_op jit(solution)/shard_map/pallas_call | solution.py:67
  99.8 26.0 %shard_map.283 = (bf16[2,4,72,1024]{3,2,1,0:T(8,128)(2,1)S(1)}, f32[2,4,1,1024]{3,2,1,0:T(1,128)S(1)}, bf16[2,4,4,72,256]{4,3,2,1,0:T(8,128)(2,1)S(1)}) custom-call(s32[2,1024,1]{2,1,0:T(8,128)S(1)} %get-tuple-element.130.code_col, s32[2,1,1024]{2,1,0:T(1,128)S(1)} %compare_select_fusion.1.code_row, ...), custom_call_target="tpu_custom_call" | custom-call | flops 8589934592 | bytes 4718592 | tf_op jit(solution)/shard_map/pallas_call | solution.py:187
  125.9 6.7 %fusion.43 = (f32[2,256]{1,0:T(2,128)S(1)}, f32[2,256,1152]{2,1,0:T(8,128)S(1)}, f32[2,256]{1,0:T(2,128)}, f32[2,256,1152]{2,1,0:T(8,128)}) fusion(f32[2,256,6912]{2,1,0:T(8,128)} %fusion.31, bf16[2,256,1152]{2,1,0:T(8,128)(2,1)S(1)} %copy-done.20, f32[1152]{0:T(1024)S(1)} %convert_element_type.140, bf16[2,1152,256]{2,1,0:T(8,128)(2,1)S(1)} %bitcast.120, ...), kind=kOutput, calls=%fused_computation.166 | convolution fusion | flops 1362492416 | bytes 12100096 | tf_op jit(solution)/shard_map/rft,fe->rte/dot_general | solution.py:1030
  133.0 1.7 copy-done.18
  134.7 5.6 %convert_reduce_fusion.1 = (f32[1152]{0:T(1024)}, bf16[2,256,1152]{2,1,0:T(8,128)(2,1)}, bf16[2,256,1152]{2,1,0:T(8,128)(2,1)}) fusion(f32[2,256,6912]{2,1,0:T(8,128)} %fusion.31, bf16[2,256,1152]{2,1,0:T(8,128)(2,1)S(1)} %copy-done.18, f32[2,256]{1,0:T(2,128)S(1)} %fusion.36, f32[2,256,1152]{2,1,0:T(8,128)S(1)} %get-tuple-element.129, ...), kind=kLoop, calls=%fused_computation.36 | loop fusion | flops 6486912 | bytes 12984832 | tf_op jit(solution)/shard_map/reduce_sum | solution.py:1018
  140.3 2.4 copy.72
  142.7 2.5 copy.71
  145.2 1.4 constant_dynamic-slice_fusion.9
  149.1 113.7 %shard_map.284 = (f32[512,1152]{1,0:T(8,128)}, f32[512,1152]{1,0:T(8,128)}, f32[4,1,1152]{2,1,0:T(1,128)}, f32[144,1152]{1,0:T(8,128)}, f32[144,1152]{1,0:T(8,128)}) custom-call(bf16[512,1152]{1,0:T(8,128)(2,1)} %bitcast.137, bf16[512,1152]{1,0:T(8,128)(2,1)} %bitcast.135, bf16[1152,512]{1,0:T(8,128)(2,1)} %pad_maximum_fusion.2.normed_turned, ...), custom_call_target="tpu_custom_call" | custom-call | flops 32614907904 | bytes 31850496 | tf_op jit(solution)/shard_map/pallas_call | solution.py:658
  262.8 3.0 multiply_reduce_fusion
  266.6 4.0 add_add_fusion.1
  270.6 1.9 reduce_sum.92
  272.5 4.8 convert_reduce_fusion.2
  277.3 2.4 copy.74
  279.7 3.4 fusion.45
  285.5 1.9 convolution_convert_fusion
  288.2 1.3 collective-permute-start.4
  290.3 1.5 collective-permute-start.6
  294.9 3.4 constant_dynamic-slice_fusion.7
  298.4 1.9 collective-permute-done.4
  300.3 7.9 %collective-permute-done.5 = bf16[2,288,256]{1,2,0:T(8,128)(2,1)S(1)} collective-permute-done((bf16[2,288,256]{1,2,0:T(8,128)(2,1)S(1)}, bf16[2,288,256]{1,2,0:T(8,128)(2,1)S(1)}, u32[]{:S(2)}, u32[]{:S(2)}) %collective-permute-start.5) | collective-permute-done | bytes 294944 | tf_op jit(solution)/shard_map/ppermute | solution.py:32
  308.2 1.3 pad_maximum_fusion.1
  309.5 2.0 copy.73
  311.6 3.0 add_convert_fusion.1
  314.5 1.5 collective-permute-start.10
  318.0 53.5 %shard_map.285 = (bf16[2,3,4,72,1024]{4,3,2,1,0:T(8,128)(2,1)}, bf16[2,3,4,4,72,256]{5,4,3,2,1,0:T(8,128)(2,1)}) custom-call(s32[2,1024,1]{2,1,0:T(8,128)S(1)} %copy-done.7, s32[2,1,1024]{2,1,0:T(1,128)S(1)} %compare_select_fusion.1.code_row, bf16[2,3,4,72,1024]{4,3,2,1,0:T(8,128)(2,1)} %get-tuple-element.46.query.key.value, ...), custom_call_target="tpu_custom_call" | custom-call | flops 21474836480 | bytes 9437184 | tf_op jit(solution)/shard_map/pallas_call | solution.py:311
  371.6 10.6 %shard_map.286 = (f32[4,144,864]{2,1,0:T(8,128)S(1)}, bf16[4,144,864]{2,1,0:T(8,128)(2,1)}, f32[864,1]{1,0:T(8,128)S(1)}) custom-call(bf16[2,864,1024]{2,1,0:T(8,128)(2,1)} %bitcast.155, bf16[2,1024,1152]{2,1,0:T(8,128)(2,1)} %get-tuple-element.55.normed), custom_call_target="tpu_custom_call" | custom-call | flops 4076863488 | bytes 11243520 | tf_op jit(solution)/shard_map/pallas_call | solution.py:745
  383.7 1.6 convert_add_fusion.3
  386.1 1.3 collective-permute-start.12
  387.5 2.5 collective-permute-start.13
  390.5 12.0 %fusion.8 = (f32[2,256]{1,0:T(2,128)S(1)}, f32[2,256]{1,0:T(2,128)S(1)}, f32[2,256,6912]{2,1,0:T(8,128)S(1)}, f32[2,256,1152]{2,1,0:T(8,128)}) fusion(bf16[2,256,1152]{2,1,0:T(8,128)(2,1)} %param.19, f32[2,256]{1,0:T(2,128)S(1)} %broadcast_multiply_fusion, f32[2,256,6912]{2,1,0:T(8,128)} %fusion.31, bf16[2,3456,256]{2,1,0:T(8,128)(2,1)} %bitcast.154, ...), kind=kOutput, calls=%fused_computation.25 | convolution fusion | flops 4081581056 | bytes 19765248 | tf_op jit(solution)/shard_map/rft,df->rtd/dot_general | solution.py:1141
  402.6 3.4 fusion.18
  406.7 4.0 fusion.11
  411.2 1.3 copy-done.17
  412.6 1.5 copy-done.14
  414.5 1.3 copy-done.26
  416.5 4.6 fusion.30
  422.3 1.2 convert_add_fusion.4
  424.7 1.6 convert_add_fusion.2
  428.3 3.4 collective-permute-start.16
  432.3 46.1 %shard_map.287 = (f32[144,1728]{1,0:T(8,128)S(1)}, f32[16,1152]{1,0:T(8,128)S(1)}, f32[4,8,1728]{2,1,0:T(8,128)S(1)}) custom-call(f32[4,24,1728]{2,1,0:T(8,128)S(1)} %maximum_maximum_fusion.1.mod, bf16[1152,1728]{1,0:T(8,128)(2,1)S(1)} %copy-done.2, bf16[8,16,144]{2,1,0:T(8,128)(2,1)S(1)} %bitcast.123), custom_call_target="tpu_custom_call" | custom-call | flops 1000000000 | bytes 10000000 | tf_op jit(solution)/shard_map/pallas_call | solution.py:860
  482.0 1.5 fusion.20
  484.7 3.5 collective-permute-start.18
  489.1 2.9 collective-permute-start.20
  492.1 1.7 gather_fusion.2
  493.8 1.3 bitcast_select_fusion
  498.2 2.1 pad_maximum_fusion.5
  (262 shorter events, 57.8 us)
Async XLA Ops:
  0.6 125.2 %copy-start = (bf16[1152,1152]{1,0:T(8,128)(2,1)S(1)}, bf16[1152,1152]{1,0:T(8,128)(2,1)}, u32[]{:S(2)}) copy-start(bf16[1152,1152]{1,0:T(8,128)(2,1)} %param.28) | copy-start | bytes 7962628
  0.7 65.8 %collective-permute-start.1 = (bf16[2,256,1152]{2,1,0:T(8,128)(2,1)}, bf16[2,256,1152]{2,1,0:T(8,128)(2,1)}, u32[]{:S(2)}, u32[]{:S(2)}) collective-permute-start(bf16[2,256,1152]{2,1,0:T(8,128)(2,1)} %param.19), channel_id=1, source_target_pairs={{0,2},{1,3},{2,0},{3,1},{4,6},{5,7},{6,4},{7,5},{8,10},{9,11},{10,... | collective-permute-start | bytes 3538952 | tf_op jit(solution)/shard_map/ppermute | solution.py:32
  3.7 65.4 %collective-permute-start = (bf16[2,256,1152]{2,1,0:T(8,128)(2,1)}, bf16[2,256,1152]{2,1,0:T(8,128)(2,1)}, u32[]{:S(2)}, u32[]{:S(2)}) collective-permute-start(bf16[2,256,1152]{2,1,0:T(8,128)(2,1)} %param.19), channel_id=1, source_target_pairs={{0,1},{1,0},{2,3},{3,2},{4,5},{5,4},{6,7},{7,6},{8,9},{9,8},{10,11... | collective-permute-start | bytes 3538952 | tf_op jit(solution)/shard_map/ppermute | solution.py:32
  15.0 6.5 %copy-start.39 = (bf16[16,1152]{1,0:T(8,128)(2,1)S(1)}, bf16[16,1152]{1,0:T(8,128)(2,1)}, u32[]{:S(2)}) copy-start(bf16[16,1152]{1,0:T(8,128)(2,1)} %param.20) | copy-start | bytes 110596
  30.7 8.3 %copy-start.55 = (s32[2,1024]{1,0:T(2,128)S(1)}, s32[2,1024]{1,0:T(2,128)}, u32[]{:S(2)}) copy-start(s32[2,1024]{1,0:T(2,128)} %param.21) | copy-start | bytes 24580
  36.4 17.5 %copy-start.54 = (bf16[6912]{0:T(1024)(128)(2,1)S(1)}, bf16[6912]{0:T(1024)(128)(2,1)}, u32[]{:S(2)}) copy-start(bf16[6912]{0:T(1024)(128)(2,1)} %param.25) | copy-start | bytes 41476
  55.7 4.7 copy-start.57
  55.7 4.8 copy-start.56
  55.7 5.4 %copy-start.58 = (bf16[1152]{0:T(1024)(128)(2,1)S(1)}, bf16[1152]{0:T(1024)(128)(2,1)}, u32[]{:S(2)}) copy-start(bf16[1152]{0:T(1024)(128)(2,1)} %param.33) | copy-start | bytes 6916
  55.7 6.6 %copy-start.65 = (pred[2]{0:T(512)(128)(4,1)S(1)}, pred[2]{0:T(512)(128)(4,1)}, u32[]{:S(2)}) copy-start(pred[2]{0:T(512)(128)(4,1)} %compare_and_fusion) | copy-start | bytes 10
  55.7 7.4 %copy-start.42 = (bf16[16,1152]{1,0:T(8,128)(2,1)S(1)}, bf16[16,1152]{1,0:T(8,128)(2,1)}, u32[]{:S(2)}) copy-start(bf16[16,1152]{1,0:T(8,128)(2,1)} %fusion.27) | copy-start | bytes 110596
  55.8 7.6 %copy-start.63 = (s32[2]{0:T(128)S(1)}, s32[2]{0:T(128)}, u32[]{:S(2)}) copy-start(s32[2]{0:T(128)} %fusion.39) | copy-start | bytes 28
  55.8 8.3 %copy-start.60 = (s32[2]{0:T(128)S(1)}, s32[2]{0:T(128)}, u32[]{:S(2)}) copy-start(s32[2]{0:T(128)} %param.23) | copy-start | bytes 28
  60.5 10.7 %copy-start.45 = (s32[2,256]{1,0:T(2,128)}, s32[2,256]{1,0:T(2,128)S(1)}, u32[]{:S(2)}) copy-start(s32[2,256]{1,0:T(2,128)S(1)} %constant_dynamic-slice_fusion.16) | copy-start | bytes 6148
  66.2 33.6 %copy-start.6 = (s32[2,1024,1]{2,1,0:T(8,128)}, s32[2,1024,1]{2,1,0:T(8,128)S(1)}, u32[]{:S(2)}) copy-start(s32[2,1024,1]{2,1,0:T(8,128)S(1)} %get-tuple-element.130.code_col) | copy-start | bytes 24580
  66.3 4.9 copy-start.34
  67.9 12.8 %collective-permute-start.2 = (bf16[1,256,1152]{2,1,0:T(8,128)(2,1)S(1)}, bf16[1,256,1152]{2,1,0:T(8,128)(2,1)S(1)}, u32[]{:S(2)}, u32[]{:S(2)}) collective-permute-start(bf16[1,256,1152]{2,1,0:T(8,128)(2,1)S(1)} %slice.79), channel_id=1, source_target_pairs={{0,1},{1,0},{2,3},{3,2},{4,5},{5,4},{6,7},{7,6},{8,9},{9,8},{10,11... | collective-permute-start | bytes 1769480 | tf_op jit(solution)/shard_map/ppermute | solution.py:32
  70.2 12.3 %copy-start.20 = (bf16[2,256,1152]{2,1,0:T(8,128)(2,1)S(1)}, bf16[2,256,1152]{2,1,0:T(8,128)(2,1)}, u32[]{:S(2)}) copy-start(bf16[2,256,1152]{2,1,0:T(8,128)(2,1)} %param.19) | copy-start | bytes 3538948
  70.2 12.3 %collective-permute-start.3 = (bf16[1,256,1152]{2,1,0:T(8,128)(2,1)S(1)}, bf16[1,256,1152]{2,1,0:T(8,128)(2,1)S(1)}, u32[]{:S(2)}, u32[]{:S(2)}) collective-permute-start(bf16[1,256,1152]{2,1,0:T(8,128)(2,1)S(1)} %slice.80), channel_id=1, source_target_pairs={{0,2},{1,3},{2,0},{3,1},{4,6},{5,7},{6,4},{7,5},{8,10},{9,11},{10,... | collective-permute-start | bytes 1769480 | tf_op jit(solution)/shard_map/ppermute | solution.py:32
  125.8 6.8 %copy-start.3 = (bf16[2,4,4,72,256]{4,3,2,1,0:T(8,128)(2,1)}, bf16[2,4,4,72,256]{4,3,2,1,0:T(8,128)(2,1)S(1)}, u32[]{:S(2)}) copy-start(bf16[2,4,4,72,256]{4,3,2,1,0:T(8,128)(2,1)S(1)} %get-tuple-element.47) | copy-start | bytes 3538948
  125.8 6.8 %copy-start.10 = (bf16[2,4,72,1024]{3,2,1,0:T(8,128)(2,1)}, bf16[2,4,72,1024]{3,2,1,0:T(8,128)(2,1)S(1)}, u32[]{:S(2)}) copy-start(bf16[2,4,72,1024]{3,2,1,0:T(8,128)(2,1)S(1)} %get-tuple-element.50.out) | copy-start | bytes 3538948
  132.6 7.7 %copy-start.12 = (f32[2,256,1152]{2,1,0:T(8,128)}, f32[2,256,1152]{2,1,0:T(8,128)S(1)}, u32[]{:S(2)}) copy-start(f32[2,256,1152]{2,1,0:T(8,128)S(1)} %get-tuple-element.129) | copy-start | bytes 7077892
  132.6 133.3 %copy-start.43 = (f32[2,256]{1,0:T(2,128)}, f32[2,256]{1,0:T(2,128)S(1)}, u32[]{:S(2)}) copy-start(f32[2,256]{1,0:T(2,128)S(1)} %broadcast_multiply_fusion.1) | copy-start | bytes 6148
  134.7 131.2 %copy-start.51 = (f32[2,256]{1,0:T(2,128)}, f32[2,256]{1,0:T(2,128)S(1)}, u32[]{:S(2)}) copy-start(f32[2,256]{1,0:T(2,128)S(1)} %fusion.36) | copy-start | bytes 6148
  149.1 113.7 %copy-start.13 = (f32[2,256,1152]{2,1,0:T(8,128)S(1)}, f32[2,256,1152]{2,1,0:T(8,128)}, u32[]{:S(2)}) copy-start(f32[2,256,1152]{2,1,0:T(8,128)} %copy-done.12) | copy-start | bytes 7077892
  272.5 4.8 copy-start.47
  284.6 27.0 %collective-permute-start.7 = (bf16[4,144,1152]{2,1,0:T(8,128)(2,1)}, bf16[4,144,1152]{2,1,0:T(8,128)(2,1)}, u32[]{:S(2)}, u32[]{:S(2)}) collective-permute-start(bf16[4,144,1152]{2,1,0:T(8,128)(2,1)} %fusion.17), channel_id=1, source_target_pairs={{0,4},{4,0},{8,12},{12,8},{16,20},{20,16},{24,28},{28,24},{1,5},{5... | collective-permute-start | bytes 3981320 | tf_op jit(solution)/shard_map/ppermute | solution.py:32
  287.4 4.3 copy-start.53
  287.4 5.7 %copy-start.37 = (f32[144,1152]{1,0:T(8,128)S(1)}, f32[144,1152]{1,0:T(8,128)}, u32[]{:S(2)}) copy-start(f32[144,1152]{1,0:T(8,128)} %get-tuple-element.66) | copy-start | bytes 1990660
  288.2 12.1 %collective-permute-start.4 = (bf16[2,288,256]{1,2,0:T(8,128)(2,1)S(1)}, bf16[2,288,256]{1,2,0:T(8,128)(2,1)S(1)}, u32[]{:S(2)}, u32[]{:S(2)}) collective-permute-start(bf16[2,288,256]{1,2,0:T(8,128)(2,1)S(1)} %get-tuple-element.150), channel_id=1, source_target_pairs={{0,1},{1,0},{2,3},{3,2},{4,5},{5,4},{6,7},{7,6},{8,9},{9,8},{10,11... | collective-permute-start | bytes 884744 | tf_op jit(solution)/shard_map/ppermute | solution.py:32
  289.4 18.8 %collective-permute-start.5 = (bf16[2,288,256]{1,2,0:T(8,128)(2,1)S(1)}, bf16[2,288,256]{1,2,0:T(8,128)(2,1)S(1)}, u32[]{:S(2)}, u32[]{:S(2)}) collective-permute-start(bf16[2,288,256]{1,2,0:T(8,128)(2,1)S(1)} %get-tuple-element.149), channel_id=1, source_target_pairs={{0,2},{1,3},{2,0},{3,1},{4,6},{5,7},{6,4},{7,5},{8,10},{9,11},{10,... | collective-permute-start | bytes 884744 | tf_op jit(solution)/shard_map/ppermute | solution.py:32
  290.3 17.9 %collective-permute-start.6 = (bf16[2,288,256]{1,2,0:T(8,128)(2,1)S(1)}, bf16[2,288,256]{1,2,0:T(8,128)(2,1)S(1)}, u32[]{:S(2)}, u32[]{:S(2)}) collective-permute-start(bf16[2,288,256]{1,2,0:T(8,128)(2,1)S(1)} %get-tuple-element.148), channel_id=1, source_target_pairs={{0,3},{1,2},{2,1},{3,0},{4,7},{5,6},{6,5},{7,4},{8,11},{9,10},{10,... | collective-permute-start | bytes 884744 | tf_op jit(solution)/shard_map/ppermute | solution.py:32
  311.6 6.5 %copy-start.7 = (s32[2,1024,1]{2,1,0:T(8,128)S(1)}, s32[2,1024,1]{2,1,0:T(8,128)}, u32[]{:S(2)}) copy-start(s32[2,1024,1]{2,1,0:T(8,128)} %copy-done.6) | copy-start | bytes 24580
  311.6 6.5 %copy-start.11 = (bf16[2,4,72,1024]{3,2,1,0:T(8,128)(2,1)S(1)}, bf16[2,4,72,1024]{3,2,1,0:T(8,128)(2,1)}, u32[]{:S(2)}) copy-start(bf16[2,4,72,1024]{3,2,1,0:T(8,128)(2,1)} %copy-done.10) | copy-start | bytes 3538948
  314.5 68.4 %collective-permute-start.10 = (bf16[144,1152]{1,0:T(8,128)(2,1)}, bf16[144,1152]{1,0:T(8,128)(2,1)S(1)}, u32[]{:S(2)}, u32[]{:S(2)}) collective-permute-start(bf16[144,1152]{1,0:T(8,128)(2,1)} %get-tuple-element.59), channel_id=1, source_target_pairs={{0,3},{1,2},{2,1},{3,0},{4,7},{5,6},{6,5},{7,4},{8,11},{9,10},{10,... | collective-permute-start | bytes 995336 | tf_op jit(solution)/shard_map/ppermute | solution.py:32
  316.0 66.9 %collective-permute-start.8 = (bf16[144,1152]{1,0:T(8,128)(2,1)}, bf16[144,1152]{1,0:T(8,128)(2,1)}, u32[]{:S(2)}, u32[]{:S(2)}) collective-permute-start(bf16[144,1152]{1,0:T(8,128)(2,1)} %get-tuple-element.57), channel_id=1, source_target_pairs={{0,1},{1,0},{2,3},{3,2},{4,5},{5,4},{6,7},{7,6},{8,9},{9,8},{10,11... | collective-permute-start | bytes 995336 | tf_op jit(solution)/shard_map/ppermute | solution.py:32
  316.8 66.8 %collective-permute-start.9 = (bf16[144,1152]{1,0:T(8,128)(2,1)S(1)}, bf16[144,1152]{1,0:T(8,128)(2,1)}, u32[]{:S(2)}, u32[]{:S(2)}) collective-permute-start(bf16[144,1152]{1,0:T(8,128)(2,1)S(1)} %get-tuple-element.58), channel_id=1, source_target_pairs={{0,2},{1,3},{2,0},{3,1},{4,6},{5,7},{6,4},{7,5},{8,10},{9,11},{10,... | collective-permute-start | bytes 995336 | tf_op jit(solution)/shard_map/ppermute | solution.py:32
  371.5 11.2 %copy-start.49 = (f32[1152]{0:T(1024)S(1)}, f32[1152]{0:T(1024)}, u32[]{:S(2)}) copy-start(f32[1152]{0:T(1024)} %get-tuple-element.124) | copy-start | bytes 13828
  371.5 11.2 %copy-start.50 = (f32[1152]{0:T(1024)S(1)}, f32[1152]{0:T(1024)}, u32[]{:S(2)}) copy-start(f32[1152]{0:T(1024)} %get-tuple-element.126) | copy-start | bytes 13828
  382.2 20.3 %copy-start.4 = (f32[4,144,864]{2,1,0:T(8,128)}, f32[4,144,864]{2,1,0:T(8,128)S(1)}, u32[]{:S(2)}) copy-start(f32[4,144,864]{2,1,0:T(8,128)S(1)} %get-tuple-element.63) | copy-start | bytes 5971972
  386.1 16.4 %copy-start.21 = (bf16[2,256,1152]{2,1,0:T(8,128)(2,1)S(1)}, bf16[2,256,1152]{2,1,0:T(8,128)(2,1)}, u32[]{:S(2)}) copy-start(bf16[2,256,1152]{2,1,0:T(8,128)(2,1)} %param.19) | copy-start | bytes 3538948
  386.1 36.1 %collective-permute-start.12 = (bf16[144,288]{1,0:T(8,128)(2,1)}, bf16[144,288]{1,0:T(8,128)(2,1)S(1)}, u32[]{:S(2)}, u32[]{:S(2)}) collective-permute-start(bf16[144,288]{1,0:T(8,128)(2,1)} %get-tuple-element.67), channel_id=1, source_target_pairs={{0,8},{4,12},{8,0},{12,4},{16,24},{20,28},{24,16},{28,20},{1,9},{5... | collective-permute-start | bytes 248840 | tf_op jit(solution)/shard_map/ppermute | solution.py:32
  387.5 34.8 %collective-permute-start.13 = (bf16[144,288]{1,0:T(8,128)(2,1)S(1)}, bf16[144,288]{1,0:T(8,128)(2,1)}, u32[]{:S(2)}, u32[]{:S(2)}) collective-permute-start(bf16[144,288]{1,0:T(8,128)(2,1)S(1)} %get-tuple-element.68), channel_id=1, source_target_pairs={{0,16},{4,20},{8,24},{12,28},{16,0},{20,4},{24,8},{28,12},{1,17},{... | collective-permute-start | bytes 248840 | tf_op jit(solution)/shard_map/ppermute | solution.py:32
  389.9 32.4 %collective-permute-start.14 = (bf16[144,288]{1,0:T(8,128)(2,1)S(1)}, bf16[144,288]{1,0:T(8,128)(2,1)}, u32[]{:S(2)}, u32[]{:S(2)}) collective-permute-start(bf16[144,288]{1,0:T(8,128)(2,1)S(1)} %get-tuple-element.69), channel_id=1, source_target_pairs={{0,24},{4,28},{8,16},{12,20},{16,8},{20,12},{24,0},{28,4},{1,25},{... | collective-permute-start | bytes 248840 | tf_op jit(solution)/shard_map/ppermute | solution.py:32
  390.5 34.2 %collective-permute-start.11 = (bf16[4,144,864]{2,1,0:T(8,128)(2,1)}, bf16[4,144,864]{2,1,0:T(8,128)(2,1)}, u32[]{:S(2)}, u32[]{:S(2)}) collective-permute-start(bf16[4,144,864]{2,1,0:T(8,128)(2,1)} %get-tuple-element.64), channel_id=1, source_target_pairs={{0,4},{4,0},{8,12},{12,8},{16,20},{20,16},{24,28},{28,24},{1,5},{5... | collective-permute-start | bytes 2985992 | tf_op jit(solution)/shard_map/ppermute | solution.py:32
  402.6 4.1 copy-start.23
  402.6 4.1 copy-start.48
  406.7 4.1 copy-start.24
  416.5 4.7 copy-start.59
  424.7 7.6 %copy-start.2 = (bf16[1152,1728]{1,0:T(8,128)(2,1)S(1)}, bf16[1152,1728]{1,0:T(8,128)(2,1)}, u32[]{:S(2)}) copy-start(bf16[1152,1728]{1,0:T(8,128)(2,1)} %copy.79.weight) | copy-start | bytes 11943940
  426.3 52.0 %copy-start.27 = (f32[4,144,864]{2,1,0:T(8,128)}, f32[4,144,864]{2,1,0:T(8,128)S(1)}, u32[]{:S(2)}) copy-start(f32[4,144,864]{2,1,0:T(8,128)S(1)} %convert_add_fusion.2) | copy-start | bytes 5971972
  427.4 64.6 %collective-permute-start.21 = (f32[144,720]{1,0:T(8,128)}, f32[144,720]{1,0:T(8,128)S(1)}, u32[]{:S(2)}, u32[]{:S(2)}) collective-permute-start(f32[144,720]{1,0:T(8,128)} %pad_maximum_fusion.6), channel_id=1, source_target_pairs={{0,4},{4,0},{8,12},{12,8},{16,20},{20,16},{24,28},{28,24},{1,5},{5... | collective-permute-start | bytes 1244168 | tf_op jit(solution)/shard_map/ppermute | solution.py:32
  427.9 54.2 %collective-permute-start.15 = (bf16[144,864]{1,0:T(8,128)(2,1)}, bf16[144,864]{1,0:T(8,128)(2,1)}, u32[]{:S(2)}, u32[]{:S(2)}) collective-permute-start(bf16[144,864]{1,0:T(8,128)(2,1)} %get-tuple-element.74), channel_id=1, source_target_pairs={{0,8},{4,12},{8,0},{12,4},{16,24},{20,28},{24,16},{28,20},{1,9},{5... | collective-permute-start | bytes 746504 | tf_op jit(solution)/shard_map/ppermute | solution.py:32
  428.3 53.7 %collective-permute-start.16 = (bf16[144,864]{1,0:T(8,128)(2,1)}, bf16[144,864]{1,0:T(8,128)(2,1)}, u32[]{:S(2)}, u32[]{:S(2)}) collective-permute-start(bf16[144,864]{1,0:T(8,128)(2,1)} %get-tuple-element.75), channel_id=1, source_target_pairs={{0,16},{4,20},{8,24},{12,28},{16,0},{20,4},{24,8},{28,12},{1,17},{... | collective-permute-start | bytes 746504 | tf_op jit(solution)/shard_map/ppermute | solution.py:32
  431.7 50.4 %collective-permute-start.17 = (bf16[144,864]{1,0:T(8,128)(2,1)S(1)}, bf16[144,864]{1,0:T(8,128)(2,1)}, u32[]{:S(2)}, u32[]{:S(2)}) collective-permute-start(bf16[144,864]{1,0:T(8,128)(2,1)S(1)} %get-tuple-element.76), channel_id=1, source_target_pairs={{0,24},{4,28},{8,16},{12,20},{16,8},{20,12},{24,0},{28,4},{1,25},{... | collective-permute-start | bytes 746504 | tf_op jit(solution)/shard_map/ppermute | solution.py:32
  432.3 46.2 %copy-start.40 = (bf16[16,1152]{1,0:T(8,128)(2,1)S(1)}, bf16[16,1152]{1,0:T(8,128)(2,1)}, u32[]{:S(2)}) copy-start(bf16[16,1152]{1,0:T(8,128)(2,1)} %param.20) | copy-start | bytes 110596
  478.3 13.8 %copy-start.8 = (f32[144,1728]{1,0:T(8,128)}, f32[144,1728]{1,0:T(8,128)S(1)}, u32[]{:S(2)}) copy-start(f32[144,1728]{1,0:T(8,128)S(1)} %get-tuple-element.190) | copy-start | bytes 2985988
  483.6 10.2 %copy-start.64 = (pred[288]{0:T(512)(128)(4,1)S(1)}, pred[288]{0:T(512)(128)(4,1)}, u32[]{:S(2)}) copy-start(pred[288]{0:T(512)(128)(4,1)} %broadcast_in_dim.120) | copy-start | bytes 868
  484.7 12.3 %collective-permute-start.18 = (f32[144,288]{1,0:T(8,128)}, f32[144,288]{1,0:T(8,128)}, u32[]{:S(2)}, u32[]{:S(2)}) collective-permute-start(f32[144,288]{1,0:T(8,128)} %get-tuple-element.161), channel_id=1, source_target_pairs={{0,0},{3,1},{2,2},{1,3},{4,4},{7,5},{6,6},{5,7},{8,8},{11,9},{10,1... | collective-permute-start | bytes 497672 | tf_op jit(solution)/shard_map/ppermute | solution.py:1201
  488.1 8.8 %collective-permute-start.19 = (f32[144,288]{1,0:T(8,128)}, f32[144,288]{1,0:T(8,128)}, u32[]{:S(2)}, u32[]{:S(2)}) collective-permute-start(f32[144,288]{1,0:T(8,128)} %get-tuple-element.163), channel_id=1, source_target_pairs={{1,0},{0,1},{3,2},{2,3},{5,4},{4,5},{7,6},{6,7},{9,8},{8,9},{11,10... | collective-permute-start | bytes 497672 | tf_op jit(solution)/shard_map/ppermute | solution.py:1201
  489.1 9.1 %collective-permute-start.20 = (f32[144,288]{1,0:T(8,128)}, f32[144,288]{1,0:T(8,128)}, u32[]{:S(2)}, u32[]{:S(2)}) collective-permute-start(f32[144,288]{1,0:T(8,128)} %get-tuple-element.162), channel_id=1, source_target_pairs={{2,0},{1,1},{0,2},{3,3},{6,4},{5,5},{4,6},{7,7},{10,8},{9,9},{8,10... | collective-permute-start | bytes 497672 | tf_op jit(solution)/shard_map/ppermute | solution.py:1201
  496.0 4.3 copy-start.9
  496.0 5.2 %copy-start.38 = (f32[144,1152]{1,0:T(8,128)S(1)}, f32[144,1152]{1,0:T(8,128)}, u32[]{:S(2)}) copy-start(f32[144,1152]{1,0:T(8,128)} %get-tuple-element.196) | copy-start | bytes 1990660
  496.1 6.1 %copy-start.1 = (bf16[1152,1152]{1,0:T(8,128)(2,1)S(1)}, bf16[1152,1152]{1,0:T(8,128)(2,1)}, u32[]{:S(2)}) copy-start(bf16[1152,1152]{1,0:T(8,128)(2,1)} %param.28) | copy-start | bytes 7962628
  (24 other events, 50.8 us)
